TPU v7x, 32 devices: a whole 2x2x4 slice. The times are simulated.
32 devices in a mesh: space: 16 (over z, y, x), tm: 2 (over core).
Axes of the slice: x: 2, y: 2, z: 4, core: 2. Of those that a mesh axis runs over, the one named last changes fastest.
Arguments:
- snapshots: bfloat16 [262144, 512], P(('space', 'tm')), may hold values from -6 to 6
- range_test: bfloat16 [512, 128], replicated, may hold values from -0.25 to 0.25
- test_rows: bfloat16 [256, 262144], P(None, ('space', 'tm')), may hold values from -0.01171875 to 0.01171875
- species: int32 [256, 1024], P(('space', 'tm')), may hold values from 0 to 3
- reaction_rates: float32 [4], replicated, may hold values from 1 to 8
- adjoint_end: float32 [256, 1024], P(('space', 'tm')), may hold values from -6 to 6
Outputs:
- adjoint: float32 [256, 1024], P(('space', 'tm'))
- time_factors: float32 [128, 512], P(None, ('space', 'tm'))
All inputs are finite; a program needn't handle non-finite values.
Results may differ from a plain program's by a relative error of at most 0.0012.
Values sent between devices are 32-bit elements; how exact they have to be, the bound alone decides.
No kernel may reach another device: no remote copies, remote signals or barrier semaphores. Data moves between devices by JAX's collectives and lax.ppermute only.
A program may use at most 64 MiB of HBM per device.

v0:
```python
import jax
import jax.numpy as jnp
from jax import lax
from jax.sharding import PartitionSpec as P

DIFFUSION = 0.2
STEP_SIZE = 0.05


def with_halo(block, sides, width):
    for axis, dim in sides:
        count = lax.axis_size(axis)
        forward = [(i, i + 1) for i in range(count - 1)]
        backward = [(target, source) for source, target in forward]
        low = lax.ppermute(
            lax.slice_in_dim(block, block.shape[dim] - width, None, axis=dim), axis, forward
        )
        high = lax.ppermute(lax.slice_in_dim(block, 0, width, axis=dim), axis, backward)
        block = jnp.concatenate([low, block, high], axis=dim)
    return block


def reverse_step(adjoint, state, coupling):
    padded = with_halo(adjoint, ((("space", "tm"), 0),), 1)
    sideways = jnp.pad(adjoint, ((0, 0), (1, 1)))
    laplace = padded[2:] + padded[:-2] + sideways[:, 2:] + sideways[:, :-2] - 4.0 * adjoint
    return (
        adjoint + DIFFUSION * laplace + STEP_SIZE * coupling * (1.0 - 3.0 * state * state) * adjoint
    )


def shards(snapshots, range_test, test_rows, species, reaction_rates, adjoint_end):
    high = lax.Precision.HIGHEST
    contract_rows = (((0,), (0,)), ((), ()))
    range_part = jnp.dot(snapshots, range_test, preferred_element_type=jnp.float32)
    gram_local = lax.dot_general(range_part, range_part, contract_rows, precision=high)
    raw_local = jnp.dot(test_rows, range_part, precision=high, preferred_element_type=jnp.float32)
    gram, projected_raw = lax.psum((gram_local, raw_local), ("space", "tm"))
    lower_factor = jnp.linalg.cholesky(gram)
    basis = jax.scipy.linalg.solve_triangular(lower_factor, range_part.T, lower=True).T
    projected = jax.scipy.linalg.solve_triangular(lower_factor, projected_raw.T, lower=True).T
    devices = lax.axis_size(("space", "tm"))
    total_times = snapshots.shape[1]
    owned = total_times // devices
    normal_matrix = lax.dot_general(projected, projected, contract_rows, precision=high)
    normal_factor = jnp.linalg.cholesky(normal_matrix)
    corange_local = jnp.dot(test_rows, snapshots, preferred_element_type=jnp.float32)
    corange_whole = lax.psum(corange_local, ("space", "tm"))
    corange_mine = lax.dynamic_slice_in_dim(
        corange_whole, lax.axis_index(("space", "tm")) * owned, owned, 1
    )
    right_side = lax.dot_general(projected, corange_mine, contract_rows, precision=high)
    factors_mine = jax.scipy.linalg.cho_solve((normal_factor, True), right_side)
    cells_total = snapshots.shape[0] * devices
    time_factors = factors_mine * cells_total ** (-0.5)
    whole_factors = lax.all_gather(factors_mine, ("space", "tm"), axis=1, tiled=True)
    window_factors = whole_factors[:, whole_factors.shape[1] - 2 :]
    states = jnp.dot(basis, window_factors, precision=high)
    rows_here = adjoint_end.shape[0]
    width_here = adjoint_end.shape[1]
    kinds = jnp.arange(reaction_rates.shape[0], dtype=jnp.int32)
    coupling = jnp.sum(jnp.where(species[:, :, None] == kinds, reaction_rates, 0.0), axis=-1)
    adjoint = adjoint_end
    for column in (1, 0):
        state = states[:, column].reshape(rows_here, width_here)
        adjoint = reverse_step(adjoint, state, coupling)
    return (adjoint, time_factors)


def solution(mesh):
    return jax.shard_map(
        shards,
        mesh=mesh,
        in_specs=(
            P(("space", "tm"), None),
            P(),
            P(None, ("space", "tm")),
            P(("space", "tm"), None),
            P(),
            P(("space", "tm"), None),
        ),
        out_specs=(P(("space", "tm"), None), P(None, ("space", "tm"))),
        check_vma=False,
    )
```

profile of v0, /device:TPU:1, one launch (start us, length us, event | category | flops | bytes accessed | tf_op | source)
XLA Modules:
  0.0 280.1 jit_solution(6332981974878304740)
XLA Ops:
  7.2 7.9 %fusion.42 = f32[256,512]{1,0:T(8,128)} fusion(bf16[256,8192]{1,0:T(8,128)(2,1)} %param.9, bf16[8192,512]{1,0:T(8,128)(2,1)} %param.7), kind=kOutput, calls=%fused_computation.68 | convolution fusion | flops 2147483648 | bytes 13107200 | tf_op jit(solution)/shard_map/dot_general | solution.py:47
  15.2 2.3 fusion.39
  17.5 7.6 %fusion.40 = f32[128,128]{0,1:T(8,128)} fusion(f32[8192,128]{1,0:T(8,128)S(1)} %fusion.39), kind=kOutput, calls=%fused_computation.66 | convolution fusion | flops 1610612736 | bytes 4259840 | tf_op jit(solution)/shard_map/dot_general | solution.py:36
  25.1 4.3 %convolution_bitcast_fusion = f32[256,128]{0,1:T(8,128)} fusion(f32[8192,128]{1,0:T(8,128)S(1)} %fusion.39, bf16[256,8192]{1,0:T(8,128)(2,1)S(1)} %copy-done.3), kind=kOutput, calls=%fused_computation | convolution fusion | flops 3221225472 | bytes 8519680 | tf_op jit(solution)/shard_map/dot_general | solution.py:37
  29.4 2.0 collective-permute-start
  31.4 4.5 %collective-permute-start.1 = (f32[1,1024]{1,0:T(1,128)S(1)}, f32[1,1024]{1,0:T(1,128)S(1)}, u32[]{:S(2)}, u32[]{:S(2)}) collective-permute-start(f32[1,1024]{1,0:T(1,128)S(1)} %get-tuple-element.11), channel_id=1, source_target_pairs={{0,1},{1,2},{2,3},{3,4},{4,5},{5,6},{6,7},{7,8},{8,9},{9,10},{10,1... | collective-permute-start | bytes 12296 | tf_op jit(solution)/shard_map/ppermute | solution.py:15
  36.0 125.1 %all-reduce.5.cloned.1.call-done = (f32[128,128]{0,1:T(8,128)}, f32[256,128]{0,1:T(8,128)}, f32[256,512]{1,0:T(8,128)}) async-done(((f32[128,128]{0,1:T(8,128)}, f32[256,128]{0,1:T(8,128)}, f32[256,512]{1,0:T(8,128)}), (f32[128,128]{0,1:T(8,128)}, f32[256,128]{0,1:T(8,128)}, f32[256,512]{1,0:T(8,128)})) %all-reduce.5.cloned.1.call-update) | async-done | bytes 720912 | tf_op jit(solution)/shard_map/psum | solution.py:38
  161.0 0.9 copy.12
  162.0 0.9 fusion.13
  162.8 11.7 %cholesky.44 = f32[128,128]{1,0:T(8,128)S(1)} custom-call(f32[128,128]{1,0:T(8,128)S(1)} %fusion.13), custom_call_target="Cholesky" | custom-call | tf_op jit(solution)/shard_map/jit(cholesky)/cholesky | solution.py:39
  175.2 0.7 fusion.2
  175.9 9.8 %custom-call.16 = f32[1,128,128]{1,2,0:T(8,128)S(1)} custom-call(f32[1,128,128]{2,1,0:T(8,128)S(1)} %fusion.2), custom_call_target="InvertDiagBlocksLowerTriangular" | custom-call | tf_op jit(solution)/shard_map/jit(_solve_triangular)/triangular_solve | solution.py:40
  185.7 8.0 %fusion.11 = f32[128,8192]{1,0:T(8,128)} fusion(f32[8192,128]{1,0:T(8,128)} %copy-done.1, f32[1,128,128]{1,2,0:T(8,128)S(1)} %custom-call.16), kind=kOutput, calls=%fused_computation.17 | convolution fusion | flops 1610612736 | bytes 8454144 | tf_op jit(solution)/shard_map/jit(_solve_triangular)/triangular_solve | solution.py:40
  194.4 11.9 %cholesky.55 = f32[128,128]{1,0:T(8,128)S(1)} custom-call(f32[128,128]{1,0:T(8,128)S(1)} %fusion.8), custom_call_target="Cholesky" | custom-call | tf_op jit(solution)/shard_map/jit(cholesky)/cholesky | solution.py:46
  207.0 0.7 fusion.3
  207.6 9.8 %custom-call.17 = f32[1,128,128]{1,2,0:T(8,128)S(1)} custom-call(f32[1,128,128]{2,1,0:T(8,128)S(1)} %fusion.3), custom_call_target="InvertDiagBlocksLowerTriangular" | custom-call | tf_op jit(solution)/shard_map/jit(_cho_solve)/triangular_solve | solution.py:53
  217.5 1.3 fusion
  219.0 0.9 broadcast_multiply_fusion
  219.9 41.6 %all_gather.3 = f32[128,512]{0,1:T(8,128)S(1)} all-gather(f32[128,16]{0,1:T(8,128)S(1)} %get-tuple-element.13), channel_id=1, replica_groups=mesh['space'=16,'tm'=2] {'space','tm'}, dimensions={1}, use_global_device_ids=true | all-gather | bytes 270336 | tf_op jit(solution)/shard_map/all_gather | solution.py:56
  261.4 4.5 %fusion.34 = f32[8192,2]{0,1:T(2,128)S(1)} fusion(f32[128,8192]{1,0:T(8,128)} %fusion.11, f32[128,512]{0,1:T(8,128)S(1)} %all_gather.3), kind=kOutput, calls=%fused_computation.60 | convolution fusion | flops 25165824 | bytes 4260864 | tf_op jit(solution)/shard_map/dot_general | solution.py:58
  266.2 2.1 collective-permute-start.2
  268.3 3.5 %collective-permute-start.3 = (f32[1,1024]{1,0:T(1,128)S(1)}, f32[1,1024]{1,0:T(1,128)S(1)}, u32[]{:S(2)}, u32[]{:S(2)}) collective-permute-start(f32[1,1024]{1,0:T(1,128)S(1)} %get-tuple-element.9), channel_id=1, source_target_pairs={{0,1},{1,2},{2,3},{3,4},{4,5},{5,6},{6,7},{7,8},{8,9},{9,10},{10,1... | collective-permute-start | bytes 12296 | tf_op jit(solution)/shard_map/ppermute | solution.py:15
  271.8 0.7 collective-permute-done.3
  272.5 0.7 fusion.25
  (37 shorter events, 2.8 us)
Async XLA Ops:
  7.2 8.0 %copy-start = (bf16[512,128]{1,0:T(8,128)(2,1)S(1)}, bf16[512,128]{1,0:T(8,128)(2,1)}, u32[]{:S(2)}) copy-start(bf16[512,128]{1,0:T(8,128)(2,1)} %param.8) | copy-start | bytes 393220
  7.2 153.9 %all-reduce.5.cloned.1.call-start = ((), (), s32[]{:S(2)}) async-start(), calls=%async_computation | async-start | bytes 1441792 | tf_op jit(solution)/shard_map/psum | solution.py:38
  7.2 7.9 %copy-start.2 = (bf16[8192,512]{1,0:T(8,128)(2,1)S(1)}, bf16[8192,512]{1,0:T(8,128)(2,1)}, u32[]{:S(2)}) copy-start(bf16[8192,512]{1,0:T(8,128)(2,1)} %param.7) | copy-start | bytes 25165828
  17.5 7.6 %copy-start.1 = (f32[8192,128]{1,0:T(8,128)}, f32[8192,128]{1,0:T(8,128)S(1)}, u32[]{:S(2)}) copy-start(f32[8192,128]{1,0:T(8,128)S(1)} %fusion.39) | copy-start | bytes 12582916
  17.5 7.6 %copy-start.3 = (bf16[256,8192]{1,0:T(8,128)(2,1)S(1)}, bf16[256,8192]{1,0:T(8,128)(2,1)}, u32[]{:S(2)}) copy-start(bf16[256,8192]{1,0:T(8,128)(2,1)} %param.9) | copy-start | bytes 12582916
  25.1 4.3 %copy-start.5 = (f32[8,1024]{1,0:T(8,128)S(1)}, f32[8,1024]{1,0:T(8,128)}, u32[]{:S(2)}) copy-start(f32[8,1024]{1,0:T(8,128)} %param.12) | copy-start | bytes 98308
  25.1 10.8 %copy-start.6 = (s32[8,1024]{1,0:T(8,128)S(1)}, s32[8,1024]{1,0:T(8,128)}, u32[]{:S(2)}) copy-start(s32[8,1024]{1,0:T(8,128)} %param.10) | copy-start | bytes 98308
  25.1 10.8 %copy-start.7 = (f32[4]{0:T(128)S(1)}, f32[4]{0:T(128)}, u32[]{:S(2)}) copy-start(f32[4]{0:T(128)} %param.11) | copy-start | bytes 52
  29.4 236.7 %collective-permute-start = (f32[1,1024]{1,0:T(1,128)S(1)}, f32[1,1024]{1,0:T(1,128)S(1)}, u32[]{:S(2)}, u32[]{:S(2)}) collective-permute-start(f32[1,1024]{1,0:T(1,128)S(1)} %get-tuple-element.10), channel_id=1, source_target_pairs={{1,0},{2,1},{3,2},{4,3},{5,4},{6,5},{7,6},{8,7},{9,8},{10,9},{11,1... | collective-permute-start | bytes 12296 | tf_op jit(solution)/shard_map/ppermute | solution.py:18
  31.4 234.7 %collective-permute-start.1 = (f32[1,1024]{1,0:T(1,128)S(1)}, f32[1,1024]{1,0:T(1,128)S(1)}, u32[]{:S(2)}, u32[]{:S(2)}) collective-permute-start(f32[1,1024]{1,0:T(1,128)S(1)} %get-tuple-element.11), channel_id=1, source_target_pairs={{0,1},{1,2},{2,3},{3,4},{4,5},{5,6},{6,7},{7,8},{8,9},{9,10},{10,1... | collective-permute-start | bytes 12296 | tf_op jit(solution)/shard_map/ppermute | solution.py:15
  185.7 8.0 %copy-start.4 = (f32[256,128]{0,1:T(8,128)S(1)}, f32[256,128]{0,1:T(8,128)}, u32[]{:S(2)}) copy-start(f32[256,128]{0,1:T(8,128)} %get-tuple-element.6) | copy-start | bytes 393220
  266.2 5.6 %collective-permute-start.2 = (f32[1,1024]{1,0:T(1,128)S(1)}, f32[1,1024]{1,0:T(1,128)S(1)}, u32[]{:S(2)}, u32[]{:S(2)}) collective-permute-start(f32[1,1024]{1,0:T(1,128)S(1)} %get-tuple-element.8), channel_id=1, source_target_pairs={{1,0},{2,1},{3,2},{4,3},{5,4},{6,5},{7,6},{8,7},{9,8},{10,9},{11,1... | collective-permute-start | bytes 12296 | tf_op jit(solution)/shard_map/ppermute | solution.py:18
  268.3 4.2 %collective-permute-start.3 = (f32[1,1024]{1,0:T(1,128)S(1)}, f32[1,1024]{1,0:T(1,128)S(1)}, u32[]{:S(2)}, u32[]{:S(2)}) collective-permute-start(f32[1,1024]{1,0:T(1,128)S(1)} %get-tuple-element.9), channel_id=1, source_target_pairs={{0,1},{1,2},{2,3},{3,4},{4,5},{5,6},{6,7},{7,8},{8,9},{9,10},{10,1... | collective-permute-start | bytes 12296 | tf_op jit(solution)/shard_map/ppermute | solution.py:15
Sparse Core Ops, SparseCore 0:
  29.5 131.4 all-reduce.4
where the time goes:
time: 280 us
  waiting for transfers between devices  126 us (45%)
  other arithmetic  47.7 us (17%)
  blocking collectives  41.6 us (15%)
  matrix products  37.5 us (13%)
  between operations  14.3 us (5%)
  starting transfers between devices  12 us (4%)
    psum x1, waiting for transfers between devices, shards(): gram, projected_raw = lax.psum((gram_local, raw_local), ('space', 'tm'))  125 us
    all_gather x1, blocking collectives, shards(): lax.all_gather(factors_mine, ('space', 'tm'), axis=1, tiled=True)  41.6 us
    another operation x3, other arithmetic, shards(): normal_factor = jnp.linalg.cholesky(normal_matrix)  12.6 us
    another operation x3, other arithmetic, shards(): lower_factor = jnp.linalg.cholesky(gram)  12.4 us
    another operation x2, other arithmetic, shards(): jax.scipy.linalg.solve_triangular(lower_factor, range_part.T, lower=True)  10.5 us
    another operation x2, other arithmetic, shards(): factors_mine = jax.scipy.linalg.cho_solve((normal_factor, True), right_side)  10.5 us
    another operation x1, matrix products, shards(): jax.scipy.linalg.solve_triangular(lower_factor, range_part.T, lower=True)  7.96 us
    ppermute x2, starting transfers between devices, with_halo(): lax.ppermute(lax.slice_in_dim(block, block.shape[dim] - width, None, axis...  7.96 us
  transfers between devices with their start and end apart: 5, of which 2 were waited for; matrix products, arithmetic and copies ran while one was open for 23% of the time, Pallas kernels for 0%

commit v1 on v0

v1 whole, which is shorter than its diff:
```python
import functools

import jax
import jax.numpy as jnp
from jax import lax
from jax.experimental import pallas as pl
from jax.experimental.pallas import tpu as pltpu
from jax.sharding import PartitionSpec as P

DIFFUSION = 0.2
STEP_SIZE = 0.05
AXES = ("space", "tm")
HIGH = lax.Precision.HIGHEST
NT = (((1,), (1,)), ((), ()))
F32 = jnp.float32
BF16 = jnp.bfloat16


def sketch_kernel(snap, test, om, range_t, ct, crit, om_t, corange, gram):
    step = pl.program_id(0)
    rank = om.shape[1]
    sketch = test.shape[0]
    times = snap.shape[1]

    @pl.when(step == 0)
    def _():
        om_t[...] = om[...].astype(F32).T.astype(BF16)
        corange[...] = jnp.zeros_like(corange)
        gram[...] = jnp.zeros_like(gram)

    states = snap[...]
    rt = lax.dot_general(om_t[...], states, NT, preferred_element_type=F32)
    range_t[...] = rt
    upper = rt.astype(BF16)
    lower = (rt - upper.astype(F32)).astype(BF16)
    both = jnp.concatenate([upper, lower], axis=0)
    gram[...] += lax.dot_general(both, both, NT, preferred_element_type=F32)
    corange[...] += jnp.dot(test[...], states, preferred_element_type=F32)

    @pl.when(step == pl.num_programs(0) - 1)
    def _():
        whole = corange[...]
        projected = jnp.dot(whole, om[...].astype(F32), precision=HIGH, preferred_element_type=F32)
        crit[0:sketch, :] = projected
        cross = gram[0:rank, rank:]
        crit[sketch:, :] = gram[0:rank, 0:rank] + cross + cross.T
        half = sketch // 2
        for h in range(2):
            turned = whole[h * half : (h + 1) * half, :].T
            ct[h] = turned
            for j in range(2):
                row = turned[times - 2 + j : times - 1 + j, :]
                for q in range(2):
                    place = sketch + j * 4 + h * 2 + q
                    crit[place : place + 1, rank // 2 :] = row[:, q * 64 : (q + 1) * 64]


def sketches(snapshots, range_test, test_rows, block=1024):
    cells, times = snapshots.shape
    rank = range_test.shape[1]
    sketch = test_rows.shape[0]
    return pl.pallas_call(
        sketch_kernel,
        grid=(cells // block,),
        in_specs=[
            pl.BlockSpec((block, times), lambda i: (i, 0)),
            pl.BlockSpec((sketch, block), lambda i: (0, i)),
            pl.BlockSpec((times, rank), lambda i: (0, 0)),
        ],
        out_specs=[
            pl.BlockSpec((rank, block), lambda i: (0, i)),
            pl.BlockSpec((2, times, sketch // 2), lambda i: (0, 0, 0)),
            pl.BlockSpec((sketch + rank, rank), lambda i: (0, 0)),
        ],
        out_shape=[
            jax.ShapeDtypeStruct((rank, cells), F32),
            jax.ShapeDtypeStruct((2, times, sketch // 2), F32),
            jax.ShapeDtypeStruct((sketch + rank, rank), F32),
        ],
        scratch_shapes=[
            pltpu.VMEM((rank, times), BF16),
            pltpu.VMEM((sketch, times), F32),
            pltpu.VMEM((2 * rank, 2 * rank), F32),
        ],
        compiler_params=pltpu.CompilerParams(
            dimension_semantics=("arbitrary",), vmem_limit_bytes=40 * 2**20
        ),
        name="sketches",
    )(snapshots, test_rows, range_test)


def solve_kernel(
    cells_total, owned, crit, mine, range_t, adjoint, species, rates, factors, first, second, augmented, lhs, upper
):
    sketch = mine.shape[2] * 2
    rank = crit.shape[1]
    half = sketch // 2
    ends = -(-owned // 8) * 8
    lhs[...] = jnp.zeros_like(lhs)
    for h in range(2):
        lhs[0:owned, h * half : (h + 1) * half] = mine[h]
        for j in range(2):
            for q in range(2):
                place = sketch + j * 4 + h * 2 + q
                lhs[ends + j : ends + j + 1, h * half + q * 64 : h * half + (q + 1) * 64] = crit[
                    place : place + 1, rank // 2 :
                ]
    projected = crit[0:sketch, :]
    turned = projected.T
    augmented[:, 0:rank] = jnp.dot(turned, projected, precision=HIGH, preferred_element_type=F32)
    augmented[:, rank:] = lax.dot_general(turned, lhs[...], NT, precision=HIGH, preferred_element_type=F32)
    gram = crit[sketch:, :]
    row_id = lax.broadcasted_iota(jnp.int32, (rank, rank), 0)
    col_id = lax.broadcasted_iota(jnp.int32, (rank, rank), 1)
    upper[...] = jnp.where(col_id > row_id, gram.T, gram)

    sub = lax.broadcasted_iota(jnp.int32, (8, 1), 0)
    lane = lax.broadcasted_iota(jnp.int32, (1, rank), 1)
    tiles = rank // 8
    for b in range(tiles):
        rows = slice(8 * b, 8 * b + 8)
        tile, _ = reduced(augmented[rows, :], 8 * b, sub)
        augmented[rows, :] = tile
        for i in range(tiles):
            if i != b:
                eliminate(augmented, i, b, tile)
        tile, roots = reduced(upper[rows, :], 8 * b, sub)
        for i in range(b + 1, tiles):
            eliminate(upper, i, b, tile)
        upper[rows, :] = jnp.where(lane >= 8 * b + sub, roots, 0.0)

    solved = augmented[:, rank:]
    out = jnp.dot(upper[...], solved, precision=HIGH, preferred_element_type=F32) * cells_total**-0.5
    factors[...] = out[:, 0:owned]

    rows_here, width = adjoint.shape
    for r in range(rows_here):
        sums = [jnp.zeros((8, width), F32) for _ in range(2)]
        for t in range(tiles):
            part = range_t[8 * t : 8 * t + 8, r * width : (r + 1) * width]
            for j in range(2):
                sums[j] = sums[j] + part * solved[8 * t : 8 * t + 8, ends + j : ends + j + 1]
        for j in range(2):
            (first if j == 1 else second)[r : r + 1, :] = jnp.sum(sums[j], axis=0, keepdims=True)

    kinds = species[...]
    coupling = jnp.zeros(kinds.shape, F32)
    for kind in range(rates.shape[0]):
        coupling = jnp.where(kinds == kind, rates[kind], coupling)
    coupling = STEP_SIZE * coupling
    value = adjoint[...]
    state = first[...]
    none = jnp.zeros((1, width), F32)
    edge = jnp.zeros((rows_here, 1), F32)
    near = jnp.concatenate([none, value[:-1]], axis=0) + jnp.concatenate([value[1:], none], axis=0)
    near = near + jnp.concatenate([edge, value[:, :-1]], axis=1) + jnp.concatenate([value[:, 1:], edge], axis=1)
    first[...] = value + DIFFUSION * (near - 4.0 * value) + coupling * (1.0 - 3.0 * state * state) * value
    state = second[...]
    second[...] = coupling * (1.0 - 3.0 * state * state)


def reduced(tile, first_col, sub):
    cols = [tile[:, first_col + k : first_col + k + 1] for k in range(8)]
    roots = tile
    for k in range(8):
        pivot = cols[k][k : k + 1, :]
        inverse = 1.0 / pivot
        row = tile[k : k + 1, :]
        scaled = row * inverse
        roots = jnp.where(sub == k, row * lax.rsqrt(pivot), roots)
        tile = jnp.where(sub == k, scaled, tile - cols[k] * scaled)
        for m in range(k + 1, 8):
            value = cols[m][k : k + 1, :] * inverse
            cols[m] = jnp.where(sub == k, value, cols[m] - cols[k] * value)
    return tile, roots


def eliminate(ref, i, b, tile):
    there = slice(8 * i, 8 * i + 8)
    other = ref[there, :]
    cols = [other[:, 8 * b + k : 8 * b + k + 1] for k in range(8)]
    for k in range(8):
        other = other - cols[k] * tile[k : k + 1, :]
    ref[there, :] = other


def solve(crit, mine, range_t, adjoint, species, rates, cells_total):
    owned = mine.shape[1]
    rank = crit.shape[1]
    sketch = 2 * mine.shape[2]
    vmem = pl.BlockSpec(memory_space=pltpu.VMEM)
    return pl.pallas_call(
        functools.partial(solve_kernel, cells_total, owned),
        in_specs=[vmem, vmem, vmem, vmem, vmem, pl.BlockSpec(memory_space=pltpu.SMEM)],
        out_specs=[vmem, vmem, vmem],
        out_shape=[
            jax.ShapeDtypeStruct((rank, owned), F32),
            jax.ShapeDtypeStruct(adjoint.shape, F32),
            jax.ShapeDtypeStruct(adjoint.shape, F32),
        ],
        scratch_shapes=[
            pltpu.VMEM((rank, 2 * rank), F32),
            pltpu.VMEM((rank, sketch), F32),
            pltpu.VMEM((rank, rank), F32),
        ],
        compiler_params=pltpu.CompilerParams(vmem_limit_bytes=40 * 2**20),
        name="solve",
    )(crit, mine, range_t, adjoint, species, rates)


def partners(count, shift, other):
    return [(i, i ^ (other << shift)) for i in range(count)]


def member(shift, size):
    return (lax.axis_index(AXES) >> shift) & (size - 1)


def pick(pieces, index):
    return lax.dynamic_index_in_dim(pieces, index, 0, keepdims=False)


def summed_pieces(pieces, count, shift):
    size = pieces.shape[0]
    me = member(shift, size)
    got = [lax.ppermute(pick(pieces, me ^ p), AXES, partners(count, shift, p)) for p in range(1, size)]
    total = pick(pieces, me)
    for piece in got:
        total = total + piece
    return total


def gathered_pieces(piece, count, shift, size):
    me = member(shift, size)
    got = [lax.ppermute(piece, AXES, partners(count, shift, p)) for p in range(1, size)]
    out = jnp.zeros((size,) + piece.shape, piece.dtype)
    for p, part in enumerate([piece] + got):
        out = lax.dynamic_update_index_in_dim(out, part, me ^ p, 0)
    return out


def stages(count):
    bits = count.bit_length() - 1
    out, shift = [(0, 2)], 1
    while shift < bits:
        width = min(2, bits - shift)
        out.append((shift, 1 << width))
        shift += width
    return out


def reduce_sketches(crit, ct, count):
    plan = stages(count)
    halves, times, width = ct.shape
    owned = times // count
    left = count
    for shift, size in plan[:-1]:
        left //= size
        crit = crit.reshape(size, -1, width)
        ct = ct.reshape(halves, left, size, owned, width)
        ct = jnp.moveaxis(ct, 2, 0).reshape(size, -1, width)
        split = crit.shape[1]
        both = summed_pieces(jnp.concatenate([crit, ct], axis=1), count, shift)
        crit, ct = both[:split], both[split:].reshape(halves, left * owned, width)
    shift, size = plan[-1]
    ct = ct.reshape(halves, size, owned, width)
    ct = jnp.moveaxis(ct, 1, 0).reshape(size, -1, width)
    split = crit.shape[0]
    whole = jnp.broadcast_to(crit[None], (size,) + crit.shape)
    both = summed_pieces(jnp.concatenate([whole, ct], axis=1), count, shift)
    crit, mine = both[:split], both[split:].reshape(halves, owned, width)
    for shift, size in plan[-2::-1]:
        crit = gathered_pieces(crit, count, shift, size).reshape(-1, width)
    return crit, mine


def shards(snapshots, range_test, test_rows, species, reaction_rates, adjoint_end):
    count = lax.axis_size(AXES)
    cells_total = snapshots.shape[0] * count
    range_t, ct, crit = sketches(snapshots, range_test, test_rows)
    crit, mine = reduce_sketches(crit, ct, count)
    time_factors, partial, rate = solve(crit, mine, range_t, adjoint_end, species, reaction_rates, cells_total)
    forward = [(i, i + 1) for i in range(count - 1)]
    backward = [(i + 1, i) for i in range(count - 1)]
    above = lax.ppermute(jnp.concatenate([partial[-1:], adjoint_end[-1:]], axis=0), AXES, forward)
    below = lax.ppermute(jnp.concatenate([partial[:1], adjoint_end[:1]], axis=0), AXES, backward)
    adjoint = jnp.concatenate(
        [partial[:1] + DIFFUSION * above[1:], partial[1:-1], partial[-1:] + DIFFUSION * below[1:]], axis=0
    )
    device = lax.axis_index(AXES)
    top = jnp.where(device > 0, above[:1] + DIFFUSION * adjoint_end[:1], 0.0)
    bottom = jnp.where(device < count - 1, below[:1] + DIFFUSION * adjoint_end[-1:], 0.0)
    padded = jnp.concatenate([top, adjoint, bottom], axis=0)
    sideways = jnp.pad(adjoint, ((0, 0), (1, 1)))
    laplace = padded[2:] + padded[:-2] + sideways[:, 2:] + sideways[:, :-2] - 4.0 * adjoint
    return (adjoint + DIFFUSION * laplace + rate * adjoint, time_factors)


def solution(mesh):
    return jax.shard_map(
        shards,
        mesh=mesh,
        in_specs=(P(AXES, None), P(), P(None, AXES), P(AXES, None), P(), P(AXES, None)),
        out_specs=(P(AXES, None), P(None, AXES)),
        check_vma=False,
    )
```

time: 280 us -> 86.3 us (0.31)
  the two profiles are of different devices: /device:TPU:1 before, /device:TPU:8 now
where the time goes in v1:
time: 86.3 us; the launch traced here: 85.9 us
  Pallas kernels  38.5 us (45%)
  starting transfers between devices  19.1 us (22%)
  waiting for transfers between devices  18.3 us (21%)
  local copies, waits for them, and re-layouts  8.07 us (9%)
  between operations  0.95 us (1%)
  other arithmetic  0.93 us (1%)
    pallas_call x1, Pallas kernels, solve(): pl.pallas_call(functools.partial(solve_kernel, cells_total, owned), in_sp...  28 us
    pallas_call x1, Pallas kernels, sketches(): pl.pallas_call(sketch_kernel, grid=(cells // block,), in_specs=[pl.BlockS...  10.5 us
    ppermute x7, waiting for transfers between devices, summed_pieces(): lax.ppermute(pick(pieces, me ^ p), AXES, partners(count, shift, p))  10.1 us
    unnamed x15, local copies, waits for them, and re-layouts  7.88 us
    ppermute x7, starting transfers between devices, summed_pieces(): lax.ppermute(pick(pieces, me ^ p), AXES, partners(count, shift, p))  7.18 us
    ppermute x1, starting transfers between devices, shards(): lax.ppermute(jnp.concatenate([partial[:1], adjoint_end[:1]], axis=0), AXE...  6.4 us
    ppermute x1, waiting for transfers between devices, shards(): lax.ppermute(jnp.concatenate([partial[-1:], adjoint_end[-1:]], axis=0), A...  4.15 us
    ppermute x4, waiting for transfers between devices, gathered_pieces(): lax.ppermute(piece, AXES, partners(count, shift, p))  4.02 us
  transfers between devices with their start and end apart: 13, of which 12 were waited for; matrix products, arithmetic and copies ran while one was open for 1% of the time, Pallas kernels for 0%

profile of v1, /device:TPU:8, one launch (start us, length us, event | category | flops | bytes accessed | tf_op | source)
XLA Modules:
  0.0 85.9 jit_solution(9885997451362776400)
XLA Ops:
  0.7 2.2 %copy-done = bf16[256,8192]{1,0:T(8,128)(2,1)S(1)} copy-done((bf16[256,8192]{1,0:T(8,128)(2,1)S(1)}, bf16[256,8192]{1,0:T(8,128)(2,1)}, u32[]{:S(2)}) %copy-start) | copy-done | bytes 4194328
  2.8 0.9 %copy-done.3 = bf16[512,128]{1,0:T(8,128)(2,1)S(1)} copy-done((bf16[512,128]{1,0:T(8,128)(2,1)S(1)}, bf16[512,128]{1,0:T(8,128)(2,1)}, u32[]{:S(2)}) %copy-start.3) | copy-done | bytes 131096
  3.7 10.5 %sketches.1 = (f32[128,8192]{1,0:T(8,128)S(1)}, f32[2,512,128]{2,1,0:T(8,128)S(1)}, f32[384,128]{1,0:T(8,128)S(1)}) custom-call(bf16[8192,512]{1,0:T(8,128)(2,1)} %snap.1, bf16[256,8192]{1,0:T(8,128)(2,1)S(1)} %copy-done, bf16[512,128]{1,0:T(8,128)(2,1)S(1)} %copy-done.3), custom_call_target="tpu_custom_call" | custom-call | tf_op jit(solution)/shard_map/sketches/pallas_call | solution.py:62
  14.3 1.9 %copy-done.1 = f32[128,8192]{1,0:T(8,128)} copy-done((f32[128,8192]{1,0:T(8,128)}, f32[128,8192]{1,0:T(8,128)S(1)}, u32[]{:S(2)}) %copy-start.1) | copy-done | bytes 4194328
  16.4 1.6 %collective-permute-done = f32[704,128]{1,0:T(8,128)S(1)} collective-permute-done((f32[704,128]{1,0:T(8,128)S(1)}, f32[704,128]{1,0:T(8,128)S(1)}, u32[]{:S(2)}, u32[]{:S(2)}) %collective-permute-start) | collective-permute-done | bytes 360480 | tf_op jit(solution)/shard_map/ppermute | solution.py:226
  18.2 1.6 %collective-permute-start.1 = (f32[176,128]{1,0:T(8,128)S(1)}, f32[176,128]{1,0:T(8,128)S(1)}, u32[]{:S(2)}, u32[]{:S(2)}) collective-permute-start(f32[176,128]{1,0:T(8,128)S(1)} %get-tuple-element.20), channel_id=1, source_target_pairs={{0,2},{1,3},{2,0},{3,1},{4,6},{5,7},{6,4},{7,5},{8,10},{9,11},{10,... | collective-permute-start | bytes 270344 | tf_op jit(solution)/shard_map/ppermute | solution.py:226
  19.8 1.5 %collective-permute-start.2 = (f32[176,128]{1,0:T(8,128)S(1)}, f32[176,128]{1,0:T(8,128)S(1)}, u32[]{:S(2)}, u32[]{:S(2)}) collective-permute-start(f32[176,128]{1,0:T(8,128)S(1)} %get-tuple-element.21), channel_id=1, source_target_pairs={{0,4},{1,5},{2,6},{3,7},{4,0},{5,1},{6,2},{7,3},{8,12},{9,13},{10,... | collective-permute-start | bytes 270344 | tf_op jit(solution)/shard_map/ppermute | solution.py:226
  21.7 1.2 %collective-permute-done.1 = f32[176,128]{1,0:T(8,128)S(1)} collective-permute-done((f32[176,128]{1,0:T(8,128)S(1)}, f32[176,128]{1,0:T(8,128)S(1)}, u32[]{:S(2)}, u32[]{:S(2)}) %collective-permute-start.1) | collective-permute-done | bytes 90144 | tf_op jit(solution)/shard_map/ppermute | solution.py:226
  22.9 2.4 %collective-permute-done.2 = f32[176,128]{1,0:T(8,128)S(1)} collective-permute-done((f32[176,128]{1,0:T(8,128)S(1)}, f32[176,128]{1,0:T(8,128)S(1)}, u32[]{:S(2)}, u32[]{:S(2)}) %collective-permute-start.2) | collective-permute-done | bytes 90144 | tf_op jit(solution)/shard_map/ppermute | solution.py:226
  25.3 1.4 %collective-permute-done.3 = f32[176,128]{1,0:T(8,128)S(1)} collective-permute-done((f32[176,128]{1,0:T(8,128)S(1)}, f32[176,128]{1,0:T(8,128)S(1)}, u32[]{:S(2)}, u32[]{:S(2)}) %collective-permute-start.3) | collective-permute-done | bytes 90144 | tf_op jit(solution)/shard_map/ppermute | solution.py:226
  27.3 2.6 %collective-permute-start.5 = (f32[80,128]{1,0:T(8,128)S(1)}, f32[80,128]{1,0:T(8,128)S(1)}, u32[]{:S(2)}, u32[]{:S(2)}) collective-permute-start(f32[80,128]{1,0:T(8,128)S(1)} %get-tuple-element.24), channel_id=1, source_target_pairs={{0,16},{1,17},{2,18},{3,19},{4,20},{5,21},{6,22},{7,23},{8,24},{9,... | collective-permute-start | bytes 122888 | tf_op jit(solution)/shard_map/ppermute | solution.py:226
  30.4 0.9 %collective-permute-done.4 = f32[80,128]{1,0:T(8,128)S(1)} collective-permute-done((f32[80,128]{1,0:T(8,128)S(1)}, f32[80,128]{1,0:T(8,128)S(1)}, u32[]{:S(2)}, u32[]{:S(2)}) %collective-permute-start.4) | collective-permute-done | bytes 40992 | tf_op jit(solution)/shard_map/ppermute | solution.py:226
  31.3 1.1 %collective-permute-done.5 = f32[80,128]{1,0:T(8,128)S(1)} collective-permute-done((f32[80,128]{1,0:T(8,128)S(1)}, f32[80,128]{1,0:T(8,128)S(1)}, u32[]{:S(2)}, u32[]{:S(2)}) %collective-permute-start.5) | collective-permute-done | bytes 40992 | tf_op jit(solution)/shard_map/ppermute | solution.py:226
  32.4 1.5 %collective-permute-done.6 = f32[80,128]{1,0:T(8,128)S(1)} collective-permute-done((f32[80,128]{1,0:T(8,128)S(1)}, f32[80,128]{1,0:T(8,128)S(1)}, u32[]{:S(2)}, u32[]{:S(2)}) %collective-permute-start.6) | collective-permute-done | bytes 40992 | tf_op jit(solution)/shard_map/ppermute | solution.py:226
  34.6 1.0 %collective-permute-start.8 = (f32[48,128]{1,0:T(8,128)S(1)}, f32[48,128]{1,0:T(8,128)S(1)}, u32[]{:S(2)}, u32[]{:S(2)}) collective-permute-start(f32[48,128]{1,0:T(8,128)S(1)} %slice.80), channel_id=1, source_target_pairs={{0,4},{1,5},{2,6},{3,7},{4,0},{5,1},{6,2},{7,3},{8,12},{9,13},{10,... | collective-permute-start | bytes 73736 | tf_op jit(solution)/shard_map/ppermute | solution.py:235
  35.6 1.9 %collective-permute-start.9 = (f32[48,128]{1,0:T(8,128)S(1)}, f32[48,128]{1,0:T(8,128)S(1)}, u32[]{:S(2)}, u32[]{:S(2)}) collective-permute-start(f32[48,128]{1,0:T(8,128)S(1)} %slice.80), channel_id=1, source_target_pairs={{0,6},{1,7},{2,4},{3,5},{4,2},{5,3},{6,0},{7,1},{8,14},{9,15},{10,... | collective-permute-start | bytes 73736 | tf_op jit(solution)/shard_map/ppermute | solution.py:235
  38.4 1.9 %collective-permute-done.9 = f32[48,128]{1,0:T(8,128)S(1)} collective-permute-done((f32[48,128]{1,0:T(8,128)S(1)}, f32[48,128]{1,0:T(8,128)S(1)}, u32[]{:S(2)}, u32[]{:S(2)}) %collective-permute-start.9) | collective-permute-done | bytes 24608 | tf_op jit(solution)/shard_map/ppermute | solution.py:235
  40.3 1.3 %collective-permute-done.10 = f32[192,128]{1,0:T(8,128)S(1)} collective-permute-done((f32[192,128]{1,0:T(8,128)S(1)}, f32[192,128]{1,0:T(8,128)S(1)}, u32[]{:S(2)}, u32[]{:S(2)}) %collective-permute-start.10) | collective-permute-done | bytes 98336 | tf_op jit(solution)/shard_map/ppermute | solution.py:235
  41.7 2.2 %copy-done.2 = f32[128,8192]{1,0:T(8,128)S(1)} copy-done((f32[128,8192]{1,0:T(8,128)S(1)}, f32[128,8192]{1,0:T(8,128)}, u32[]{:S(2)}) %copy-start.2) | copy-done | bytes 4194328
  43.8 28.0 %solve.1 = (f32[128,16]{1,0:T(8,128)S(1)}, f32[8,1024]{1,0:T(8,128)S(1)}, f32[8,1024]{1,0:T(8,128)S(1)}) custom-call(f32[384,128]{1,0:T(8,128)S(1)} %bitcast.64, f32[2,16,128]{2,1,0:T(8,128)S(1)} %bitcast.68, f32[128,8192]{1,0:T(8,128)S(1)} %copy-done.2, f32[8,1024]{1,0:T(8,128)S(1)} %copy-done.4, s32[8,1024]{1,0:T(8,128)S(1)} %copy-done.5, f32[4]{0:T(128)S(1)} %copy-done.6), custom_call_target="tpu_custom_call" | custom-call | tf_op jit(solution)/shard_map/solve/pallas_call | solution.py:192
  71.9 6.4 %collective-permute-start.12 = (f32[2,1024]{1,0:T(2,128)S(1)}, f32[2,1024]{1,0:T(2,128)S(1)}, u32[]{:S(2)}, u32[]{:S(2)}) collective-permute-start(f32[2,1024]{1,0:T(2,128)S(1)} %pad_maximum_fusion.2), channel_id=1, source_target_pairs={{1,0},{2,1},{3,2},{4,3},{5,4},{6,5},{7,6},{8,7},{9,8},{10,9},{11,1... | collective-permute-start | bytes 24584 | tf_op jit(solution)/shard_map/ppermute | solution.py:286
  78.3 1.9 %collective-permute-start.11 = (f32[2,1024]{1,0:T(2,128)S(1)}, f32[2,1024]{1,0:T(2,128)S(1)}, u32[]{:S(2)}, u32[]{:S(2)}) collective-permute-start(f32[2,1024]{1,0:T(2,128)S(1)} %pad_maximum_fusion.1), channel_id=1, source_target_pairs={{0,1},{1,2},{2,3},{3,4},{4,5},{5,6},{6,7},{7,8},{8,9},{9,10},{10,1... | collective-permute-start | bytes 24584 | tf_op jit(solution)/shard_map/ppermute | solution.py:285
  81.0 4.1 %collective-permute-done.11 = f32[2,1024]{1,0:T(2,128)S(1)} collective-permute-done((f32[2,1024]{1,0:T(2,128)S(1)}, f32[2,1024]{1,0:T(2,128)S(1)}, u32[]{:S(2)}, u32[]{:S(2)}) %collective-permute-start.11) | collective-permute-done | bytes 8224 | tf_op jit(solution)/shard_map/ppermute | solution.py:285
  85.2 0.7 fusion.32
  (50 shorter events, 4.2 us)
Async XLA Ops:
  0.6 2.2 %copy-start = (bf16[256,8192]{1,0:T(8,128)(2,1)S(1)}, bf16[256,8192]{1,0:T(8,128)(2,1)}, u32[]{:S(2)}) copy-start(bf16[256,8192]{1,0:T(8,128)(2,1)} %test.1) | copy-start | bytes 12582916
  2.8 0.9 %copy-start.3 = (bf16[512,128]{1,0:T(8,128)(2,1)S(1)}, bf16[512,128]{1,0:T(8,128)(2,1)}, u32[]{:S(2)}) copy-start(bf16[512,128]{1,0:T(8,128)(2,1)} %om.1) | copy-start | bytes 393220
  14.3 1.9 %copy-start.1 = (f32[128,8192]{1,0:T(8,128)}, f32[128,8192]{1,0:T(8,128)S(1)}, u32[]{:S(2)}) copy-start(f32[128,8192]{1,0:T(8,128)S(1)} %get-tuple-element.10.range_t) | copy-start | bytes 12582916
  16.2 25.4 %copy-start.4 = (f32[8,1024]{1,0:T(8,128)S(1)}, f32[8,1024]{1,0:T(8,128)}, u32[]{:S(2)}) copy-start(f32[8,1024]{1,0:T(8,128)} %adjoint.1) | copy-start | bytes 98308
  16.2 25.4 %copy-start.5 = (s32[8,1024]{1,0:T(8,128)S(1)}, s32[8,1024]{1,0:T(8,128)}, u32[]{:S(2)}) copy-start(s32[8,1024]{1,0:T(8,128)} %species.1) | copy-start | bytes 98308
  16.2 25.4 %copy-start.6 = (f32[4]{0:T(128)S(1)}, f32[4]{0:T(128)}, u32[]{:S(2)}) copy-start(f32[4]{0:T(128)} %rates.1) | copy-start | bytes 52
  16.3 1.7 %collective-permute-start = (f32[704,128]{1,0:T(8,128)S(1)}, f32[704,128]{1,0:T(8,128)S(1)}, u32[]{:S(2)}, u32[]{:S(2)}) collective-permute-start(f32[704,128]{1,0:T(8,128)S(1)} %fusion.1), channel_id=1, source_target_pairs={{0,1},{1,0},{2,3},{3,2},{4,5},{5,4},{6,7},{7,6},{8,9},{9,8},{10,11... | collective-permute-start | bytes 1081352 | tf_op jit(solution)/shard_map/ppermute | solution.py:226
  18.2 4.7 %collective-permute-start.1 = (f32[176,128]{1,0:T(8,128)S(1)}, f32[176,128]{1,0:T(8,128)S(1)}, u32[]{:S(2)}, u32[]{:S(2)}) collective-permute-start(f32[176,128]{1,0:T(8,128)S(1)} %get-tuple-element.20), channel_id=1, source_target_pairs={{0,2},{1,3},{2,0},{3,1},{4,6},{5,7},{6,4},{7,5},{8,10},{9,11},{10,... | collective-permute-start | bytes 270344 | tf_op jit(solution)/shard_map/ppermute | solution.py:226
  19.8 5.5 %collective-permute-start.2 = (f32[176,128]{1,0:T(8,128)S(1)}, f32[176,128]{1,0:T(8,128)S(1)}, u32[]{:S(2)}, u32[]{:S(2)}) collective-permute-start(f32[176,128]{1,0:T(8,128)S(1)} %get-tuple-element.21), channel_id=1, source_target_pairs={{0,4},{1,5},{2,6},{3,7},{4,0},{5,1},{6,2},{7,3},{8,12},{9,13},{10,... | collective-permute-start | bytes 270344 | tf_op jit(solution)/shard_map/ppermute | solution.py:226
  21.3 5.4 %collective-permute-start.3 = (f32[176,128]{1,0:T(8,128)S(1)}, f32[176,128]{1,0:T(8,128)S(1)}, u32[]{:S(2)}, u32[]{:S(2)}) collective-permute-start(f32[176,128]{1,0:T(8,128)S(1)} %get-tuple-element.22), channel_id=1, source_target_pairs={{0,6},{1,7},{2,4},{3,5},{4,2},{5,3},{6,0},{7,1},{8,14},{9,15},{10,... | collective-permute-start | bytes 270344 | tf_op jit(solution)/shard_map/ppermute | solution.py:226
  26.8 4.5 %collective-permute-start.4 = (f32[80,128]{1,0:T(8,128)S(1)}, f32[80,128]{1,0:T(8,128)S(1)}, u32[]{:S(2)}, u32[]{:S(2)}) collective-permute-start(f32[80,128]{1,0:T(8,128)S(1)} %get-tuple-element.23), channel_id=1, source_target_pairs={{0,8},{1,9},{2,10},{3,11},{4,12},{5,13},{6,14},{7,15},{8,0},{9,1},... | collective-permute-start | bytes 122888 | tf_op jit(solution)/shard_map/ppermute | solution.py:226
  27.3 5.1 %collective-permute-start.5 = (f32[80,128]{1,0:T(8,128)S(1)}, f32[80,128]{1,0:T(8,128)S(1)}, u32[]{:S(2)}, u32[]{:S(2)}) collective-permute-start(f32[80,128]{1,0:T(8,128)S(1)} %get-tuple-element.24), channel_id=1, source_target_pairs={{0,16},{1,17},{2,18},{3,19},{4,20},{5,21},{6,22},{7,23},{8,24},{9,... | collective-permute-start | bytes 122888 | tf_op jit(solution)/shard_map/ppermute | solution.py:226
  29.9 4.0 %collective-permute-start.6 = (f32[80,128]{1,0:T(8,128)S(1)}, f32[80,128]{1,0:T(8,128)S(1)}, u32[]{:S(2)}, u32[]{:S(2)}) collective-permute-start(f32[80,128]{1,0:T(8,128)S(1)} %get-tuple-element.25), channel_id=1, source_target_pairs={{0,24},{1,25},{2,26},{3,27},{4,28},{5,29},{6,30},{7,31},{8,16},{9,... | collective-permute-start | bytes 122888 | tf_op jit(solution)/shard_map/ppermute | solution.py:226
  33.9 3.9 %collective-permute-start.7 = (f32[48,128]{1,0:T(8,128)S(1)}, f32[48,128]{1,0:T(8,128)S(1)}, u32[]{:S(2)}, u32[]{:S(2)}) collective-permute-start(f32[48,128]{1,0:T(8,128)S(1)} %slice.80), channel_id=1, source_target_pairs={{0,2},{1,3},{2,0},{3,1},{4,6},{5,7},{6,4},{7,5},{8,10},{9,11},{10,... | collective-permute-start | bytes 73736 | tf_op jit(solution)/shard_map/ppermute | solution.py:235
  34.6 3.8 %collective-permute-start.8 = (f32[48,128]{1,0:T(8,128)S(1)}, f32[48,128]{1,0:T(8,128)S(1)}, u32[]{:S(2)}, u32[]{:S(2)}) collective-permute-start(f32[48,128]{1,0:T(8,128)S(1)} %slice.80), channel_id=1, source_target_pairs={{0,4},{1,5},{2,6},{3,7},{4,0},{5,1},{6,2},{7,3},{8,12},{9,13},{10,... | collective-permute-start | bytes 73736 | tf_op jit(solution)/shard_map/ppermute | solution.py:235
  35.6 4.7 %collective-permute-start.9 = (f32[48,128]{1,0:T(8,128)S(1)}, f32[48,128]{1,0:T(8,128)S(1)}, u32[]{:S(2)}, u32[]{:S(2)}) collective-permute-start(f32[48,128]{1,0:T(8,128)S(1)} %slice.80), channel_id=1, source_target_pairs={{0,6},{1,7},{2,4},{3,5},{4,2},{5,3},{6,0},{7,1},{8,14},{9,15},{10,... | collective-permute-start | bytes 73736 | tf_op jit(solution)/shard_map/ppermute | solution.py:235
  40.3 1.3 %collective-permute-start.10 = (f32[192,128]{1,0:T(8,128)S(1)}, f32[192,128]{1,0:T(8,128)S(1)}, u32[]{:S(2)}, u32[]{:S(2)}) collective-permute-start(f32[192,128]{1,0:T(8,128)S(1)} %bitcast.78), channel_id=1, source_target_pairs={{0,1},{1,0},{2,3},{3,2},{4,5},{5,4},{6,7},{7,6},{8,9},{9,8},{10,11... | collective-permute-start | bytes 294920 | tf_op jit(solution)/shard_map/ppermute | solution.py:235
  41.7 2.2 %copy-start.2 = (f32[128,8192]{1,0:T(8,128)S(1)}, f32[128,8192]{1,0:T(8,128)}, u32[]{:S(2)}) copy-start(f32[128,8192]{1,0:T(8,128)} %copy-done.1) | copy-start | bytes 12582916
  71.9 9.1 %collective-permute-start.12 = (f32[2,1024]{1,0:T(2,128)S(1)}, f32[2,1024]{1,0:T(2,128)S(1)}, u32[]{:S(2)}, u32[]{:S(2)}) collective-permute-start(f32[2,1024]{1,0:T(2,128)S(1)} %pad_maximum_fusion.2), channel_id=1, source_target_pairs={{1,0},{2,1},{3,2},{4,3},{5,4},{6,5},{7,6},{8,7},{9,8},{10,9},{11,1... | collective-permute-start | bytes 24584 | tf_op jit(solution)/shard_map/ppermute | solution.py:286
  78.3 6.8 %collective-permute-start.11 = (f32[2,1024]{1,0:T(2,128)S(1)}, f32[2,1024]{1,0:T(2,128)S(1)}, u32[]{:S(2)}, u32[]{:S(2)}) collective-permute-start(f32[2,1024]{1,0:T(2,128)S(1)} %pad_maximum_fusion.1), channel_id=1, source_target_pairs={{0,1},{1,2},{2,3},{3,4},{4,5},{5,6},{6,7},{7,8},{8,9},{9,10},{10,1... | collective-permute-start | bytes 24584 | tf_op jit(solution)/shard_map/ppermute | solution.py:285

commit v2 on v1

--- a/solution.py
+++ b/solution.py
@@ -16,82 +16,123 @@
 BF16 = jnp.bfloat16
 
 
-def sketch_kernel(snap, test, om, range_t, ct, crit, om_t, corange, gram):
-    step = pl.program_id(0)
+def sketch_kernel(
+    chunks, ahead, snap, test, om, range_out, ct, crit, snap_v, test_v, om_v, range_t, om_t, corange, gram, split, sems
+):
+    cells, times = snap.shape
     rank = om.shape[1]
     sketch = test.shape[0]
-    times = snap.shape[1]
-
-    @pl.when(step == 0)
-    def _():
-        om_t[...] = om[...].astype(F32).T.astype(BF16)
-        corange[...] = jnp.zeros_like(corange)
-        gram[...] = jnp.zeros_like(gram)
-
-    states = snap[...]
-    rt = lax.dot_general(om_t[...], states, NT, preferred_element_type=F32)
-    range_t[...] = rt
-    upper = rt.astype(BF16)
-    lower = (rt - upper.astype(F32)).astype(BF16)
-    both = jnp.concatenate([upper, lower], axis=0)
-    gram[...] += lax.dot_general(both, both, NT, preferred_element_type=F32)
-    corange[...] += jnp.dot(test[...], states, preferred_element_type=F32)
-
-    @pl.when(step == pl.num_programs(0) - 1)
-    def _():
-        whole = corange[...]
-        projected = jnp.dot(whole, om[...].astype(F32), precision=HIGH, preferred_element_type=F32)
-        crit[0:sketch, :] = projected
-        cross = gram[0:rank, rank:]
-        crit[sketch:, :] = gram[0:rank, 0:rank] + cross + cross.T
-        half = sketch // 2
-        for h in range(2):
-            turned = whole[h * half : (h + 1) * half, :].T
-            ct[h] = turned
-            for j in range(2):
-                row = turned[times - 2 + j : times - 1 + j, :]
-                for q in range(2):
-                    place = sketch + j * 4 + h * 2 + q
-                    crit[place : place + 1, rank // 2 :] = row[:, q * 64 : (q + 1) * 64]
-
-
-def sketches(snapshots, range_test, test_rows, block=1024):
+    block = cells // chunks
+
+    def place(i):
+        return pl.ds(pl.multiple_of(i * block, block), block)
+
+    def copies(i):
+        at = place(i)
+        return (
+            pltpu.make_async_copy(snap.at[at, :], snap_v.at[at, :], sems.at[2 * i]),
+            pltpu.make_async_copy(test.at[:, at], test_v.at[:, at], sems.at[2 * i + 1]),
+        )
+
+    def leaving(i):
+        return pltpu.make_async_copy(range_t.at[:, place(i)], range_out.at[:, place(i)], sems.at[2 * chunks + 1 + i])
+
+    own = pltpu.make_async_copy(om, om_v, sems.at[2 * chunks])
+    own.start()
+    for i in range(min(ahead, chunks)):
+        for copy in copies(i):
+            copy.start()
+    corange[...] = jnp.zeros_like(corange)
+    gram[...] = jnp.zeros_like(gram)
+    split[1] = jnp.zeros(split.shape[1:], BF16)
+    own.wait()
+    om_t[...] = om_v[...].astype(F32).T.astype(BF16)
+
+    def step(i, carry):
+        for copy in copies(i):
+            copy.wait()
+
+        @pl.when(i + ahead < chunks)
+        def _():
+            for copy in copies(i + ahead):
+                copy.start()
+
+        at = place(i)
+        states = snap_v[at, :]
+        before = split[(i + 1) % 2]
+        gram[...] += lax.dot_general(before, before, NT, preferred_element_type=F32)
+        rt = lax.dot_general(om_t[...], states, NT, preferred_element_type=F32)
+        range_t[:, at] = rt
+        leaving(i).start()
+        upper = rt.astype(BF16)
+        split[i % 2, 0:rank] = upper
+        split[i % 2, rank:] = (rt - upper.astype(F32)).astype(BF16)
+        corange[...] += jnp.dot(test_v[:, at], states, preferred_element_type=F32)
+        return carry
+
+    lax.fori_loop(0, chunks, step, 0)
+    last = split[(chunks + 1) % 2]
+    gram[...] += lax.dot_general(last, last, NT, preferred_element_type=F32)
+    whole = corange[...]
+    crit[0:sketch, :] = jnp.dot(whole, om_v[...].astype(F32), precision=HIGH, preferred_element_type=F32)
+    cross = gram[0:rank, rank:]
+    crit[sketch:, :] = gram[0:rank, 0:rank] + cross + cross.T
+    half = sketch // 2
+    for h in range(2):
+        turned = whole[h * half : (h + 1) * half, :].T
+        ct[h] = turned
+        for j in range(2):
+            row = turned[times - 2 + j : times - 1 + j, :]
+            for q in range(2):
+                there = sketch + j * 4 + h * 2 + q
+                crit[there : there + 1, rank // 2 :] = row[:, q * 64 : (q + 1) * 64]
+    for i in range(chunks):
+        leaving(i).wait()
+
+
+def sketches(snapshots, range_test, test_rows, chunks=8, ahead=3):
     cells, times = snapshots.shape
     rank = range_test.shape[1]
     sketch = test_rows.shape[0]
+    far = pl.BlockSpec(memory_space=pltpu.HBM)
+    near = pl.BlockSpec(memory_space=pltpu.VMEM)
     return pl.pallas_call(
-        sketch_kernel,
-        grid=(cells // block,),
-        in_specs=[
-            pl.BlockSpec((block, times), lambda i: (i, 0)),
-            pl.BlockSpec((sketch, block), lambda i: (0, i)),
-            pl.BlockSpec((times, rank), lambda i: (0, 0)),
-        ],
-        out_specs=[
-            pl.BlockSpec((rank, block), lambda i: (0, i)),
-            pl.BlockSpec((2, times, sketch // 2), lambda i: (0, 0, 0)),
-            pl.BlockSpec((sketch + rank, rank), lambda i: (0, 0)),
-        ],
+        functools.partial(sketch_kernel, chunks, ahead),
+        in_specs=[far, far, far],
+        out_specs=[far, near, near],
         out_shape=[
-            jax.ShapeDtypeStruct((rank, cells), F32),
+            pltpu.HBM((rank, cells), F32),
             jax.ShapeDtypeStruct((2, times, sketch // 2), F32),
             jax.ShapeDtypeStruct((sketch + rank, rank), F32),
         ],
         scratch_shapes=[
+            pltpu.VMEM((cells, times), BF16),
+            pltpu.VMEM((sketch, cells), BF16),
+            pltpu.VMEM((times, rank), BF16),
+            pltpu.VMEM((rank, cells), F32),
             pltpu.VMEM((rank, times), BF16),
             pltpu.VMEM((sketch, times), F32),
             pltpu.VMEM((2 * rank, 2 * rank), F32),
+            pltpu.VMEM((2, 2 * rank, cells // chunks), BF16),
+            pltpu.SemaphoreType.DMA((3 * chunks + 1,)),
         ],
-        compiler_params=pltpu.CompilerParams(
-            dimension_semantics=("arbitrary",), vmem_limit_bytes=40 * 2**20
-        ),
+        compiler_params=pltpu.CompilerParams(vmem_limit_bytes=40 * 2**20),
         name="sketches",
-    )(snapshots, test_rows, range_test)
+    )(*[pltpu.with_memory_space_constraint(x, pltpu.HBM) for x in (snapshots, test_rows, range_test)])
 
 
 def solve_kernel(
-    cells_total, owned, crit, mine, range_t, adjoint, species, rates, factors, first, second, augmented, lhs, upper
+    cells_total, owned, crit, mine, range_in, adjoint, species, rates, factors, first, second,
+    augmented, lhs, upper, chol, range_t, sems
 ):
+    pieces = sems.shape[0]
+    many = range_in.shape[0] // pieces
+    arriving = [
+        pltpu.make_async_copy(range_in.at[pl.ds(i * many, many)], range_t.at[pl.ds(i * many, many)], sems.at[i])
+        for i in range(pieces)
+    ]
+    for copy in arriving:
+        copy.start()
     sketch = mine.shape[2] * 2
     rank = crit.shape[1]
     half = sketch // 2
@@ -114,25 +155,48 @@
     col_id = lax.broadcasted_iota(jnp.int32, (rank, rank), 1)
     upper[...] = jnp.where(col_id > row_id, gram.T, gram)
 
-    sub = lax.broadcasted_iota(jnp.int32, (8, 1), 0)
-    lane = lax.broadcasted_iota(jnp.int32, (1, rank), 1)
+    sub = lax.broadcasted_iota(jnp.int32, (8, rank), 0)
+    lane = lax.broadcasted_iota(jnp.int32, (8, rank), 1)
     tiles = rank // 8
-    for b in range(tiles):
-        rows = slice(8 * b, 8 * b + 8)
-        tile, _ = reduced(augmented[rows, :], 8 * b, sub)
-        augmented[rows, :] = tile
-        for i in range(tiles):
-            if i != b:
-                eliminate(augmented, i, b, tile)
-        tile, roots = reduced(upper[rows, :], 8 * b, sub)
-        for i in range(b + 1, tiles):
-            eliminate(upper, i, b, tile)
-        upper[rows, :] = jnp.where(lane >= 8 * b + sub, roots, 0.0)
+    per = tiles // 2
+    size = 8 * per
+    for start in range(0, rank, size):
+        here = slice(start, start + size)
+        left = [[augmented[start + 8 * i : start + 8 * i + 8, :rank], augmented[start + 8 * i : start + 8 * i + 8, rank:]] for i in range(per)]
+        right = [[upper[start + 8 * i : start + 8 * i + 8, :]] for i in range(per)]
+        for b in range(per):
+            at = start + 8 * b
+            left[b], _ = reduced(left[b], at, sub)
+            right[b], roots = reduced(right[b], at, sub)
+            chol[at : at + 8, :] = jnp.where(lane >= at + sub, roots, 0.0)
+            for i in range(b + 1, b + per):
+                left[i % per] = eliminated(left[i % per], at, left[b])
+                right[i % per] = eliminated(right[i % per], at, right[b])
+        panel = [jnp.concatenate([row[p] for row in left], axis=0) for p in range(2)]
+        panel = jnp.concatenate(panel, axis=1)
+        others = [slice(0, start), slice(start + size, rank)]
+        taken = jnp.concatenate([augmented[o, :rank] for o in others if o.stop > o.start], axis=0)
+        change = jnp.dot(taken, spread(panel, start, rank), precision=HIGH, preferred_element_type=F32)
+        done = 0
+        for o in others:
+            if o.stop > o.start:
+                many = o.stop - o.start
+                augmented[o, :] = augmented[o, :] - change[done : done + many, :]
+                done += many
+        augmented[here, :] = panel
+        rest = slice(start + size, rank)
+        if rest.stop > rest.start:
+            panel = jnp.concatenate([row[0] for row in right], axis=0)
+            upper[rest, :] = upper[rest, :] - jnp.dot(
+                upper[rest, :], spread(panel, start, rank), precision=HIGH, preferred_element_type=F32
+            )
 
     solved = augmented[:, rank:]
-    out = jnp.dot(upper[...], solved, precision=HIGH, preferred_element_type=F32) * cells_total**-0.5
+    out = jnp.dot(chol[...], solved, precision=HIGH, preferred_element_type=F32) * cells_total**-0.5
     factors[...] = out[:, 0:owned]
 
+    for copy in arriving:
+        copy.wait()
     rows_here, width = adjoint.shape
     for r in range(rows_here):
         sums = [jnp.zeros((8, width), F32) for _ in range(2)]
@@ -159,29 +223,38 @@
     second[...] = coupling * (1.0 - 3.0 * state * state)
 
 
+def spread(panel, first, rank):
+    rows = [jnp.zeros((first, panel.shape[1]), F32), panel, jnp.zeros((rank - first - panel.shape[0], panel.shape[1]), F32)]
+    return jnp.concatenate([r for r in rows if r.shape[0]], axis=0)
+
+
 def reduced(tile, first_col, sub):
-    cols = [tile[:, first_col + k : first_col + k + 1] for k in range(8)]
-    roots = tile
+    block = tile[0].shape
+    cols = [jnp.broadcast_to(tile[0][:, first_col + k : first_col + k + 1], block) for k in range(8)]
+    roots = tile[0]
     for k in range(8):
-        pivot = cols[k][k : k + 1, :]
+        pivot = jnp.broadcast_to(cols[k][k : k + 1, :], block)
         inverse = 1.0 / pivot
-        row = tile[k : k + 1, :]
-        scaled = row * inverse
-        roots = jnp.where(sub == k, row * lax.rsqrt(pivot), roots)
-        tile = jnp.where(sub == k, scaled, tile - cols[k] * scaled)
+        rows = [jnp.broadcast_to(part[k : k + 1, :], block) for part in tile]
+        here = sub == k
+        roots = jnp.where(here, rows[0] * lax.rsqrt(pivot), roots)
+        scaled = [row * inverse for row in rows]
+        tile = [jnp.where(here, row, part - cols[k] * row) for row, part in zip(scaled, tile)]
         for m in range(k + 1, 8):
-            value = cols[m][k : k + 1, :] * inverse
-            cols[m] = jnp.where(sub == k, value, cols[m] - cols[k] * value)
+            value = jnp.broadcast_to(cols[m][k : k + 1, :], block) * inverse
+            cols[m] = jnp.where(here, value, cols[m] - cols[k] * value)
     return tile, roots
 
 
-def eliminate(ref, i, b, tile):
-    there = slice(8 * i, 8 * i + 8)
-    other = ref[there, :]
-    cols = [other[:, 8 * b + k : 8 * b + k + 1] for k in range(8)]
-    for k in range(8):
-        other = other - cols[k] * tile[k : k + 1, :]
-    ref[there, :] = other
+def eliminated(parts, first_col, tile):
+    cols = [jnp.broadcast_to(parts[0][:, first_col + k : first_col + k + 1], tile[0].shape) for k in range(8)]
+    out = []
+    for part, known in zip(parts, tile):
+        terms = [cols[k] * jnp.broadcast_to(known[k : k + 1, :], part.shape) for k in range(8)]
+        while len(terms) > 1:
+            terms = [terms[i] + terms[i + 1] for i in range(0, len(terms), 2)]
+        out.append(part - terms[0])
+    return out
 
 
 def solve(crit, mine, range_t, adjoint, species, rates, cells_total):
@@ -191,7 +264,7 @@
     vmem = pl.BlockSpec(memory_space=pltpu.VMEM)
     return pl.pallas_call(
         functools.partial(solve_kernel, cells_total, owned),
-        in_specs=[vmem, vmem, vmem, vmem, vmem, pl.BlockSpec(memory_space=pltpu.SMEM)],
+        in_specs=[vmem, vmem, pl.BlockSpec(memory_space=pltpu.HBM), vmem, vmem, pl.BlockSpec(memory_space=pltpu.SMEM)],
         out_specs=[vmem, vmem, vmem],
         out_shape=[
             jax.ShapeDtypeStruct((rank, owned), F32),
@@ -202,10 +275,13 @@
             pltpu.VMEM((rank, 2 * rank), F32),
             pltpu.VMEM((rank, sketch), F32),
             pltpu.VMEM((rank, rank), F32),
+            pltpu.VMEM((rank, rank), F32),
+            pltpu.VMEM(range_t.shape, F32),
+            pltpu.SemaphoreType.DMA((8,)),
         ],
-        compiler_params=pltpu.CompilerParams(vmem_limit_bytes=40 * 2**20),
+        compiler_params=pltpu.CompilerParams(vmem_limit_bytes=16 * 2**20),
         name="solve",
-    )(crit, mine, range_t, adjoint, species, rates)
+    )(crit, mine, pltpu.with_memory_space_constraint(range_t, pltpu.HBM), adjoint, species, rates)
 
 
 def partners(count, shift, other):
@@ -280,14 +356,19 @@
     range_t, ct, crit = sketches(snapshots, range_test, test_rows)
     crit, mine = reduce_sketches(crit, ct, count)
     time_factors, partial, rate = solve(crit, mine, range_t, adjoint_end, species, reaction_rates, cells_total)
-    forward = [(i, i + 1) for i in range(count - 1)]
-    backward = [(i + 1, i) for i in range(count - 1)]
-    above = lax.ppermute(jnp.concatenate([partial[-1:], adjoint_end[-1:]], axis=0), AXES, forward)
-    below = lax.ppermute(jnp.concatenate([partial[:1], adjoint_end[:1]], axis=0), AXES, backward)
+    device = lax.axis_index(AXES)
+    even = device % 2 == 0
+    head = jnp.concatenate([partial[:1], adjoint_end[:1]], axis=0)
+    tail = jnp.concatenate([partial[-1:], adjoint_end[-1:]], axis=0)
+    pairs = [(i, i ^ 1) for i in range(count)]
+    across = [(i, i + 1) for i in range(1, count - 1, 2)] + [(i + 1, i) for i in range(1, count - 1, 2)]
+    far = lax.ppermute(jnp.where(even, head, tail), AXES, across)
+    near = lax.ppermute(jnp.where(even, tail, head), AXES, pairs)
+    above = jnp.where(even, far, near)
+    below = jnp.where(even, near, far)
     adjoint = jnp.concatenate(
         [partial[:1] + DIFFUSION * above[1:], partial[1:-1], partial[-1:] + DIFFUSION * below[1:]], axis=0
     )
-    device = lax.axis_index(AXES)
     top = jnp.where(device > 0, above[:1] + DIFFUSION * adjoint_end[:1], 0.0)
     bottom = jnp.where(device < count - 1, below[:1] + DIFFUSION * adjoint_end[-1:], 0.0)
     padded = jnp.concatenate([top, adjoint, bottom], axis=0)

time: 86.3 us -> 54.5 us (0.63)
  the two profiles are of different devices: /device:TPU:8 before, /device:TPU:1 now
where the time goes in v2:
time: 54.5 us; the launch traced here: 53.9 us
  starting transfers between devices  18.8 us (34%)
  Pallas kernels  17.9 us (33%)
  waiting for transfers between devices  14.4 us (26%)
  other arithmetic  0.94 us (2%)
  between operations  0.92 us (2%)
  local copies, waits for them, and re-layouts  0.88 us (2%)
    ppermute x7, waiting for transfers between devices, summed_pieces(): lax.ppermute(pick(pieces, me ^ p), AXES, partners(count, shift, p))  10.7 us
    pallas_call x1, Pallas kernels, sketches(): pl.pallas_call(functools.partial(sketch_kernel, chunks, ahead), in_specs=...  9.51 us
    pallas_call x1, Pallas kernels, solve(): pl.pallas_call(functools.partial(solve_kernel, cells_total, owned), in_sp...  8.42 us
    ppermute x4, starting transfers between devices, gathered_pieces(): lax.ppermute(piece, AXES, partners(count, shift, p))  7.95 us
    ppermute x7, starting transfers between devices, summed_pieces(): lax.ppermute(pick(pieces, me ^ p), AXES, partners(count, shift, p))  7.46 us
    ppermute x1, starting transfers between devices, shards(): far = lax.ppermute(jnp.where(even, head, tail), AXES, across)  3.36 us
    ppermute x4, waiting for transfers between devices, gathered_pieces(): lax.ppermute(piece, AXES, partners(count, shift, p))  2.94 us
  transfers between devices with their start and end apart: 13, of which 11 were waited for; matrix products, arithmetic and copies ran while one was open for 1% of the time, Pallas kernels for 0%

profile of v2, /device:TPU:1, one launch (start us, length us, event | category | flops | bytes accessed | tf_op | source)
XLA Modules:
  0.0 53.9 jit_solution(4688673915981011687)
XLA Ops:
  0.6 9.5 %sketches.1 = (f32[128,8192]{1,0:T(8,128)}, f32[2,512,128]{2,1,0:T(8,128)S(1)}, f32[384,128]{1,0:T(8,128)S(1)}) custom-call(bf16[8192,512]{1,0:T(8,128)(2,1)} %snap.1, bf16[256,8192]{1,0:T(8,128)(2,1)} %test.1, bf16[512,128]{1,0:T(8,128)(2,1)} %om.1), custom_call_target="tpu_custom_call" | custom-call | tf_op jit(solution)/shard_map/sketches/pallas_call | solution.py:99
  10.4 1.6 %collective-permute-done = f32[704,128]{1,0:T(8,128)S(1)} collective-permute-done((f32[704,128]{1,0:T(8,128)S(1)}, f32[704,128]{1,0:T(8,128)S(1)}, u32[]{:S(2)}, u32[]{:S(2)}) %collective-permute-start) | collective-permute-done | bytes 360480 | tf_op jit(solution)/shard_map/ppermute | solution.py:302
  12.2 2.4 %collective-permute-start.1 = (f32[176,128]{1,0:T(8,128)S(1)}, f32[176,128]{1,0:T(8,128)S(1)}, u32[]{:S(2)}, u32[]{:S(2)}) collective-permute-start(f32[176,128]{1,0:T(8,128)S(1)} %get-tuple-element.20), channel_id=1, source_target_pairs={{0,2},{1,3},{2,0},{3,1},{4,6},{5,7},{6,4},{7,5},{8,10},{9,11},{10,... | collective-permute-start | bytes 270344 | tf_op jit(solution)/shard_map/ppermute | solution.py:302
  14.6 1.2 %collective-permute-start.2 = (f32[176,128]{1,0:T(8,128)S(1)}, f32[176,128]{1,0:T(8,128)S(1)}, u32[]{:S(2)}, u32[]{:S(2)}) collective-permute-start(f32[176,128]{1,0:T(8,128)S(1)} %get-tuple-element.21), channel_id=1, source_target_pairs={{0,4},{1,5},{2,6},{3,7},{4,0},{5,1},{6,2},{7,3},{8,12},{9,13},{10,... | collective-permute-start | bytes 270344 | tf_op jit(solution)/shard_map/ppermute | solution.py:302
  15.8 1.4 %collective-permute-done.1 = f32[176,128]{1,0:T(8,128)S(1)} collective-permute-done((f32[176,128]{1,0:T(8,128)S(1)}, f32[176,128]{1,0:T(8,128)S(1)}, u32[]{:S(2)}, u32[]{:S(2)}) %collective-permute-start.1) | collective-permute-done | bytes 90144 | tf_op jit(solution)/shard_map/ppermute | solution.py:302
  17.3 0.7 %collective-permute-done.2 = f32[176,128]{1,0:T(8,128)S(1)} collective-permute-done((f32[176,128]{1,0:T(8,128)S(1)}, f32[176,128]{1,0:T(8,128)S(1)}, u32[]{:S(2)}, u32[]{:S(2)}) %collective-permute-start.2) | collective-permute-done | bytes 90144 | tf_op jit(solution)/shard_map/ppermute | solution.py:302
  18.0 2.1 %collective-permute-done.3 = f32[176,128]{1,0:T(8,128)S(1)} collective-permute-done((f32[176,128]{1,0:T(8,128)S(1)}, f32[176,128]{1,0:T(8,128)S(1)}, u32[]{:S(2)}, u32[]{:S(2)}) %collective-permute-start.3) | collective-permute-done | bytes 90144 | tf_op jit(solution)/shard_map/ppermute | solution.py:302
  20.2 1.4 %collective-permute-start.4 = (f32[80,128]{1,0:T(8,128)S(1)}, f32[80,128]{1,0:T(8,128)S(1)}, u32[]{:S(2)}, u32[]{:S(2)}) collective-permute-start(f32[80,128]{1,0:T(8,128)S(1)} %get-tuple-element.23), channel_id=1, source_target_pairs={{0,8},{1,9},{2,10},{3,11},{4,12},{5,13},{6,14},{7,15},{8,0},{9,1},... | collective-permute-start | bytes 122888 | tf_op jit(solution)/shard_map/ppermute | solution.py:302
  21.6 2.3 %collective-permute-start.5 = (f32[80,128]{1,0:T(8,128)S(1)}, f32[80,128]{1,0:T(8,128)S(1)}, u32[]{:S(2)}, u32[]{:S(2)}) collective-permute-start(f32[80,128]{1,0:T(8,128)S(1)} %get-tuple-element.24), channel_id=1, source_target_pairs={{0,16},{1,17},{2,18},{3,19},{4,20},{5,21},{6,22},{7,23},{8,24},{9,... | collective-permute-start | bytes 122888 | tf_op jit(solution)/shard_map/ppermute | solution.py:302
  23.9 1.9 %collective-permute-done.5 = f32[80,128]{1,0:T(8,128)S(1)} collective-permute-done((f32[80,128]{1,0:T(8,128)S(1)}, f32[80,128]{1,0:T(8,128)S(1)}, u32[]{:S(2)}, u32[]{:S(2)}) %collective-permute-start.5) | collective-permute-done | bytes 40992 | tf_op jit(solution)/shard_map/ppermute | solution.py:302
  25.8 2.9 %collective-permute-done.6 = f32[80,128]{1,0:T(8,128)S(1)} collective-permute-done((f32[80,128]{1,0:T(8,128)S(1)}, f32[80,128]{1,0:T(8,128)S(1)}, u32[]{:S(2)}, u32[]{:S(2)}) %collective-permute-start.6) | collective-permute-done | bytes 40992 | tf_op jit(solution)/shard_map/ppermute | solution.py:302
  28.7 1.0 %collective-permute-start.7 = (f32[48,128]{1,0:T(8,128)S(1)}, f32[48,128]{1,0:T(8,128)S(1)}, u32[]{:S(2)}, u32[]{:S(2)}) collective-permute-start(f32[48,128]{1,0:T(8,128)S(1)} %slice.80), channel_id=1, source_target_pairs={{0,2},{1,3},{2,0},{3,1},{4,6},{5,7},{6,4},{7,5},{8,10},{9,11},{10,... | collective-permute-start | bytes 73736 | tf_op jit(solution)/shard_map/ppermute | solution.py:311
  29.7 0.2 collective-permute-start.8
  29.9 1.5 %collective-permute-start.9 = (f32[48,128]{1,0:T(8,128)S(1)}, f32[48,128]{1,0:T(8,128)S(1)}, u32[]{:S(2)}, u32[]{:S(2)}) collective-permute-start(f32[48,128]{1,0:T(8,128)S(1)} %slice.80), channel_id=1, source_target_pairs={{0,6},{1,7},{2,4},{3,5},{4,2},{5,3},{6,0},{7,1},{8,14},{9,15},{10,... | collective-permute-start | bytes 73736 | tf_op jit(solution)/shard_map/ppermute | solution.py:311
  31.4 0.3 collective-permute-done.7
  31.7 0.6 %collective-permute-done.8 = f32[48,128]{1,0:T(8,128)S(1)} collective-permute-done((f32[48,128]{1,0:T(8,128)S(1)}, f32[48,128]{1,0:T(8,128)S(1)}, u32[]{:S(2)}, u32[]{:S(2)}) %collective-permute-start.8) | collective-permute-done | bytes 24608 | tf_op jit(solution)/shard_map/ppermute | solution.py:311
  32.4 1.1 %collective-permute-done.9 = f32[48,128]{1,0:T(8,128)S(1)} collective-permute-done((f32[48,128]{1,0:T(8,128)S(1)}, f32[48,128]{1,0:T(8,128)S(1)}, u32[]{:S(2)}, u32[]{:S(2)}) %collective-permute-start.9) | collective-permute-done | bytes 24608 | tf_op jit(solution)/shard_map/ppermute | solution.py:311
  33.5 5.2 %collective-permute-start.10 = (f32[192,128]{1,0:T(8,128)S(1)}, f32[192,128]{1,0:T(8,128)S(1)}, u32[]{:S(2)}, u32[]{:S(2)}) collective-permute-start(f32[192,128]{1,0:T(8,128)S(1)} %bitcast.78), channel_id=1, source_target_pairs={{0,1},{1,0},{2,3},{3,2},{4,5},{5,4},{6,7},{7,6},{8,9},{9,8},{10,11... | collective-permute-start | bytes 294920 | tf_op jit(solution)/shard_map/ppermute | solution.py:311
  38.8 0.9 %collective-permute-done.10 = f32[192,128]{1,0:T(8,128)S(1)} collective-permute-done((f32[192,128]{1,0:T(8,128)S(1)}, f32[192,128]{1,0:T(8,128)S(1)}, u32[]{:S(2)}, u32[]{:S(2)}) %collective-permute-start.10) | collective-permute-done | bytes 98336 | tf_op jit(solution)/shard_map/ppermute | solution.py:311
  39.7 8.4 %solve.1 = (f32[128,16]{1,0:T(8,128)S(1)}, f32[8,1024]{1,0:T(8,128)S(1)}, f32[8,1024]{1,0:T(8,128)S(1)}) custom-call(f32[384,128]{1,0:T(8,128)S(1)} %bitcast.64, f32[2,16,128]{2,1,0:T(8,128)S(1)} %bitcast.68, f32[128,8192]{1,0:T(8,128)} %get-tuple-element.10.range_in, f32[8,1024]{1,0:T(8,128)S(1)} %copy-done, s32[8,1024]{1,0:T(8,128)S(1)} %copy-done.1, ...), custom_call_target="tpu_custom_call" | custom-call | tf_op jit(solution)/shard_map/solve/pallas_call | solution.py:265
  48.2 3.4 %collective-permute-start.11 = (f32[2,1024]{1,0:T(2,128)S(1)}, f32[2,1024]{1,0:T(2,128)S(1)}, u32[]{:S(2)}, u32[]{:S(2)}) collective-permute-start(f32[2,1024]{1,0:T(2,128)S(1)} %get-tuple-element.38), channel_id=1, source_target_pairs={{1,2},{3,4},{5,6},{7,8},{9,10},{11,12},{13,14},{15,16},{17,18},{19... | collective-permute-start | bytes 24584 | tf_op jit(solution)/shard_map/ppermute | solution.py:365
  51.7 0.7 %copy.14 = f32[128,16]{0,1:T(8,128)} copy(f32[128,16]{1,0:T(8,128)S(1)} %get-tuple-element.19) | data formatting | bytes 16384
  52.3 0.8 %collective-permute-done.11 = f32[2,1024]{1,0:T(2,128)S(1)} collective-permute-done((f32[2,1024]{1,0:T(2,128)S(1)}, f32[2,1024]{1,0:T(2,128)S(1)}, u32[]{:S(2)}, u32[]{:S(2)}) %collective-permute-start.11) | collective-permute-done | bytes 8224 | tf_op jit(solution)/shard_map/ppermute | solution.py:365
  53.2 0.7 %fusion.32 = f32[8,1024]{1,0:T(8,128)} fusion(f32[8,1024]{1,0:T(8,128)S(1)} %pad_maximum_fusion, f32[1,1024]{1,0:T(1,128)S(1)} %get-tuple-element.34, f32[1,1024]{1,0:T(1,128)S(1)} %get-tuple-element.29, f32[6,1024]{1,0:T(8,128)S(1)} %slice.70, f32[1,1024]{1,0:T(1,128)S(1)} %get-tuple-element.28, f32[1,1024]{1,0:T(1,128)S(1)} %get-tuple-element.35, ...), kind=kLoop, calls=%fused_computation.56 | loop fusion | flops 106496 | bytes 139264 | tf_op jit(solution)/shard_map/add | solution.py:377
  (42 shorter events, 0.7 us)
Async XLA Ops:
  10.2 29.5 %copy-start = (f32[8,1024]{1,0:T(8,128)S(1)}, f32[8,1024]{1,0:T(8,128)}, u32[]{:S(2)}) copy-start(f32[8,1024]{1,0:T(8,128)} %adjoint.1) | copy-start | bytes 98308
  10.2 29.5 %copy-start.1 = (s32[8,1024]{1,0:T(8,128)S(1)}, s32[8,1024]{1,0:T(8,128)}, u32[]{:S(2)}) copy-start(s32[8,1024]{1,0:T(8,128)} %species.1) | copy-start | bytes 98308
  10.2 29.5 %copy-start.2 = (f32[4]{0:T(128)S(1)}, f32[4]{0:T(128)}, u32[]{:S(2)}) copy-start(f32[4]{0:T(128)} %rates.1) | copy-start | bytes 52
  10.3 1.7 %collective-permute-start = (f32[704,128]{1,0:T(8,128)S(1)}, f32[704,128]{1,0:T(8,128)S(1)}, u32[]{:S(2)}, u32[]{:S(2)}) collective-permute-start(f32[704,128]{1,0:T(8,128)S(1)} %fusion.1), channel_id=1, source_target_pairs={{0,1},{1,0},{2,3},{3,2},{4,5},{5,4},{6,7},{7,6},{8,9},{9,8},{10,11... | collective-permute-start | bytes 1081352 | tf_op jit(solution)/shard_map/ppermute | solution.py:302
  12.2 5.1 %collective-permute-start.1 = (f32[176,128]{1,0:T(8,128)S(1)}, f32[176,128]{1,0:T(8,128)S(1)}, u32[]{:S(2)}, u32[]{:S(2)}) collective-permute-start(f32[176,128]{1,0:T(8,128)S(1)} %get-tuple-element.20), channel_id=1, source_target_pairs={{0,2},{1,3},{2,0},{3,1},{4,6},{5,7},{6,4},{7,5},{8,10},{9,11},{10,... | collective-permute-start | bytes 270344 | tf_op jit(solution)/shard_map/ppermute | solution.py:302
  14.6 3.4 %collective-permute-start.2 = (f32[176,128]{1,0:T(8,128)S(1)}, f32[176,128]{1,0:T(8,128)S(1)}, u32[]{:S(2)}, u32[]{:S(2)}) collective-permute-start(f32[176,128]{1,0:T(8,128)S(1)} %get-tuple-element.21), channel_id=1, source_target_pairs={{0,4},{1,5},{2,6},{3,7},{4,0},{5,1},{6,2},{7,3},{8,12},{9,13},{10,... | collective-permute-start | bytes 270344 | tf_op jit(solution)/shard_map/ppermute | solution.py:302
  15.8 4.3 %collective-permute-start.3 = (f32[176,128]{1,0:T(8,128)S(1)}, f32[176,128]{1,0:T(8,128)S(1)}, u32[]{:S(2)}, u32[]{:S(2)}) collective-permute-start(f32[176,128]{1,0:T(8,128)S(1)} %get-tuple-element.22), channel_id=1, source_target_pairs={{0,6},{1,7},{2,4},{3,5},{4,2},{5,3},{6,0},{7,1},{8,14},{9,15},{10,... | collective-permute-start | bytes 270344 | tf_op jit(solution)/shard_map/ppermute | solution.py:302
  20.2 3.7 %collective-permute-start.4 = (f32[80,128]{1,0:T(8,128)S(1)}, f32[80,128]{1,0:T(8,128)S(1)}, u32[]{:S(2)}, u32[]{:S(2)}) collective-permute-start(f32[80,128]{1,0:T(8,128)S(1)} %get-tuple-element.23), channel_id=1, source_target_pairs={{0,8},{1,9},{2,10},{3,11},{4,12},{5,13},{6,14},{7,15},{8,0},{9,1},... | collective-permute-start | bytes 122888 | tf_op jit(solution)/shard_map/ppermute | solution.py:302
  21.6 4.2 %collective-permute-start.5 = (f32[80,128]{1,0:T(8,128)S(1)}, f32[80,128]{1,0:T(8,128)S(1)}, u32[]{:S(2)}, u32[]{:S(2)}) collective-permute-start(f32[80,128]{1,0:T(8,128)S(1)} %get-tuple-element.24), channel_id=1, source_target_pairs={{0,16},{1,17},{2,18},{3,19},{4,20},{5,21},{6,22},{7,23},{8,24},{9,... | collective-permute-start | bytes 122888 | tf_op jit(solution)/shard_map/ppermute | solution.py:302
  23.9 4.8 %collective-permute-start.6 = (f32[80,128]{1,0:T(8,128)S(1)}, f32[80,128]{1,0:T(8,128)S(1)}, u32[]{:S(2)}, u32[]{:S(2)}) collective-permute-start(f32[80,128]{1,0:T(8,128)S(1)} %get-tuple-element.25), channel_id=1, source_target_pairs={{0,24},{1,25},{2,26},{3,27},{4,28},{5,29},{6,30},{7,31},{8,16},{9,... | collective-permute-start | bytes 122888 | tf_op jit(solution)/shard_map/ppermute | solution.py:302
  28.7 3.0 %collective-permute-start.7 = (f32[48,128]{1,0:T(8,128)S(1)}, f32[48,128]{1,0:T(8,128)S(1)}, u32[]{:S(2)}, u32[]{:S(2)}) collective-permute-start(f32[48,128]{1,0:T(8,128)S(1)} %slice.80), channel_id=1, source_target_pairs={{0,2},{1,3},{2,0},{3,1},{4,6},{5,7},{6,4},{7,5},{8,10},{9,11},{10,... | collective-permute-start | bytes 73736 | tf_op jit(solution)/shard_map/ppermute | solution.py:311
  29.7 2.7 %collective-permute-start.8 = (f32[48,128]{1,0:T(8,128)S(1)}, f32[48,128]{1,0:T(8,128)S(1)}, u32[]{:S(2)}, u32[]{:S(2)}) collective-permute-start(f32[48,128]{1,0:T(8,128)S(1)} %slice.80), channel_id=1, source_target_pairs={{0,4},{1,5},{2,6},{3,7},{4,0},{5,1},{6,2},{7,3},{8,12},{9,13},{10,... | collective-permute-start | bytes 73736 | tf_op jit(solution)/shard_map/ppermute | solution.py:311
  29.9 3.6 %collective-permute-start.9 = (f32[48,128]{1,0:T(8,128)S(1)}, f32[48,128]{1,0:T(8,128)S(1)}, u32[]{:S(2)}, u32[]{:S(2)}) collective-permute-start(f32[48,128]{1,0:T(8,128)S(1)} %slice.80), channel_id=1, source_target_pairs={{0,6},{1,7},{2,4},{3,5},{4,2},{5,3},{6,0},{7,1},{8,14},{9,15},{10,... | collective-permute-start | bytes 73736 | tf_op jit(solution)/shard_map/ppermute | solution.py:311
  33.5 6.2 %collective-permute-start.10 = (f32[192,128]{1,0:T(8,128)S(1)}, f32[192,128]{1,0:T(8,128)S(1)}, u32[]{:S(2)}, u32[]{:S(2)}) collective-permute-start(f32[192,128]{1,0:T(8,128)S(1)} %bitcast.78), channel_id=1, source_target_pairs={{0,1},{1,0},{2,3},{3,2},{4,5},{5,4},{6,7},{7,6},{8,9},{9,8},{10,11... | collective-permute-start | bytes 294920 | tf_op jit(solution)/shard_map/ppermute | solution.py:311
  48.2 5.0 %collective-permute-start.11 = (f32[2,1024]{1,0:T(2,128)S(1)}, f32[2,1024]{1,0:T(2,128)S(1)}, u32[]{:S(2)}, u32[]{:S(2)}) collective-permute-start(f32[2,1024]{1,0:T(2,128)S(1)} %get-tuple-element.38), channel_id=1, source_target_pairs={{1,2},{3,4},{5,6},{7,8},{9,10},{11,12},{13,14},{15,16},{17,18},{19... | collective-permute-start | bytes 24584 | tf_op jit(solution)/shard_map/ppermute | solution.py:365
  51.6 1.6 %collective-permute-start.12 = (f32[2,1024]{1,0:T(2,128)S(1)}, f32[2,1024]{1,0:T(2,128)S(1)}, u32[]{:S(2)}, u32[]{:S(2)}) collective-permute-start(f32[2,1024]{1,0:T(2,128)S(1)} %get-tuple-element.39), channel_id=1, source_target_pairs={{0,1},{1,0},{2,3},{3,2},{4,5},{5,4},{6,7},{7,6},{8,9},{9,8},{10,11... | collective-permute-start | bytes 24584 | tf_op jit(solution)/shard_map/ppermute | solution.py:366

commit v3 on v2

--- a/solution.py
+++ b/solution.py
@@ -122,17 +122,9 @@
 
 
 def solve_kernel(
-    cells_total, owned, crit, mine, range_in, adjoint, species, rates, factors, first, second,
-    augmented, lhs, upper, chol, range_t, sems
+    cells_total, owned, crit, mine, range_t, adjoint, species, rates, factors, first, second,
+    augmented, lhs, upper, chol
 ):
-    pieces = sems.shape[0]
-    many = range_in.shape[0] // pieces
-    arriving = [
-        pltpu.make_async_copy(range_in.at[pl.ds(i * many, many)], range_t.at[pl.ds(i * many, many)], sems.at[i])
-        for i in range(pieces)
-    ]
-    for copy in arriving:
-        copy.start()
     sketch = mine.shape[2] * 2
     rank = crit.shape[1]
     half = sketch // 2
@@ -193,10 +185,8 @@
 
     solved = augmented[:, rank:]
     out = jnp.dot(chol[...], solved, precision=HIGH, preferred_element_type=F32) * cells_total**-0.5
-    factors[...] = out[:, 0:owned]
-
-    for copy in arriving:
-        copy.wait()
+    factors[...] = out.T[0:owned]
+
     rows_here, width = adjoint.shape
     for r in range(rows_here):
         sums = [jnp.zeros((8, width), F32) for _ in range(2)]
@@ -257,6 +247,32 @@
     return out
 
 
+def fetch_kernel(source, out, sems):
+    pieces = sems.shape[0]
+    many = source.shape[0] // pieces
+    copies = [
+        pltpu.make_async_copy(source.at[pl.ds(i * many, many)], out.at[pl.ds(i * many, many)], sems.at[i])
+        for i in range(pieces)
+    ]
+    for copy in copies:
+        copy.start()
+    for copy in copies:
+        copy.wait()
+
+
+def fetch(array):
+    return pl.pallas_call(
+        fetch_kernel,
+        in_specs=[pl.BlockSpec(memory_space=pltpu.HBM)],
+        out_specs=pl.BlockSpec(memory_space=pltpu.VMEM),
+        out_shape=jax.ShapeDtypeStruct(array.shape, array.dtype),
+        scratch_shapes=[pltpu.SemaphoreType.DMA((8,))],
+        compiler_params=pltpu.CompilerParams(vmem_limit_bytes=2**20),
+        cost_estimate=pl.CostEstimate(flops=0, bytes_accessed=8 * array.size, transcendentals=0),
+        name="fetch",
+    )(pltpu.with_memory_space_constraint(array, pltpu.HBM))
+
+
 def solve(crit, mine, range_t, adjoint, species, rates, cells_total):
     owned = mine.shape[1]
     rank = crit.shape[1]
@@ -264,10 +280,10 @@
     vmem = pl.BlockSpec(memory_space=pltpu.VMEM)
     return pl.pallas_call(
         functools.partial(solve_kernel, cells_total, owned),
-        in_specs=[vmem, vmem, pl.BlockSpec(memory_space=pltpu.HBM), vmem, vmem, pl.BlockSpec(memory_space=pltpu.SMEM)],
+        in_specs=[vmem, vmem, vmem, vmem, vmem, pl.BlockSpec(memory_space=pltpu.SMEM)],
         out_specs=[vmem, vmem, vmem],
         out_shape=[
-            jax.ShapeDtypeStruct((rank, owned), F32),
+            jax.ShapeDtypeStruct((owned, rank), F32),
             jax.ShapeDtypeStruct(adjoint.shape, F32),
             jax.ShapeDtypeStruct(adjoint.shape, F32),
         ],
@@ -276,12 +292,10 @@
             pltpu.VMEM((rank, sketch), F32),
             pltpu.VMEM((rank, rank), F32),
             pltpu.VMEM((rank, rank), F32),
-            pltpu.VMEM(range_t.shape, F32),
-            pltpu.SemaphoreType.DMA((8,)),
         ],
         compiler_params=pltpu.CompilerParams(vmem_limit_bytes=16 * 2**20),
         name="solve",
-    )(crit, mine, pltpu.with_memory_space_constraint(range_t, pltpu.HBM), adjoint, species, rates)
+    )(crit, mine, range_t, adjoint, species, rates)
 
 
 def partners(count, shift, other):
@@ -325,7 +339,7 @@
     return out
 
 
-def reduce_sketches(crit, ct, count):
+def reduce_sketches(crit, ct, range_t, count):
     plan = stages(count)
     halves, times, width = ct.shape
     owned = times // count
@@ -339,6 +353,8 @@
         both = summed_pieces(jnp.concatenate([crit, ct], axis=1), count, shift)
         crit, ct = both[:split], both[split:].reshape(halves, left * owned, width)
     shift, size = plan[-1]
+    crit, ct, range_t = lax.optimization_barrier((crit, ct, range_t))
+    range_t = fetch(range_t)
     ct = ct.reshape(halves, size, owned, width)
     ct = jnp.moveaxis(ct, 1, 0).reshape(size, -1, width)
     split = crit.shape[0]
@@ -347,14 +363,14 @@
     crit, mine = both[:split], both[split:].reshape(halves, owned, width)
     for shift, size in plan[-2::-1]:
         crit = gathered_pieces(crit, count, shift, size).reshape(-1, width)
-    return crit, mine
+    return crit, mine, range_t
 
 
 def shards(snapshots, range_test, test_rows, species, reaction_rates, adjoint_end):
     count = lax.axis_size(AXES)
     cells_total = snapshots.shape[0] * count
     range_t, ct, crit = sketches(snapshots, range_test, test_rows)
-    crit, mine = reduce_sketches(crit, ct, count)
+    crit, mine, range_t = reduce_sketches(crit, ct, range_t, count)
     time_factors, partial, rate = solve(crit, mine, range_t, adjoint_end, species, reaction_rates, cells_total)
     device = lax.axis_index(AXES)
     even = device % 2 == 0
@@ -374,7 +390,7 @@
     padded = jnp.concatenate([top, adjoint, bottom], axis=0)
     sideways = jnp.pad(adjoint, ((0, 0), (1, 1)))
     laplace = padded[2:] + padded[:-2] + sideways[:, 2:] + sideways[:, :-2] - 4.0 * adjoint
-    return (adjoint + DIFFUSION * laplace + rate * adjoint, time_factors)
+    return (adjoint + DIFFUSION * laplace + rate * adjoint, time_factors.T)
 
 
 def solution(mesh):

time: 54.5 us -> 53.2 us (0.976)
  waiting for transfers between devices: 14.4 us -> 12.8 us
  Pallas kernels: 17.9 us -> 18.9 us
  local copies, waits for them, and re-layouts: 0.88 us -> 0.21 us
    ppermute x7, waiting for transfers between devices: 10.7 us -> 8.39 us  [summed_pieces(): lax.ppermute(pick(pieces, me ^ p), AXES, partners(count, shift, p))]
    pallas_call x0 -> x1, Pallas kernels: none -> 2.23 us  [fetch(): pl.pallas_call(fetch_kernel, in_specs=[pl.BlockSpec(memory_space=pltpu.HB...]
    pallas_call x1, Pallas kernels: 8.42 us -> 7.11 us  [solve(): pl.pallas_call(functools.partial(solve_kernel, cells_total, owned), in_sp...]
    unnamed x7 -> x6, local copies, waits for them, and re-layouts: 0.69 us -> 0.01 us
    ppermute x1, waiting for transfers between devices: 0.83 us -> 1.5 us  [shards(): far = lax.ppermute(jnp.where(even, head, tail), AXES, across)]
  transfers between devices with their start and end apart: 13 -> 13, of which waited for: 11 -> 10; matrix products, arithmetic and copies ran while one was open for 1% -> 0% of each run, Pallas kernels for 0% -> 4%
where the time goes in v3:
time: 53.2 us; the launch traced here: 52.6 us
  Pallas kernels  18.9 us (36%)
  starting transfers between devices  18.8 us (35%)
  waiting for transfers between devices  12.8 us (24%)
  other arithmetic  0.94 us (2%)
  between operations  0.91 us (2%)
    pallas_call x1, Pallas kernels, sketches(): pl.pallas_call(functools.partial(sketch_kernel, chunks, ahead), in_specs=...  9.51 us
    ppermute x7, waiting for transfers between devices, summed_pieces(): lax.ppermute(pick(pieces, me ^ p), AXES, partners(count, shift, p))  8.39 us
    ppermute x4, starting transfers between devices, gathered_pieces(): lax.ppermute(piece, AXES, partners(count, shift, p))  7.95 us
    ppermute x7, starting transfers between devices, summed_pieces(): lax.ppermute(pick(pieces, me ^ p), AXES, partners(count, shift, p))  7.46 us
    pallas_call x1, Pallas kernels, solve(): pl.pallas_call(functools.partial(solve_kernel, cells_total, owned), in_sp...  7.11 us
    ppermute x1, starting transfers between devices, shards(): far = lax.ppermute(jnp.where(even, head, tail), AXES, across)  3.36 us
    ppermute x4, waiting for transfers between devices, gathered_pieces(): lax.ppermute(piece, AXES, partners(count, shift, p))  2.94 us
    pallas_call x1, Pallas kernels, fetch(): pl.pallas_call(fetch_kernel, in_specs=[pl.BlockSpec(memory_space=pltpu.HB...  2.23 us
  transfers between devices with their start and end apart: 13, of which 10 were waited for; matrix products, arithmetic and copies ran while one was open for 0% of the time, Pallas kernels for 4%

profile of v3, /device:TPU:1, one launch (start us, length us, event | category | flops | bytes accessed | tf_op | source)
XLA Modules:
  0.0 52.6 jit_solution(8140780790025425627)
XLA Ops:
  0.6 9.5 %sketches.1 = (f32[128,8192]{1,0:T(8,128)}, f32[2,512,128]{2,1,0:T(8,128)S(1)}, f32[384,128]{1,0:T(8,128)S(1)}) custom-call(bf16[8192,512]{1,0:T(8,128)(2,1)} %snap.1, bf16[256,8192]{1,0:T(8,128)(2,1)} %test.1, bf16[512,128]{1,0:T(8,128)(2,1)} %om.1), custom_call_target="tpu_custom_call" | custom-call | tf_op jit(solution)/shard_map/sketches/pallas_call | solution.py:99
  10.2 0.1 collective-permute-start
  10.4 1.6 %collective-permute-done = f32[704,128]{1,0:T(8,128)S(1)} collective-permute-done((f32[704,128]{1,0:T(8,128)S(1)}, f32[704,128]{1,0:T(8,128)S(1)}, u32[]{:S(2)}, u32[]{:S(2)}) %collective-permute-start) | collective-permute-done | bytes 360480 | tf_op jit(solution)/shard_map/ppermute | solution.py:316
  12.1 2.4 %collective-permute-start.1 = (f32[176,128]{1,0:T(8,128)S(1)}, f32[176,128]{1,0:T(8,128)S(1)}, u32[]{:S(2)}, u32[]{:S(2)}) collective-permute-start(f32[176,128]{1,0:T(8,128)S(1)} %get-tuple-element.20), channel_id=1, source_target_pairs={{0,2},{1,3},{2,0},{3,1},{4,6},{5,7},{6,4},{7,5},{8,10},{9,11},{10,... | collective-permute-start | bytes 270344 | tf_op jit(solution)/shard_map/ppermute | solution.py:316
  14.5 1.2 %collective-permute-start.2 = (f32[176,128]{1,0:T(8,128)S(1)}, f32[176,128]{1,0:T(8,128)S(1)}, u32[]{:S(2)}, u32[]{:S(2)}) collective-permute-start(f32[176,128]{1,0:T(8,128)S(1)} %get-tuple-element.21), channel_id=1, source_target_pairs={{0,4},{1,5},{2,6},{3,7},{4,0},{5,1},{6,2},{7,3},{8,12},{9,13},{10,... | collective-permute-start | bytes 270344 | tf_op jit(solution)/shard_map/ppermute | solution.py:316
  15.8 1.4 %collective-permute-done.1 = f32[176,128]{1,0:T(8,128)S(1)} collective-permute-done((f32[176,128]{1,0:T(8,128)S(1)}, f32[176,128]{1,0:T(8,128)S(1)}, u32[]{:S(2)}, u32[]{:S(2)}) %collective-permute-start.1) | collective-permute-done | bytes 90144 | tf_op jit(solution)/shard_map/ppermute | solution.py:316
  17.2 0.7 %collective-permute-done.2 = f32[176,128]{1,0:T(8,128)S(1)} collective-permute-done((f32[176,128]{1,0:T(8,128)S(1)}, f32[176,128]{1,0:T(8,128)S(1)}, u32[]{:S(2)}, u32[]{:S(2)}) %collective-permute-start.2) | collective-permute-done | bytes 90144 | tf_op jit(solution)/shard_map/ppermute | solution.py:316
  17.9 2.1 %collective-permute-done.3 = f32[176,128]{1,0:T(8,128)S(1)} collective-permute-done((f32[176,128]{1,0:T(8,128)S(1)}, f32[176,128]{1,0:T(8,128)S(1)}, u32[]{:S(2)}, u32[]{:S(2)}) %collective-permute-start.3) | collective-permute-done | bytes 90144 | tf_op jit(solution)/shard_map/ppermute | solution.py:316
  20.2 1.4 %collective-permute-start.4 = (f32[80,128]{1,0:T(8,128)S(1)}, f32[80,128]{1,0:T(8,128)S(1)}, u32[]{:S(2)}, u32[]{:S(2)}) collective-permute-start(f32[80,128]{1,0:T(8,128)S(1)} %get-tuple-element.23), channel_id=1, source_target_pairs={{0,8},{1,9},{2,10},{3,11},{4,12},{5,13},{6,14},{7,15},{8,0},{9,1},... | collective-permute-start | bytes 122888 | tf_op jit(solution)/shard_map/ppermute | solution.py:316
  21.5 2.3 %collective-permute-start.5 = (f32[80,128]{1,0:T(8,128)S(1)}, f32[80,128]{1,0:T(8,128)S(1)}, u32[]{:S(2)}, u32[]{:S(2)}) collective-permute-start(f32[80,128]{1,0:T(8,128)S(1)} %get-tuple-element.24), channel_id=1, source_target_pairs={{0,16},{1,17},{2,18},{3,19},{4,20},{5,21},{6,22},{7,23},{8,24},{9,... | collective-permute-start | bytes 122888 | tf_op jit(solution)/shard_map/ppermute | solution.py:316
  23.9 2.2 %fetch.1.range_t = f32[128,8192]{1,0:T(8,128)S(1)} custom-call(f32[128,8192]{1,0:T(8,128)} %get-tuple-element.16.source), custom_call_target="tpu_custom_call" | custom-call | bytes 8388608 | tf_op jit(solution)/shard_map/fetch/pallas_call | solution.py:264
  26.1 2.5 %collective-permute-done.6 = f32[80,128]{1,0:T(8,128)S(1)} collective-permute-done((f32[80,128]{1,0:T(8,128)S(1)}, f32[80,128]{1,0:T(8,128)S(1)}, u32[]{:S(2)}, u32[]{:S(2)}) %collective-permute-start.6) | collective-permute-done | bytes 40992 | tf_op jit(solution)/shard_map/ppermute | solution.py:316
  28.7 1.0 %collective-permute-start.7 = (f32[48,128]{1,0:T(8,128)S(1)}, f32[48,128]{1,0:T(8,128)S(1)}, u32[]{:S(2)}, u32[]{:S(2)}) collective-permute-start(f32[48,128]{1,0:T(8,128)S(1)} %slice.80), channel_id=1, source_target_pairs={{0,2},{1,3},{2,0},{3,1},{4,6},{5,7},{6,4},{7,5},{8,10},{9,11},{10,... | collective-permute-start | bytes 73736 | tf_op jit(solution)/shard_map/ppermute | solution.py:325
  29.6 0.2 collective-permute-start.8
  29.9 1.5 %collective-permute-start.9 = (f32[48,128]{1,0:T(8,128)S(1)}, f32[48,128]{1,0:T(8,128)S(1)}, u32[]{:S(2)}, u32[]{:S(2)}) collective-permute-start(f32[48,128]{1,0:T(8,128)S(1)} %slice.80), channel_id=1, source_target_pairs={{0,6},{1,7},{2,4},{3,5},{4,2},{5,3},{6,0},{7,1},{8,14},{9,15},{10,... | collective-permute-start | bytes 73736 | tf_op jit(solution)/shard_map/ppermute | solution.py:325
  31.4 0.3 collective-permute-done.7
  31.7 0.6 %collective-permute-done.8 = f32[48,128]{1,0:T(8,128)S(1)} collective-permute-done((f32[48,128]{1,0:T(8,128)S(1)}, f32[48,128]{1,0:T(8,128)S(1)}, u32[]{:S(2)}, u32[]{:S(2)}) %collective-permute-start.8) | collective-permute-done | bytes 24608 | tf_op jit(solution)/shard_map/ppermute | solution.py:325
  32.3 1.1 %collective-permute-done.9 = f32[48,128]{1,0:T(8,128)S(1)} collective-permute-done((f32[48,128]{1,0:T(8,128)S(1)}, f32[48,128]{1,0:T(8,128)S(1)}, u32[]{:S(2)}, u32[]{:S(2)}) %collective-permute-start.9) | collective-permute-done | bytes 24608 | tf_op jit(solution)/shard_map/ppermute | solution.py:325
  33.4 5.2 %collective-permute-start.10 = (f32[192,128]{1,0:T(8,128)S(1)}, f32[192,128]{1,0:T(8,128)S(1)}, u32[]{:S(2)}, u32[]{:S(2)}) collective-permute-start(f32[192,128]{1,0:T(8,128)S(1)} %bitcast.80), channel_id=1, source_target_pairs={{0,1},{1,0},{2,3},{3,2},{4,5},{5,4},{6,7},{7,6},{8,9},{9,8},{10,11... | collective-permute-start | bytes 294920 | tf_op jit(solution)/shard_map/ppermute | solution.py:325
  38.7 0.9 %collective-permute-done.10 = f32[192,128]{1,0:T(8,128)S(1)} collective-permute-done((f32[192,128]{1,0:T(8,128)S(1)}, f32[192,128]{1,0:T(8,128)S(1)}, u32[]{:S(2)}, u32[]{:S(2)}) %collective-permute-start.10) | collective-permute-done | bytes 98336 | tf_op jit(solution)/shard_map/ppermute | solution.py:325
  39.7 7.1 %solve.1 = (f32[16,128]{1,0:T(8,128)}, f32[8,1024]{1,0:T(8,128)S(1)}, f32[8,1024]{1,0:T(8,128)S(1)}) custom-call(f32[384,128]{1,0:T(8,128)S(1)} %bitcast.66, f32[2,16,128]{2,1,0:T(8,128)S(1)} %bitcast.70, f32[128,8192]{1,0:T(8,128)S(1)} %fetch.1.range_t, f32[8,1024]{1,0:T(8,128)S(1)} %copy-done, s32[8,1024]{1,0:T(8,128)S(1)} %copy-done.1, f32[4]{0:T(128)S(1)} %copy-done.2), custom_call_target="tpu_custom_call" | custom-call | tf_op jit(solution)/shard_map/solve/pallas_call | solution.py:281
  46.8 3.4 %collective-permute-start.11 = (f32[2,1024]{1,0:T(2,128)S(1)}, f32[2,1024]{1,0:T(2,128)S(1)}, u32[]{:S(2)}, u32[]{:S(2)}) collective-permute-start(f32[2,1024]{1,0:T(2,128)S(1)} %get-tuple-element.38), channel_id=1, source_target_pairs={{1,2},{3,4},{5,6},{7,8},{9,10},{11,12},{13,14},{15,16},{17,18},{19... | collective-permute-start | bytes 24584 | tf_op jit(solution)/shard_map/ppermute | solution.py:381
  50.3 1.5 %collective-permute-done.11 = f32[2,1024]{1,0:T(2,128)S(1)} collective-permute-done((f32[2,1024]{1,0:T(2,128)S(1)}, f32[2,1024]{1,0:T(2,128)S(1)}, u32[]{:S(2)}, u32[]{:S(2)}) %collective-permute-start.11) | collective-permute-done | bytes 8224 | tf_op jit(solution)/shard_map/ppermute | solution.py:381
  51.9 0.7 %fusion.32 = f32[8,1024]{1,0:T(8,128)} fusion(f32[8,1024]{1,0:T(8,128)S(1)} %pad_maximum_fusion, f32[1,1024]{1,0:T(1,128)S(1)} %get-tuple-element.34, f32[1,1024]{1,0:T(1,128)S(1)} %get-tuple-element.29, f32[6,1024]{1,0:T(8,128)S(1)} %slice.70, f32[1,1024]{1,0:T(1,128)S(1)} %get-tuple-element.28, f32[1,1024]{1,0:T(1,128)S(1)} %get-tuple-element.35, ...), kind=kLoop, calls=%fused_computation.56 | loop fusion | flops 106496 | bytes 139264 | tf_op jit(solution)/shard_map/add | solution.py:393
  (42 shorter events, 0.5 us)
Async XLA Ops:
  10.2 1.7 %collective-permute-start = (f32[704,128]{1,0:T(8,128)S(1)}, f32[704,128]{1,0:T(8,128)S(1)}, u32[]{:S(2)}, u32[]{:S(2)}) collective-permute-start(f32[704,128]{1,0:T(8,128)S(1)} %fusion.1), channel_id=1, source_target_pairs={{0,1},{1,0},{2,3},{3,2},{4,5},{5,4},{6,7},{7,6},{8,9},{9,8},{10,11... | collective-permute-start | bytes 1081352 | tf_op jit(solution)/shard_map/ppermute | solution.py:316
  12.1 5.1 %collective-permute-start.1 = (f32[176,128]{1,0:T(8,128)S(1)}, f32[176,128]{1,0:T(8,128)S(1)}, u32[]{:S(2)}, u32[]{:S(2)}) collective-permute-start(f32[176,128]{1,0:T(8,128)S(1)} %get-tuple-element.20), channel_id=1, source_target_pairs={{0,2},{1,3},{2,0},{3,1},{4,6},{5,7},{6,4},{7,5},{8,10},{9,11},{10,... | collective-permute-start | bytes 270344 | tf_op jit(solution)/shard_map/ppermute | solution.py:316
  14.5 3.4 %collective-permute-start.2 = (f32[176,128]{1,0:T(8,128)S(1)}, f32[176,128]{1,0:T(8,128)S(1)}, u32[]{:S(2)}, u32[]{:S(2)}) collective-permute-start(f32[176,128]{1,0:T(8,128)S(1)} %get-tuple-element.21), channel_id=1, source_target_pairs={{0,4},{1,5},{2,6},{3,7},{4,0},{5,1},{6,2},{7,3},{8,12},{9,13},{10,... | collective-permute-start | bytes 270344 | tf_op jit(solution)/shard_map/ppermute | solution.py:316
  15.8 4.3 %collective-permute-start.3 = (f32[176,128]{1,0:T(8,128)S(1)}, f32[176,128]{1,0:T(8,128)S(1)}, u32[]{:S(2)}, u32[]{:S(2)}) collective-permute-start(f32[176,128]{1,0:T(8,128)S(1)} %get-tuple-element.22), channel_id=1, source_target_pairs={{0,6},{1,7},{2,4},{3,5},{4,2},{5,3},{6,0},{7,1},{8,14},{9,15},{10,... | collective-permute-start | bytes 270344 | tf_op jit(solution)/shard_map/ppermute | solution.py:316
  20.2 5.9 %collective-permute-start.4 = (f32[80,128]{1,0:T(8,128)S(1)}, f32[80,128]{1,0:T(8,128)S(1)}, u32[]{:S(2)}, u32[]{:S(2)}) collective-permute-start(f32[80,128]{1,0:T(8,128)S(1)} %get-tuple-element.23), channel_id=1, source_target_pairs={{0,8},{1,9},{2,10},{3,11},{4,12},{5,13},{6,14},{7,15},{8,0},{9,1},... | collective-permute-start | bytes 122888 | tf_op jit(solution)/shard_map/ppermute | solution.py:316
  21.5 4.6 %collective-permute-start.5 = (f32[80,128]{1,0:T(8,128)S(1)}, f32[80,128]{1,0:T(8,128)S(1)}, u32[]{:S(2)}, u32[]{:S(2)}) collective-permute-start(f32[80,128]{1,0:T(8,128)S(1)} %get-tuple-element.24), channel_id=1, source_target_pairs={{0,16},{1,17},{2,18},{3,19},{4,20},{5,21},{6,22},{7,23},{8,24},{9,... | collective-permute-start | bytes 122888 | tf_op jit(solution)/shard_map/ppermute | solution.py:316
  23.8 4.8 %collective-permute-start.6 = (f32[80,128]{1,0:T(8,128)S(1)}, f32[80,128]{1,0:T(8,128)S(1)}, u32[]{:S(2)}, u32[]{:S(2)}) collective-permute-start(f32[80,128]{1,0:T(8,128)S(1)} %get-tuple-element.25), channel_id=1, source_target_pairs={{0,24},{1,25},{2,26},{3,27},{4,28},{5,29},{6,30},{7,31},{8,16},{9,... | collective-permute-start | bytes 122888 | tf_op jit(solution)/shard_map/ppermute | solution.py:316
  23.8 15.8 %copy-start = (f32[8,1024]{1,0:T(8,128)S(1)}, f32[8,1024]{1,0:T(8,128)}, u32[]{:S(2)}) copy-start(f32[8,1024]{1,0:T(8,128)} %adjoint.1) | copy-start | bytes 98308
  23.9 15.8 %copy-start.1 = (s32[8,1024]{1,0:T(8,128)S(1)}, s32[8,1024]{1,0:T(8,128)}, u32[]{:S(2)}) copy-start(s32[8,1024]{1,0:T(8,128)} %species.1) | copy-start | bytes 98308
  23.9 15.8 %copy-start.2 = (f32[4]{0:T(128)S(1)}, f32[4]{0:T(128)}, u32[]{:S(2)}) copy-start(f32[4]{0:T(128)} %rates.1) | copy-start | bytes 52
  28.7 3.0 %collective-permute-start.7 = (f32[48,128]{1,0:T(8,128)S(1)}, f32[48,128]{1,0:T(8,128)S(1)}, u32[]{:S(2)}, u32[]{:S(2)}) collective-permute-start(f32[48,128]{1,0:T(8,128)S(1)} %slice.80), channel_id=1, source_target_pairs={{0,2},{1,3},{2,0},{3,1},{4,6},{5,7},{6,4},{7,5},{8,10},{9,11},{10,... | collective-permute-start | bytes 73736 | tf_op jit(solution)/shard_map/ppermute | solution.py:325
  29.6 2.7 %collective-permute-start.8 = (f32[48,128]{1,0:T(8,128)S(1)}, f32[48,128]{1,0:T(8,128)S(1)}, u32[]{:S(2)}, u32[]{:S(2)}) collective-permute-start(f32[48,128]{1,0:T(8,128)S(1)} %slice.80), channel_id=1, source_target_pairs={{0,4},{1,5},{2,6},{3,7},{4,0},{5,1},{6,2},{7,3},{8,12},{9,13},{10,... | collective-permute-start | bytes 73736 | tf_op jit(solution)/shard_map/ppermute | solution.py:325
  29.9 3.6 %collective-permute-start.9 = (f32[48,128]{1,0:T(8,128)S(1)}, f32[48,128]{1,0:T(8,128)S(1)}, u32[]{:S(2)}, u32[]{:S(2)}) collective-permute-start(f32[48,128]{1,0:T(8,128)S(1)} %slice.80), channel_id=1, source_target_pairs={{0,6},{1,7},{2,4},{3,5},{4,2},{5,3},{6,0},{7,1},{8,14},{9,15},{10,... | collective-permute-start | bytes 73736 | tf_op jit(solution)/shard_map/ppermute | solution.py:325
  33.4 6.2 %collective-permute-start.10 = (f32[192,128]{1,0:T(8,128)S(1)}, f32[192,128]{1,0:T(8,128)S(1)}, u32[]{:S(2)}, u32[]{:S(2)}) collective-permute-start(f32[192,128]{1,0:T(8,128)S(1)} %bitcast.80), channel_id=1, source_target_pairs={{0,1},{1,0},{2,3},{3,2},{4,5},{5,4},{6,7},{7,6},{8,9},{9,8},{10,11... | collective-permute-start | bytes 294920 | tf_op jit(solution)/shard_map/ppermute | solution.py:325
  46.8 5.0 %collective-permute-start.11 = (f32[2,1024]{1,0:T(2,128)S(1)}, f32[2,1024]{1,0:T(2,128)S(1)}, u32[]{:S(2)}, u32[]{:S(2)}) collective-permute-start(f32[2,1024]{1,0:T(2,128)S(1)} %get-tuple-element.38), channel_id=1, source_target_pairs={{1,2},{3,4},{5,6},{7,8},{9,10},{11,12},{13,14},{15,16},{17,18},{19... | collective-permute-start | bytes 24584 | tf_op jit(solution)/shard_map/ppermute | solution.py:381
  50.2 1.6 %collective-permute-start.12 = (f32[2,1024]{1,0:T(2,128)S(1)}, f32[2,1024]{1,0:T(2,128)S(1)}, u32[]{:S(2)}, u32[]{:S(2)}) collective-permute-start(f32[2,1024]{1,0:T(2,128)S(1)} %get-tuple-element.39), channel_id=1, source_target_pairs={{0,1},{1,0},{2,3},{3,2},{4,5},{5,4},{6,7},{7,6},{8,9},{9,8},{10,11... | collective-permute-start | bytes 24584 | tf_op jit(solution)/shard_map/ppermute | solution.py:382

commit v4 on v3

--- a/solution.py
+++ b/solution.py
@@ -10,6 +10,7 @@
 DIFFUSION = 0.2
 STEP_SIZE = 0.05
 AXES = ("space", "tm")
+ROWS = 16
 HIGH = lax.Precision.HIGHEST
 NT = (((1,), (1,)), ((), ()))
 F32 = jnp.float32
@@ -147,35 +148,41 @@
     col_id = lax.broadcasted_iota(jnp.int32, (rank, rank), 1)
     upper[...] = jnp.where(col_id > row_id, gram.T, gram)
 
-    sub = lax.broadcasted_iota(jnp.int32, (8, rank), 0)
-    lane = lax.broadcasted_iota(jnp.int32, (8, rank), 1)
+    many = ROWS
+    sub = lax.broadcasted_iota(jnp.int32, (many, rank), 0)
+    lane = lax.broadcasted_iota(jnp.int32, (many, rank), 1)
     tiles = rank // 8
-    per = tiles // 2
-    size = 8 * per
+    size = rank // 2
+    per = size // many
     for start in range(0, rank, size):
-        here = slice(start, start + size)
-        left = [[augmented[start + 8 * i : start + 8 * i + 8, :rank], augmented[start + 8 * i : start + 8 * i + 8, rank:]] for i in range(per)]
-        right = [[upper[start + 8 * i : start + 8 * i + 8, :]] for i in range(per)]
+        left, right = [], []
+        for i in range(per):
+            rows = slice(start + many * i, start + many * (i + 1))
+            left.append([augmented[rows, :rank], augmented[rows, rank:]])
+            right.append([upper[rows, :]])
         for b in range(per):
-            at = start + 8 * b
-            left[b], _ = reduced(left[b], at, sub)
-            right[b], roots = reduced(right[b], at, sub)
-            chol[at : at + 8, :] = jnp.where(lane >= at + sub, roots, 0.0)
+            at = start + many * b
+            left[b], _ = reduced(left[b], at, sub, False)
+            right[b], roots = reduced(right[b], at, sub, True)
+            chol[at : at + many, :] = jnp.where(lane >= at + sub, roots, 0.0)
             for i in range(b + 1, b + per):
                 left[i % per] = eliminated(left[i % per], at, left[b])
-                right[i % per] = eliminated(right[i % per], at, right[b])
+            for i in range(b + 1, per):
+                right[i] = eliminated(right[i], at, right[b])
+            for i in range(b):
+                right[i] = eliminated(right[i], at, right[b])
         panel = [jnp.concatenate([row[p] for row in left], axis=0) for p in range(2)]
-        panel = jnp.concatenate(panel, axis=1)
-        others = [slice(0, start), slice(start + size, rank)]
-        taken = jnp.concatenate([augmented[o, :rank] for o in others if o.stop > o.start], axis=0)
+        ahead = slice(0 if start + size < rank else rank, 2 * rank)
+        panel = jnp.concatenate(panel, axis=1)[:, ahead]
+        others = [o for o in (slice(0, start), slice(start + size, rank)) if o.stop > o.start]
+        taken = jnp.concatenate([augmented[o, :rank] for o in others], axis=0)
         change = jnp.dot(taken, spread(panel, start, rank), precision=HIGH, preferred_element_type=F32)
         done = 0
         for o in others:
-            if o.stop > o.start:
-                many = o.stop - o.start
-                augmented[o, :] = augmented[o, :] - change[done : done + many, :]
-                done += many
-        augmented[here, :] = panel
+            count = o.stop - o.start
+            augmented[o, ahead] = augmented[o, ahead] - change[done : done + count, :]
+            done += count
+        augmented[start : start + size, ahead] = panel
         rest = slice(start + size, rank)
         if rest.stop > rest.start:
             panel = jnp.concatenate([row[0] for row in right], axis=0)
@@ -184,8 +191,8 @@
             )
 
     solved = augmented[:, rank:]
-    out = jnp.dot(chol[...], solved, precision=HIGH, preferred_element_type=F32) * cells_total**-0.5
-    factors[...] = out.T[0:owned]
+    out = jnp.dot(chol[...], solved, precision=HIGH, preferred_element_type=F32)
+    factors[...] = out[:, 0:owned] * cells_total**-0.5
 
     rows_here, width = adjoint.shape
     for r in range(rows_here):
@@ -218,29 +225,31 @@
     return jnp.concatenate([r for r in rows if r.shape[0]], axis=0)
 
 
-def reduced(tile, first_col, sub):
+def reduced(tile, first_col, sub, want_roots):
     block = tile[0].shape
-    cols = [jnp.broadcast_to(tile[0][:, first_col + k : first_col + k + 1], block) for k in range(8)]
+    cols = [jnp.broadcast_to(tile[0][:, first_col + k : first_col + k + 1], block) for k in range(block[0])]
     roots = tile[0]
-    for k in range(8):
+    for k in range(block[0]):
         pivot = jnp.broadcast_to(cols[k][k : k + 1, :], block)
         inverse = 1.0 / pivot
         rows = [jnp.broadcast_to(part[k : k + 1, :], block) for part in tile]
         here = sub == k
-        roots = jnp.where(here, rows[0] * lax.rsqrt(pivot), roots)
+        if want_roots:
+            roots = jnp.where(here, rows[0] * lax.rsqrt(pivot), roots)
         scaled = [row * inverse for row in rows]
         tile = [jnp.where(here, row, part - cols[k] * row) for row, part in zip(scaled, tile)]
-        for m in range(k + 1, 8):
+        for m in range(k + 1, block[0]):
             value = jnp.broadcast_to(cols[m][k : k + 1, :], block) * inverse
             cols[m] = jnp.where(here, value, cols[m] - cols[k] * value)
     return tile, roots
 
 
 def eliminated(parts, first_col, tile):
-    cols = [jnp.broadcast_to(parts[0][:, first_col + k : first_col + k + 1], tile[0].shape) for k in range(8)]
+    block = tile[0].shape
+    cols = [jnp.broadcast_to(parts[0][:, first_col + k : first_col + k + 1], block) for k in range(block[0])]
     out = []
     for part, known in zip(parts, tile):
-        terms = [cols[k] * jnp.broadcast_to(known[k : k + 1, :], part.shape) for k in range(8)]
+        terms = [cols[k] * jnp.broadcast_to(known[k : k + 1, :], block) for k in range(block[0])]
         while len(terms) > 1:
             terms = [terms[i] + terms[i + 1] for i in range(0, len(terms), 2)]
         out.append(part - terms[0])
@@ -283,7 +292,7 @@
         in_specs=[vmem, vmem, vmem, vmem, vmem, pl.BlockSpec(memory_space=pltpu.SMEM)],
         out_specs=[vmem, vmem, vmem],
         out_shape=[
-            jax.ShapeDtypeStruct((owned, rank), F32),
+            jax.ShapeDtypeStruct((rank, owned), F32),
             jax.ShapeDtypeStruct(adjoint.shape, F32),
             jax.ShapeDtypeStruct(adjoint.shape, F32),
         ],
@@ -313,7 +322,7 @@
 def summed_pieces(pieces, count, shift):
     size = pieces.shape[0]
     me = member(shift, size)
-    got = [lax.ppermute(pick(pieces, me ^ p), AXES, partners(count, shift, p)) for p in range(1, size)]
+    got = [lax.ppermute(pick(pieces, me ^ p), AXES, partners(count, shift, p)) for p in range(size - 1, 0, -1)]
     total = pick(pieces, me)
     for piece in got:
         total = total + piece
@@ -322,9 +331,9 @@
 
 def gathered_pieces(piece, count, shift, size):
     me = member(shift, size)
-    got = [lax.ppermute(piece, AXES, partners(count, shift, p)) for p in range(1, size)]
+    got = [lax.ppermute(piece, AXES, partners(count, shift, p)) for p in range(size - 1, 0, -1)]
     out = jnp.zeros((size,) + piece.shape, piece.dtype)
-    for p, part in enumerate([piece] + got):
+    for p, part in zip([0] + list(range(size - 1, 0, -1)), [piece] + got):
         out = lax.dynamic_update_index_in_dim(out, part, me ^ p, 0)
     return out
 
@@ -390,7 +399,7 @@
     padded = jnp.concatenate([top, adjoint, bottom], axis=0)
     sideways = jnp.pad(adjoint, ((0, 0), (1, 1)))
     laplace = padded[2:] + padded[:-2] + sideways[:, 2:] + sideways[:, :-2] - 4.0 * adjoint
-    return (adjoint + DIFFUSION * laplace + rate * adjoint, time_factors.T)
+    return (adjoint + DIFFUSION * laplace + rate * adjoint, time_factors)
 
 
 def solution(mesh):

time: 53.2 us -> 50.2 us (0.944)
  starting transfers between devices: 18.8 us -> 17 us
  Pallas kernels: 18.9 us -> 18 us
  local copies, waits for them, and re-layouts: 0.21 us -> 0.88 us
  waiting for transfers between devices: 12.8 us -> 12.2 us
    ppermute x7, waiting for transfers between devices: 8.39 us -> 6.86 us  [summed_pieces(): lax.ppermute(pick(pieces, me ^ p), AXES, partners(count, shift, p))]
    ppermute x4, starting transfers between devices: 7.95 us -> 6.58 us  [gathered_pieces(): lax.ppermute(piece, AXES, partners(count, shift, p))]
    ppermute x1, starting transfers between devices: 3.36 us -> 2.36 us  [shards(): far = lax.ppermute(jnp.where(even, head, tail), AXES, across)]
    pallas_call x1, Pallas kernels: 7.11 us -> 6.28 us  [solve(): pl.pallas_call(functools.partial(solve_kernel, cells_total, owned), in_sp...]
    unnamed x6 -> x7, local copies, waits for them, and re-layouts: 0.01 us -> 0.68 us
    ppermute x4, waiting for transfers between devices: 2.94 us -> 3.51 us  [gathered_pieces(): lax.ppermute(piece, AXES, partners(count, shift, p))]
  transfers between devices with their start and end apart: 13 -> 13, of which waited for: 10 -> 9; matrix products, arithmetic and copies ran while one was open for 0% -> 1% of each run, Pallas kernels for 4% -> 4%
where the time goes in v4:
time: 50.2 us; the launch traced here: 49.9 us
  Pallas kernels  18 us (36%)
  starting transfers between devices  17 us (34%)
  waiting for transfers between devices  12.2 us (24%)
  other arithmetic  0.94 us (2%)
  between operations  0.92 us (2%)
  local copies, waits for them, and re-layouts  0.88 us (2%)
    pallas_call x1, Pallas kernels, sketches(): pl.pallas_call(functools.partial(sketch_kernel, chunks, ahead), in_specs=...  9.51 us
    ppermute x7, starting transfers between devices, summed_pieces(): lax.ppermute(pick(pieces, me ^ p), AXES, partners(count, shift, p))  7.99 us
    ppermute x7, waiting for transfers between devices, summed_pieces(): lax.ppermute(pick(pieces, me ^ p), AXES, partners(count, shift, p))  6.86 us
    ppermute x4, starting transfers between devices, gathered_pieces(): lax.ppermute(piece, AXES, partners(count, shift, p))  6.58 us
    pallas_call x1, Pallas kernels, solve(): pl.pallas_call(functools.partial(solve_kernel, cells_total, owned), in_sp...  6.28 us
    ppermute x4, waiting for transfers between devices, gathered_pieces(): lax.ppermute(piece, AXES, partners(count, shift, p))  3.51 us
    ppermute x1, starting transfers between devices, shards(): far = lax.ppermute(jnp.where(even, head, tail), AXES, across)  2.36 us
    pallas_call x1, Pallas kernels, fetch(): pl.pallas_call(fetch_kernel, in_specs=[pl.BlockSpec(memory_space=pltpu.HB...  2.22 us
  transfers between devices with their start and end apart: 13, of which 9 were waited for; matrix products, arithmetic and copies ran while one was open for 1% of the time, Pallas kernels for 4%

profile of v4, /device:TPU:1, one launch (start us, length us, event | category | flops | bytes accessed | tf_op | source)
XLA Modules:
  0.0 49.9 jit_solution(1721672092902662269)
XLA Ops:
  0.6 9.5 %sketches.1 = (f32[128,8192]{1,0:T(8,128)}, f32[2,512,128]{2,1,0:T(8,128)S(1)}, f32[384,128]{1,0:T(8,128)S(1)}) custom-call(bf16[8192,512]{1,0:T(8,128)(2,1)} %snap.1, bf16[256,8192]{1,0:T(8,128)(2,1)} %test.1, bf16[512,128]{1,0:T(8,128)(2,1)} %om.1), custom_call_target="tpu_custom_call" | custom-call | tf_op jit(solution)/shard_map/sketches/pallas_call | solution.py:100
  10.2 0.1 collective-permute-start
  10.4 1.6 %collective-permute-done = f32[704,128]{1,0:T(8,128)S(1)} collective-permute-done((f32[704,128]{1,0:T(8,128)S(1)}, f32[704,128]{1,0:T(8,128)S(1)}, u32[]{:S(2)}, u32[]{:S(2)}) %collective-permute-start) | collective-permute-done | bytes 360480 | tf_op jit(solution)/shard_map/ppermute | solution.py:325
  12.1 3.4 %collective-permute-start.1 = (f32[176,128]{1,0:T(8,128)S(1)}, f32[176,128]{1,0:T(8,128)S(1)}, u32[]{:S(2)}, u32[]{:S(2)}) collective-permute-start(f32[176,128]{1,0:T(8,128)S(1)} %get-tuple-element.26), channel_id=1, source_target_pairs={{0,6},{1,7},{2,4},{3,5},{4,2},{5,3},{6,0},{7,1},{8,14},{9,15},{10,... | collective-permute-start | bytes 270344 | tf_op jit(solution)/shard_map/ppermute | solution.py:325
  15.5 0.2 collective-permute-start.2
  15.7 0.1 collective-permute-start.3
  15.9 2.3 %collective-permute-done.1 = f32[176,128]{1,0:T(8,128)S(1)} collective-permute-done((f32[176,128]{1,0:T(8,128)S(1)}, f32[176,128]{1,0:T(8,128)S(1)}, u32[]{:S(2)}, u32[]{:S(2)}) %collective-permute-start.1) | collective-permute-done | bytes 90144 | tf_op jit(solution)/shard_map/ppermute | solution.py:325
  18.2 1.8 %collective-permute-done.2 = f32[176,128]{1,0:T(8,128)S(1)} collective-permute-done((f32[176,128]{1,0:T(8,128)S(1)}, f32[176,128]{1,0:T(8,128)S(1)}, u32[]{:S(2)}, u32[]{:S(2)}) %collective-permute-start.2) | collective-permute-done | bytes 90144 | tf_op jit(solution)/shard_map/ppermute | solution.py:325
  20.1 3.8 %collective-permute-start.4 = (f32[80,128]{1,0:T(8,128)S(1)}, f32[80,128]{1,0:T(8,128)S(1)}, u32[]{:S(2)}, u32[]{:S(2)}) collective-permute-start(f32[80,128]{1,0:T(8,128)S(1)} %get-tuple-element.29), channel_id=1, source_target_pairs={{0,24},{1,25},{2,26},{3,27},{4,28},{5,29},{6,30},{7,31},{8,16},{9,... | collective-permute-start | bytes 122888 | tf_op jit(solution)/shard_map/ppermute | solution.py:325
  23.9 0.4 collective-permute-start.6
  24.2 2.2 %fetch.1.range_t = f32[128,8192]{1,0:T(8,128)S(1)} custom-call(f32[128,8192]{1,0:T(8,128)} %get-tuple-element.16.source), custom_call_target="tpu_custom_call" | custom-call | bytes 8388608 | tf_op jit(solution)/shard_map/fetch/pallas_call | solution.py:273
  26.5 1.1 %collective-permute-done.5 = f32[80,128]{1,0:T(8,128)S(1)} collective-permute-done((f32[80,128]{1,0:T(8,128)S(1)}, f32[80,128]{1,0:T(8,128)S(1)}, u32[]{:S(2)}, u32[]{:S(2)}) %collective-permute-start.5) | collective-permute-done | bytes 40992 | tf_op jit(solution)/shard_map/ppermute | solution.py:325
  27.6 1.0 %collective-permute-start.7 = (f32[48,128]{1,0:T(8,128)S(1)}, f32[48,128]{1,0:T(8,128)S(1)}, u32[]{:S(2)}, u32[]{:S(2)}) collective-permute-start(f32[48,128]{1,0:T(8,128)S(1)} %slice.80), channel_id=1, source_target_pairs={{0,6},{1,7},{2,4},{3,5},{4,2},{5,3},{6,0},{7,1},{8,14},{9,15},{10,... | collective-permute-start | bytes 73736 | tf_op jit(solution)/shard_map/ppermute | solution.py:334
  28.6 2.3 %collective-permute-start.8 = (f32[48,128]{1,0:T(8,128)S(1)}, f32[48,128]{1,0:T(8,128)S(1)}, u32[]{:S(2)}, u32[]{:S(2)}) collective-permute-start(f32[48,128]{1,0:T(8,128)S(1)} %slice.80), channel_id=1, source_target_pairs={{0,4},{1,5},{2,6},{3,7},{4,0},{5,1},{6,2},{7,3},{8,12},{9,13},{10,... | collective-permute-start | bytes 73736 | tf_op jit(solution)/shard_map/ppermute | solution.py:334
  31.0 0.3 collective-permute-done.7
  31.3 0.8 %collective-permute-done.8 = f32[48,128]{1,0:T(8,128)S(1)} collective-permute-done((f32[48,128]{1,0:T(8,128)S(1)}, f32[48,128]{1,0:T(8,128)S(1)}, u32[]{:S(2)}, u32[]{:S(2)}) %collective-permute-start.8) | collective-permute-done | bytes 24608 | tf_op jit(solution)/shard_map/ppermute | solution.py:334
  32.1 1.5 %collective-permute-done.9 = f32[48,128]{1,0:T(8,128)S(1)} collective-permute-done((f32[48,128]{1,0:T(8,128)S(1)}, f32[48,128]{1,0:T(8,128)S(1)}, u32[]{:S(2)}, u32[]{:S(2)}) %collective-permute-start.9) | collective-permute-done | bytes 24608 | tf_op jit(solution)/shard_map/ppermute | solution.py:334
  33.6 3.3 %collective-permute-start.10 = (f32[192,128]{1,0:T(8,128)S(1)}, f32[192,128]{1,0:T(8,128)S(1)}, u32[]{:S(2)}, u32[]{:S(2)}) collective-permute-start(f32[192,128]{1,0:T(8,128)S(1)} %bitcast.79), channel_id=1, source_target_pairs={{0,1},{1,0},{2,3},{3,2},{4,5},{5,4},{6,7},{7,6},{8,9},{9,8},{10,11... | collective-permute-start | bytes 294920 | tf_op jit(solution)/shard_map/ppermute | solution.py:334
  36.9 0.9 %collective-permute-done.10 = f32[192,128]{1,0:T(8,128)S(1)} collective-permute-done((f32[192,128]{1,0:T(8,128)S(1)}, f32[192,128]{1,0:T(8,128)S(1)}, u32[]{:S(2)}, u32[]{:S(2)}) %collective-permute-start.10) | collective-permute-done | bytes 98336 | tf_op jit(solution)/shard_map/ppermute | solution.py:334
  37.9 6.3 %solve.1 = (f32[128,16]{1,0:T(8,128)S(1)}, f32[8,1024]{1,0:T(8,128)S(1)}, f32[8,1024]{1,0:T(8,128)S(1)}) custom-call(f32[384,128]{1,0:T(8,128)S(1)} %bitcast.65, f32[2,16,128]{2,1,0:T(8,128)S(1)} %bitcast.69, f32[128,8192]{1,0:T(8,128)S(1)} %fetch.1.range_t, f32[8,1024]{1,0:T(8,128)S(1)} %copy-done, s32[8,1024]{1,0:T(8,128)S(1)} %copy-done.1, f32[4]{0:T(128)S(1)} %copy-done.2), custom_call_target="tpu_custom_call" | custom-call | tf_op jit(solution)/shard_map/solve/pallas_call | solution.py:290
  44.2 2.4 %collective-permute-start.11 = (f32[2,1024]{1,0:T(2,128)S(1)}, f32[2,1024]{1,0:T(2,128)S(1)}, u32[]{:S(2)}, u32[]{:S(2)}) collective-permute-start(f32[2,1024]{1,0:T(2,128)S(1)} %get-tuple-element.44), channel_id=1, source_target_pairs={{1,2},{3,4},{5,6},{7,8},{9,10},{11,12},{13,14},{15,16},{17,18},{19... | collective-permute-start | bytes 24584 | tf_op jit(solution)/shard_map/ppermute | solution.py:390
  46.7 0.7 %copy.14 = f32[128,16]{0,1:T(8,128)} copy(f32[128,16]{1,0:T(8,128)S(1)} %get-tuple-element.25) | data formatting | bytes 16384
  47.3 1.8 %collective-permute-done.11 = f32[2,1024]{1,0:T(2,128)S(1)} collective-permute-done((f32[2,1024]{1,0:T(2,128)S(1)}, f32[2,1024]{1,0:T(2,128)S(1)}, u32[]{:S(2)}, u32[]{:S(2)}) %collective-permute-start.11) | collective-permute-done | bytes 8224 | tf_op jit(solution)/shard_map/ppermute | solution.py:390
  49.2 0.7 %fusion.32 = f32[8,1024]{1,0:T(8,128)} fusion(f32[8,1024]{1,0:T(8,128)S(1)} %pad_maximum_fusion, f32[1,1024]{1,0:T(1,128)S(1)} %get-tuple-element.40, f32[1,1024]{1,0:T(1,128)S(1)} %get-tuple-element.35, f32[6,1024]{1,0:T(8,128)S(1)} %slice.70, f32[1,1024]{1,0:T(1,128)S(1)} %get-tuple-element.34, f32[1,1024]{1,0:T(1,128)S(1)} %get-tuple-element.41, ...), kind=kLoop, calls=%fused_computation.56 | loop fusion | flops 106496 | bytes 139264 | tf_op jit(solution)/shard_map/add | solution.py:402
  (43 shorter events, 0.6 us)
Async XLA Ops:
  10.2 1.7 %collective-permute-start = (f32[704,128]{1,0:T(8,128)S(1)}, f32[704,128]{1,0:T(8,128)S(1)}, u32[]{:S(2)}, u32[]{:S(2)}) collective-permute-start(f32[704,128]{1,0:T(8,128)S(1)} %fusion.1), channel_id=1, source_target_pairs={{0,1},{1,0},{2,3},{3,2},{4,5},{5,4},{6,7},{7,6},{8,9},{9,8},{10,11... | collective-permute-start | bytes 1081352 | tf_op jit(solution)/shard_map/ppermute | solution.py:325
  12.1 6.1 %collective-permute-start.1 = (f32[176,128]{1,0:T(8,128)S(1)}, f32[176,128]{1,0:T(8,128)S(1)}, u32[]{:S(2)}, u32[]{:S(2)}) collective-permute-start(f32[176,128]{1,0:T(8,128)S(1)} %get-tuple-element.26), channel_id=1, source_target_pairs={{0,6},{1,7},{2,4},{3,5},{4,2},{5,3},{6,0},{7,1},{8,14},{9,15},{10,... | collective-permute-start | bytes 270344 | tf_op jit(solution)/shard_map/ppermute | solution.py:325
  15.5 4.5 %collective-permute-start.2 = (f32[176,128]{1,0:T(8,128)S(1)}, f32[176,128]{1,0:T(8,128)S(1)}, u32[]{:S(2)}, u32[]{:S(2)}) collective-permute-start(f32[176,128]{1,0:T(8,128)S(1)} %get-tuple-element.27), channel_id=1, source_target_pairs={{0,4},{1,5},{2,6},{3,7},{4,0},{5,1},{6,2},{7,3},{8,12},{9,13},{10,... | collective-permute-start | bytes 270344 | tf_op jit(solution)/shard_map/ppermute | solution.py:325
  15.7 4.2 %collective-permute-start.3 = (f32[176,128]{1,0:T(8,128)S(1)}, f32[176,128]{1,0:T(8,128)S(1)}, u32[]{:S(2)}, u32[]{:S(2)}) collective-permute-start(f32[176,128]{1,0:T(8,128)S(1)} %get-tuple-element.28), channel_id=1, source_target_pairs={{0,2},{1,3},{2,0},{3,1},{4,6},{5,7},{6,4},{7,5},{8,10},{9,11},{10,... | collective-permute-start | bytes 270344 | tf_op jit(solution)/shard_map/ppermute | solution.py:325
  20.1 6.4 %collective-permute-start.4 = (f32[80,128]{1,0:T(8,128)S(1)}, f32[80,128]{1,0:T(8,128)S(1)}, u32[]{:S(2)}, u32[]{:S(2)}) collective-permute-start(f32[80,128]{1,0:T(8,128)S(1)} %get-tuple-element.29), channel_id=1, source_target_pairs={{0,24},{1,25},{2,26},{3,27},{4,28},{5,29},{6,30},{7,31},{8,16},{9,... | collective-permute-start | bytes 122888 | tf_op jit(solution)/shard_map/ppermute | solution.py:325
  23.8 3.8 %collective-permute-start.5 = (f32[80,128]{1,0:T(8,128)S(1)}, f32[80,128]{1,0:T(8,128)S(1)}, u32[]{:S(2)}, u32[]{:S(2)}) collective-permute-start(f32[80,128]{1,0:T(8,128)S(1)} %get-tuple-element.30), channel_id=1, source_target_pairs={{0,16},{1,17},{2,18},{3,19},{4,20},{5,21},{6,22},{7,23},{8,24},{9,... | collective-permute-start | bytes 122888 | tf_op jit(solution)/shard_map/ppermute | solution.py:325
  23.9 3.8 %collective-permute-start.6 = (f32[80,128]{1,0:T(8,128)S(1)}, f32[80,128]{1,0:T(8,128)S(1)}, u32[]{:S(2)}, u32[]{:S(2)}) collective-permute-start(f32[80,128]{1,0:T(8,128)S(1)} %get-tuple-element.31), channel_id=1, source_target_pairs={{0,8},{1,9},{2,10},{3,11},{4,12},{5,13},{6,14},{7,15},{8,0},{9,1},... | collective-permute-start | bytes 122888 | tf_op jit(solution)/shard_map/ppermute | solution.py:325
  24.2 13.6 %copy-start = (f32[8,1024]{1,0:T(8,128)S(1)}, f32[8,1024]{1,0:T(8,128)}, u32[]{:S(2)}) copy-start(f32[8,1024]{1,0:T(8,128)} %adjoint.1) | copy-start | bytes 98308
  24.2 13.6 %copy-start.1 = (s32[8,1024]{1,0:T(8,128)S(1)}, s32[8,1024]{1,0:T(8,128)}, u32[]{:S(2)}) copy-start(s32[8,1024]{1,0:T(8,128)} %species.1) | copy-start | bytes 98308
  24.2 13.6 %copy-start.2 = (f32[4]{0:T(128)S(1)}, f32[4]{0:T(128)}, u32[]{:S(2)}) copy-start(f32[4]{0:T(128)} %rates.1) | copy-start | bytes 52
  27.6 3.6 %collective-permute-start.7 = (f32[48,128]{1,0:T(8,128)S(1)}, f32[48,128]{1,0:T(8,128)S(1)}, u32[]{:S(2)}, u32[]{:S(2)}) collective-permute-start(f32[48,128]{1,0:T(8,128)S(1)} %slice.80), channel_id=1, source_target_pairs={{0,6},{1,7},{2,4},{3,5},{4,2},{5,3},{6,0},{7,1},{8,14},{9,15},{10,... | collective-permute-start | bytes 73736 | tf_op jit(solution)/shard_map/ppermute | solution.py:334
  28.6 3.5 %collective-permute-start.8 = (f32[48,128]{1,0:T(8,128)S(1)}, f32[48,128]{1,0:T(8,128)S(1)}, u32[]{:S(2)}, u32[]{:S(2)}) collective-permute-start(f32[48,128]{1,0:T(8,128)S(1)} %slice.80), channel_id=1, source_target_pairs={{0,4},{1,5},{2,6},{3,7},{4,0},{5,1},{6,2},{7,3},{8,12},{9,13},{10,... | collective-permute-start | bytes 73736 | tf_op jit(solution)/shard_map/ppermute | solution.py:334
  30.9 2.7 %collective-permute-start.9 = (f32[48,128]{1,0:T(8,128)S(1)}, f32[48,128]{1,0:T(8,128)S(1)}, u32[]{:S(2)}, u32[]{:S(2)}) collective-permute-start(f32[48,128]{1,0:T(8,128)S(1)} %slice.80), channel_id=1, source_target_pairs={{0,2},{1,3},{2,0},{3,1},{4,6},{5,7},{6,4},{7,5},{8,10},{9,11},{10,... | collective-permute-start | bytes 73736 | tf_op jit(solution)/shard_map/ppermute | solution.py:334
  33.6 4.2 %collective-permute-start.10 = (f32[192,128]{1,0:T(8,128)S(1)}, f32[192,128]{1,0:T(8,128)S(1)}, u32[]{:S(2)}, u32[]{:S(2)}) collective-permute-start(f32[192,128]{1,0:T(8,128)S(1)} %bitcast.79), channel_id=1, source_target_pairs={{0,1},{1,0},{2,3},{3,2},{4,5},{5,4},{6,7},{7,6},{8,9},{9,8},{10,11... | collective-permute-start | bytes 294920 | tf_op jit(solution)/shard_map/ppermute | solution.py:334
  44.2 5.0 %collective-permute-start.11 = (f32[2,1024]{1,0:T(2,128)S(1)}, f32[2,1024]{1,0:T(2,128)S(1)}, u32[]{:S(2)}, u32[]{:S(2)}) collective-permute-start(f32[2,1024]{1,0:T(2,128)S(1)} %get-tuple-element.44), channel_id=1, source_target_pairs={{1,2},{3,4},{5,6},{7,8},{9,10},{11,12},{13,14},{15,16},{17,18},{19... | collective-permute-start | bytes 24584 | tf_op jit(solution)/shard_map/ppermute | solution.py:390
  46.6 2.6 %collective-permute-start.12 = (f32[2,1024]{1,0:T(2,128)S(1)}, f32[2,1024]{1,0:T(2,128)S(1)}, u32[]{:S(2)}, u32[]{:S(2)}) collective-permute-start(f32[2,1024]{1,0:T(2,128)S(1)} %get-tuple-element.45), channel_id=1, source_target_pairs={{0,1},{1,0},{2,3},{3,2},{4,5},{5,4},{6,7},{7,6},{8,9},{9,8},{10,11... | collective-permute-start | bytes 24584 | tf_op jit(solution)/shard_map/ppermute | solution.py:391

commit v5 on v4

--- a/solution.py
+++ b/solution.py
@@ -18,64 +18,65 @@
 
 
 def sketch_kernel(
-    chunks, ahead, snap, test, om, range_out, ct, crit, snap_v, test_v, om_v, range_t, om_t, corange, gram, split, sems
+    sizes, ahead, snap, test, om, range_out, ct, crit,
+    snap_v, test_v, om_v, range_t, om_t, corange, gram, split, sems,
 ):
-    cells, times = snap.shape
+    times = snap.shape[1]
     rank = om.shape[1]
     sketch = test.shape[0]
-    block = cells // chunks
-
-    def place(i):
-        return pl.ds(pl.multiple_of(i * block, block), block)
+    blocks = len(sizes)
+    places = [pl.ds(sum(sizes[:i]), sizes[i]) for i in range(blocks)]
 
     def copies(i):
-        at = place(i)
+        at = places[i]
         return (
             pltpu.make_async_copy(snap.at[at, :], snap_v.at[at, :], sems.at[2 * i]),
             pltpu.make_async_copy(test.at[:, at], test_v.at[:, at], sems.at[2 * i + 1]),
         )
 
     def leaving(i):
-        return pltpu.make_async_copy(range_t.at[:, place(i)], range_out.at[:, place(i)], sems.at[2 * chunks + 1 + i])
-
-    own = pltpu.make_async_copy(om, om_v, sems.at[2 * chunks])
+        return pltpu.make_async_copy(range_t.at[:, places[i]], range_out.at[:, places[i]], sems.at[2 * blocks + 1 + i])
+
+    def gram_of(i):
+        part = split[:, places[i]]
+        return lax.dot_general(part, part, NT, preferred_element_type=F32)
+
+    own = pltpu.make_async_copy(om, om_v, sems.at[2 * blocks])
     own.start()
-    for i in range(min(ahead, chunks)):
+    for i in range(min(ahead, blocks)):
         for copy in copies(i):
             copy.start()
     corange[...] = jnp.zeros_like(corange)
     gram[...] = jnp.zeros_like(gram)
-    split[1] = jnp.zeros(split.shape[1:], BF16)
     own.wait()
     om_t[...] = om_v[...].astype(F32).T.astype(BF16)
-
-    def step(i, carry):
+    for i in range(blocks):
         for copy in copies(i):
             copy.wait()
-
-        @pl.when(i + ahead < chunks)
-        def _():
+        if i + ahead < blocks:
             for copy in copies(i + ahead):
                 copy.start()
-
-        at = place(i)
+        at = places[i]
         states = snap_v[at, :]
-        before = split[(i + 1) % 2]
-        gram[...] += lax.dot_general(before, before, NT, preferred_element_type=F32)
+        if i:
+            gram[...] += gram_of(i - 1)
         rt = lax.dot_general(om_t[...], states, NT, preferred_element_type=F32)
         range_t[:, at] = rt
         leaving(i).start()
         upper = rt.astype(BF16)
-        split[i % 2, 0:rank] = upper
-        split[i % 2, rank:] = (rt - upper.astype(F32)).astype(BF16)
+        split[0:rank, at] = upper
+        split[rank:, at] = (rt - upper.astype(F32)).astype(BF16)
         corange[...] += jnp.dot(test_v[:, at], states, preferred_element_type=F32)
-        return carry
-
-    lax.fori_loop(0, chunks, step, 0)
-    last = split[(chunks + 1) % 2]
-    gram[...] += lax.dot_general(last, last, NT, preferred_element_type=F32)
+    gram[...] += gram_of(blocks - 1)
     whole = corange[...]
-    crit[0:sketch, :] = jnp.dot(whole, om_v[...].astype(F32), precision=HIGH, preferred_element_type=F32)
+    high = whole.astype(BF16)
+    rest = whole - high.astype(F32)
+    middle = rest.astype(BF16)
+    low = (rest - middle.astype(F32)).astype(BF16)
+    projected = jnp.zeros((sketch, rank), F32)
+    for part in (low, middle, high):
+        projected = projected + jnp.dot(part, om_v[...], preferred_element_type=F32)
+    crit[0:sketch, :] = projected
     cross = gram[0:rank, rank:]
     crit[sketch:, :] = gram[0:rank, 0:rank] + cross + cross.T
     half = sketch // 2
@@ -87,18 +88,19 @@
             for q in range(2):
                 there = sketch + j * 4 + h * 2 + q
                 crit[there : there + 1, rank // 2 :] = row[:, q * 64 : (q + 1) * 64]
-    for i in range(chunks):
+    for i in range(blocks):
         leaving(i).wait()
 
 
-def sketches(snapshots, range_test, test_rows, chunks=8, ahead=3):
+def sketches(snapshots, range_test, test_rows, shares=(1, 1, 2, 2, 2), ahead=3):
     cells, times = snapshots.shape
     rank = range_test.shape[1]
     sketch = test_rows.shape[0]
+    sizes = [share * cells // sum(shares) for share in shares]
     far = pl.BlockSpec(memory_space=pltpu.HBM)
     near = pl.BlockSpec(memory_space=pltpu.VMEM)
     return pl.pallas_call(
-        functools.partial(sketch_kernel, chunks, ahead),
+        functools.partial(sketch_kernel, sizes, ahead),
         in_specs=[far, far, far],
         out_specs=[far, near, near],
         out_shape=[
@@ -114,10 +116,10 @@
             pltpu.VMEM((rank, times), BF16),
             pltpu.VMEM((sketch, times), F32),
             pltpu.VMEM((2 * rank, 2 * rank), F32),
-            pltpu.VMEM((2, 2 * rank, cells // chunks), BF16),
-            pltpu.SemaphoreType.DMA((3 * chunks + 1,)),
+            pltpu.VMEM((2 * rank, cells), BF16),
+            pltpu.SemaphoreType.DMA((3 * len(sizes) + 1,)),
         ],
-        compiler_params=pltpu.CompilerParams(vmem_limit_bytes=40 * 2**20),
+        compiler_params=pltpu.CompilerParams(vmem_limit_bytes=44 * 2**20),
         name="sketches",
     )(*[pltpu.with_memory_space_constraint(x, pltpu.HBM) for x in (snapshots, test_rows, range_test)])
 

time: 50.2 us -> 48.9 us (0.974)
  Pallas kernels: 18 us -> 16.7 us
    pallas_call x1, Pallas kernels: 9.51 us -> 8.22 us  [sketches(): pl.pallas_call(functools.partial(sketch_kernel, sizes, ahead), in_specs=[...]
  transfers between devices with their start and end apart: 13 -> 13, of which waited for: 9 -> 9; matrix products, arithmetic and copies ran while one was open for 1% -> 1% of each run, Pallas kernels for 4% -> 5%
where the time goes in v5:
time: 48.9 us; the launch traced here: 48.7 us
  starting transfers between devices  17 us (35%)
  Pallas kernels  16.7 us (34%)
  waiting for transfers between devices  12.2 us (25%)
  other arithmetic  0.94 us (2%)
  between operations  0.92 us (2%)
  local copies, waits for them, and re-layouts  0.88 us (2%)
    pallas_call x1, Pallas kernels, sketches(): pl.pallas_call(functools.partial(sketch_kernel, sizes, ahead), in_specs=[...  8.22 us
    ppermute x7, starting transfers between devices, summed_pieces(): lax.ppermute(pick(pieces, me ^ p), AXES, partners(count, shift, p))  7.98 us
    ppermute x7, waiting for transfers between devices, summed_pieces(): lax.ppermute(pick(pieces, me ^ p), AXES, partners(count, shift, p))  6.86 us
    ppermute x4, starting transfers between devices, gathered_pieces(): lax.ppermute(piece, AXES, partners(count, shift, p))  6.59 us
    pallas_call x1, Pallas kernels, solve(): pl.pallas_call(functools.partial(solve_kernel, cells_total, owned), in_sp...  6.28 us
    ppermute x4, waiting for transfers between devices, gathered_pieces(): lax.ppermute(piece, AXES, partners(count, shift, p))  3.51 us
    ppermute x1, starting transfers between devices, shards(): far = lax.ppermute(jnp.where(even, head, tail), AXES, across)  2.36 us
    pallas_call x1, Pallas kernels, fetch(): pl.pallas_call(fetch_kernel, in_specs=[pl.BlockSpec(memory_space=pltpu.HB...  2.22 us
  transfers between devices with their start and end apart: 13, of which 9 were waited for; matrix products, arithmetic and copies ran while one was open for 1% of the time, Pallas kernels for 5%

profile of v5, /device:TPU:1, one launch (start us, length us, event | category | flops | bytes accessed | tf_op | source)
XLA Modules:
  0.0 48.7 jit_solution(14622093591487519645)
XLA Ops:
  0.6 8.2 %sketches.1 = (f32[128,8192]{1,0:T(8,128)}, f32[2,512,128]{2,1,0:T(8,128)S(1)}, f32[384,128]{1,0:T(8,128)S(1)}) custom-call(bf16[8192,512]{1,0:T(8,128)(2,1)} %snap.1, bf16[256,8192]{1,0:T(8,128)(2,1)} %test.1, bf16[512,128]{1,0:T(8,128)(2,1)} %om.1), custom_call_target="tpu_custom_call" | custom-call | tf_op jit(solution)/shard_map/sketches/pallas_call | solution.py:102
  9.0 0.1 collective-permute-start
  9.1 1.6 %collective-permute-done = f32[704,128]{1,0:T(8,128)S(1)} collective-permute-done((f32[704,128]{1,0:T(8,128)S(1)}, f32[704,128]{1,0:T(8,128)S(1)}, u32[]{:S(2)}, u32[]{:S(2)}) %collective-permute-start) | collective-permute-done | bytes 360480 | tf_op jit(solution)/shard_map/ppermute | solution.py:327
  10.9 3.4 %collective-permute-start.1 = (f32[176,128]{1,0:T(8,128)S(1)}, f32[176,128]{1,0:T(8,128)S(1)}, u32[]{:S(2)}, u32[]{:S(2)}) collective-permute-start(f32[176,128]{1,0:T(8,128)S(1)} %get-tuple-element.26), channel_id=1, source_target_pairs={{0,6},{1,7},{2,4},{3,5},{4,2},{5,3},{6,0},{7,1},{8,14},{9,15},{10,... | collective-permute-start | bytes 270344 | tf_op jit(solution)/shard_map/ppermute | solution.py:327
  14.2 0.2 collective-permute-start.2
  14.4 0.1 collective-permute-start.3
  14.6 2.3 %collective-permute-done.1 = f32[176,128]{1,0:T(8,128)S(1)} collective-permute-done((f32[176,128]{1,0:T(8,128)S(1)}, f32[176,128]{1,0:T(8,128)S(1)}, u32[]{:S(2)}, u32[]{:S(2)}) %collective-permute-start.1) | collective-permute-done | bytes 90144 | tf_op jit(solution)/shard_map/ppermute | solution.py:327
  16.9 1.8 %collective-permute-done.2 = f32[176,128]{1,0:T(8,128)S(1)} collective-permute-done((f32[176,128]{1,0:T(8,128)S(1)}, f32[176,128]{1,0:T(8,128)S(1)}, u32[]{:S(2)}, u32[]{:S(2)}) %collective-permute-start.2) | collective-permute-done | bytes 90144 | tf_op jit(solution)/shard_map/ppermute | solution.py:327
  18.8 3.8 %collective-permute-start.4 = (f32[80,128]{1,0:T(8,128)S(1)}, f32[80,128]{1,0:T(8,128)S(1)}, u32[]{:S(2)}, u32[]{:S(2)}) collective-permute-start(f32[80,128]{1,0:T(8,128)S(1)} %get-tuple-element.29), channel_id=1, source_target_pairs={{0,24},{1,25},{2,26},{3,27},{4,28},{5,29},{6,30},{7,31},{8,16},{9,... | collective-permute-start | bytes 122888 | tf_op jit(solution)/shard_map/ppermute | solution.py:327
  22.6 0.4 collective-permute-start.6
  22.9 2.2 %fetch.1.range_t = f32[128,8192]{1,0:T(8,128)S(1)} custom-call(f32[128,8192]{1,0:T(8,128)} %get-tuple-element.16.source), custom_call_target="tpu_custom_call" | custom-call | bytes 8388608 | tf_op jit(solution)/shard_map/fetch/pallas_call | solution.py:275
  25.2 1.1 %collective-permute-done.5 = f32[80,128]{1,0:T(8,128)S(1)} collective-permute-done((f32[80,128]{1,0:T(8,128)S(1)}, f32[80,128]{1,0:T(8,128)S(1)}, u32[]{:S(2)}, u32[]{:S(2)}) %collective-permute-start.5) | collective-permute-done | bytes 40992 | tf_op jit(solution)/shard_map/ppermute | solution.py:327
  26.3 1.0 %collective-permute-start.7 = (f32[48,128]{1,0:T(8,128)S(1)}, f32[48,128]{1,0:T(8,128)S(1)}, u32[]{:S(2)}, u32[]{:S(2)}) collective-permute-start(f32[48,128]{1,0:T(8,128)S(1)} %slice.80), channel_id=1, source_target_pairs={{0,6},{1,7},{2,4},{3,5},{4,2},{5,3},{6,0},{7,1},{8,14},{9,15},{10,... | collective-permute-start | bytes 73736 | tf_op jit(solution)/shard_map/ppermute | solution.py:336
  27.3 2.3 %collective-permute-start.8 = (f32[48,128]{1,0:T(8,128)S(1)}, f32[48,128]{1,0:T(8,128)S(1)}, u32[]{:S(2)}, u32[]{:S(2)}) collective-permute-start(f32[48,128]{1,0:T(8,128)S(1)} %slice.80), channel_id=1, source_target_pairs={{0,4},{1,5},{2,6},{3,7},{4,0},{5,1},{6,2},{7,3},{8,12},{9,13},{10,... | collective-permute-start | bytes 73736 | tf_op jit(solution)/shard_map/ppermute | solution.py:336
  29.7 0.3 collective-permute-done.7
  30.0 0.8 %collective-permute-done.8 = f32[48,128]{1,0:T(8,128)S(1)} collective-permute-done((f32[48,128]{1,0:T(8,128)S(1)}, f32[48,128]{1,0:T(8,128)S(1)}, u32[]{:S(2)}, u32[]{:S(2)}) %collective-permute-start.8) | collective-permute-done | bytes 24608 | tf_op jit(solution)/shard_map/ppermute | solution.py:336
  30.8 1.5 %collective-permute-done.9 = f32[48,128]{1,0:T(8,128)S(1)} collective-permute-done((f32[48,128]{1,0:T(8,128)S(1)}, f32[48,128]{1,0:T(8,128)S(1)}, u32[]{:S(2)}, u32[]{:S(2)}) %collective-permute-start.9) | collective-permute-done | bytes 24608 | tf_op jit(solution)/shard_map/ppermute | solution.py:336
  32.3 3.3 %collective-permute-start.10 = (f32[192,128]{1,0:T(8,128)S(1)}, f32[192,128]{1,0:T(8,128)S(1)}, u32[]{:S(2)}, u32[]{:S(2)}) collective-permute-start(f32[192,128]{1,0:T(8,128)S(1)} %bitcast.79), channel_id=1, source_target_pairs={{0,1},{1,0},{2,3},{3,2},{4,5},{5,4},{6,7},{7,6},{8,9},{9,8},{10,11... | collective-permute-start | bytes 294920 | tf_op jit(solution)/shard_map/ppermute | solution.py:336
  35.6 0.9 %collective-permute-done.10 = f32[192,128]{1,0:T(8,128)S(1)} collective-permute-done((f32[192,128]{1,0:T(8,128)S(1)}, f32[192,128]{1,0:T(8,128)S(1)}, u32[]{:S(2)}, u32[]{:S(2)}) %collective-permute-start.10) | collective-permute-done | bytes 98336 | tf_op jit(solution)/shard_map/ppermute | solution.py:336
  36.6 6.3 %solve.1 = (f32[128,16]{1,0:T(8,128)S(1)}, f32[8,1024]{1,0:T(8,128)S(1)}, f32[8,1024]{1,0:T(8,128)S(1)}) custom-call(f32[384,128]{1,0:T(8,128)S(1)} %bitcast.65, f32[2,16,128]{2,1,0:T(8,128)S(1)} %bitcast.69, f32[128,8192]{1,0:T(8,128)S(1)} %fetch.1.range_t, f32[8,1024]{1,0:T(8,128)S(1)} %copy-done, s32[8,1024]{1,0:T(8,128)S(1)} %copy-done.1, f32[4]{0:T(128)S(1)} %copy-done.2), custom_call_target="tpu_custom_call" | custom-call | tf_op jit(solution)/shard_map/solve/pallas_call | solution.py:292
  42.9 2.4 %collective-permute-start.11 = (f32[2,1024]{1,0:T(2,128)S(1)}, f32[2,1024]{1,0:T(2,128)S(1)}, u32[]{:S(2)}, u32[]{:S(2)}) collective-permute-start(f32[2,1024]{1,0:T(2,128)S(1)} %get-tuple-element.44), channel_id=1, source_target_pairs={{1,2},{3,4},{5,6},{7,8},{9,10},{11,12},{13,14},{15,16},{17,18},{19... | collective-permute-start | bytes 24584 | tf_op jit(solution)/shard_map/ppermute | solution.py:392
  45.4 0.7 %copy.14 = f32[128,16]{0,1:T(8,128)} copy(f32[128,16]{1,0:T(8,128)S(1)} %get-tuple-element.25) | data formatting | bytes 16384
  46.0 1.8 %collective-permute-done.11 = f32[2,1024]{1,0:T(2,128)S(1)} collective-permute-done((f32[2,1024]{1,0:T(2,128)S(1)}, f32[2,1024]{1,0:T(2,128)S(1)}, u32[]{:S(2)}, u32[]{:S(2)}) %collective-permute-start.11) | collective-permute-done | bytes 8224 | tf_op jit(solution)/shard_map/ppermute | solution.py:392
  47.9 0.7 %fusion.32 = f32[8,1024]{1,0:T(8,128)} fusion(f32[8,1024]{1,0:T(8,128)S(1)} %pad_maximum_fusion, f32[1,1024]{1,0:T(1,128)S(1)} %get-tuple-element.40, f32[1,1024]{1,0:T(1,128)S(1)} %get-tuple-element.35, f32[6,1024]{1,0:T(8,128)S(1)} %slice.70, f32[1,1024]{1,0:T(1,128)S(1)} %get-tuple-element.34, f32[1,1024]{1,0:T(1,128)S(1)} %get-tuple-element.41, ...), kind=kLoop, calls=%fused_computation.56 | loop fusion | flops 106496 | bytes 139264 | tf_op jit(solution)/shard_map/add | solution.py:404
  (43 shorter events, 0.6 us)
Async XLA Ops:
  9.0 1.7 %collective-permute-start = (f32[704,128]{1,0:T(8,128)S(1)}, f32[704,128]{1,0:T(8,128)S(1)}, u32[]{:S(2)}, u32[]{:S(2)}) collective-permute-start(f32[704,128]{1,0:T(8,128)S(1)} %fusion.1), channel_id=1, source_target_pairs={{0,1},{1,0},{2,3},{3,2},{4,5},{5,4},{6,7},{7,6},{8,9},{9,8},{10,11... | collective-permute-start | bytes 1081352 | tf_op jit(solution)/shard_map/ppermute | solution.py:327
  10.9 6.1 %collective-permute-start.1 = (f32[176,128]{1,0:T(8,128)S(1)}, f32[176,128]{1,0:T(8,128)S(1)}, u32[]{:S(2)}, u32[]{:S(2)}) collective-permute-start(f32[176,128]{1,0:T(8,128)S(1)} %get-tuple-element.26), channel_id=1, source_target_pairs={{0,6},{1,7},{2,4},{3,5},{4,2},{5,3},{6,0},{7,1},{8,14},{9,15},{10,... | collective-permute-start | bytes 270344 | tf_op jit(solution)/shard_map/ppermute | solution.py:327
  14.2 4.5 %collective-permute-start.2 = (f32[176,128]{1,0:T(8,128)S(1)}, f32[176,128]{1,0:T(8,128)S(1)}, u32[]{:S(2)}, u32[]{:S(2)}) collective-permute-start(f32[176,128]{1,0:T(8,128)S(1)} %get-tuple-element.27), channel_id=1, source_target_pairs={{0,4},{1,5},{2,6},{3,7},{4,0},{5,1},{6,2},{7,3},{8,12},{9,13},{10,... | collective-permute-start | bytes 270344 | tf_op jit(solution)/shard_map/ppermute | solution.py:327
  14.4 4.2 %collective-permute-start.3 = (f32[176,128]{1,0:T(8,128)S(1)}, f32[176,128]{1,0:T(8,128)S(1)}, u32[]{:S(2)}, u32[]{:S(2)}) collective-permute-start(f32[176,128]{1,0:T(8,128)S(1)} %get-tuple-element.28), channel_id=1, source_target_pairs={{0,2},{1,3},{2,0},{3,1},{4,6},{5,7},{6,4},{7,5},{8,10},{9,11},{10,... | collective-permute-start | bytes 270344 | tf_op jit(solution)/shard_map/ppermute | solution.py:327
  18.8 6.4 %collective-permute-start.4 = (f32[80,128]{1,0:T(8,128)S(1)}, f32[80,128]{1,0:T(8,128)S(1)}, u32[]{:S(2)}, u32[]{:S(2)}) collective-permute-start(f32[80,128]{1,0:T(8,128)S(1)} %get-tuple-element.29), channel_id=1, source_target_pairs={{0,24},{1,25},{2,26},{3,27},{4,28},{5,29},{6,30},{7,31},{8,16},{9,... | collective-permute-start | bytes 122888 | tf_op jit(solution)/shard_map/ppermute | solution.py:327
  22.5 3.8 %collective-permute-start.5 = (f32[80,128]{1,0:T(8,128)S(1)}, f32[80,128]{1,0:T(8,128)S(1)}, u32[]{:S(2)}, u32[]{:S(2)}) collective-permute-start(f32[80,128]{1,0:T(8,128)S(1)} %get-tuple-element.30), channel_id=1, source_target_pairs={{0,16},{1,17},{2,18},{3,19},{4,20},{5,21},{6,22},{7,23},{8,24},{9,... | collective-permute-start | bytes 122888 | tf_op jit(solution)/shard_map/ppermute | solution.py:327
  22.6 3.8 %collective-permute-start.6 = (f32[80,128]{1,0:T(8,128)S(1)}, f32[80,128]{1,0:T(8,128)S(1)}, u32[]{:S(2)}, u32[]{:S(2)}) collective-permute-start(f32[80,128]{1,0:T(8,128)S(1)} %get-tuple-element.31), channel_id=1, source_target_pairs={{0,8},{1,9},{2,10},{3,11},{4,12},{5,13},{6,14},{7,15},{8,0},{9,1},... | collective-permute-start | bytes 122888 | tf_op jit(solution)/shard_map/ppermute | solution.py:327
  22.9 13.6 %copy-start = (f32[8,1024]{1,0:T(8,128)S(1)}, f32[8,1024]{1,0:T(8,128)}, u32[]{:S(2)}) copy-start(f32[8,1024]{1,0:T(8,128)} %adjoint.1) | copy-start | bytes 98308
  22.9 13.6 %copy-start.1 = (s32[8,1024]{1,0:T(8,128)S(1)}, s32[8,1024]{1,0:T(8,128)}, u32[]{:S(2)}) copy-start(s32[8,1024]{1,0:T(8,128)} %species.1) | copy-start | bytes 98308
  22.9 13.6 %copy-start.2 = (f32[4]{0:T(128)S(1)}, f32[4]{0:T(128)}, u32[]{:S(2)}) copy-start(f32[4]{0:T(128)} %rates.1) | copy-start | bytes 52
  26.3 3.6 %collective-permute-start.7 = (f32[48,128]{1,0:T(8,128)S(1)}, f32[48,128]{1,0:T(8,128)S(1)}, u32[]{:S(2)}, u32[]{:S(2)}) collective-permute-start(f32[48,128]{1,0:T(8,128)S(1)} %slice.80), channel_id=1, source_target_pairs={{0,6},{1,7},{2,4},{3,5},{4,2},{5,3},{6,0},{7,1},{8,14},{9,15},{10,... | collective-permute-start | bytes 73736 | tf_op jit(solution)/shard_map/ppermute | solution.py:336
  27.3 3.5 %collective-permute-start.8 = (f32[48,128]{1,0:T(8,128)S(1)}, f32[48,128]{1,0:T(8,128)S(1)}, u32[]{:S(2)}, u32[]{:S(2)}) collective-permute-start(f32[48,128]{1,0:T(8,128)S(1)} %slice.80), channel_id=1, source_target_pairs={{0,4},{1,5},{2,6},{3,7},{4,0},{5,1},{6,2},{7,3},{8,12},{9,13},{10,... | collective-permute-start | bytes 73736 | tf_op jit(solution)/shard_map/ppermute | solution.py:336
  29.6 2.7 %collective-permute-start.9 = (f32[48,128]{1,0:T(8,128)S(1)}, f32[48,128]{1,0:T(8,128)S(1)}, u32[]{:S(2)}, u32[]{:S(2)}) collective-permute-start(f32[48,128]{1,0:T(8,128)S(1)} %slice.80), channel_id=1, source_target_pairs={{0,2},{1,3},{2,0},{3,1},{4,6},{5,7},{6,4},{7,5},{8,10},{9,11},{10,... | collective-permute-start | bytes 73736 | tf_op jit(solution)/shard_map/ppermute | solution.py:336
  32.3 4.2 %collective-permute-start.10 = (f32[192,128]{1,0:T(8,128)S(1)}, f32[192,128]{1,0:T(8,128)S(1)}, u32[]{:S(2)}, u32[]{:S(2)}) collective-permute-start(f32[192,128]{1,0:T(8,128)S(1)} %bitcast.79), channel_id=1, source_target_pairs={{0,1},{1,0},{2,3},{3,2},{4,5},{5,4},{6,7},{7,6},{8,9},{9,8},{10,11... | collective-permute-start | bytes 294920 | tf_op jit(solution)/shard_map/ppermute | solution.py:336
  42.9 5.0 %collective-permute-start.11 = (f32[2,1024]{1,0:T(2,128)S(1)}, f32[2,1024]{1,0:T(2,128)S(1)}, u32[]{:S(2)}, u32[]{:S(2)}) collective-permute-start(f32[2,1024]{1,0:T(2,128)S(1)} %get-tuple-element.44), channel_id=1, source_target_pairs={{1,2},{3,4},{5,6},{7,8},{9,10},{11,12},{13,14},{15,16},{17,18},{19... | collective-permute-start | bytes 24584 | tf_op jit(solution)/shard_map/ppermute | solution.py:392
  45.3 2.6 %collective-permute-start.12 = (f32[2,1024]{1,0:T(2,128)S(1)}, f32[2,1024]{1,0:T(2,128)S(1)}, u32[]{:S(2)}, u32[]{:S(2)}) collective-permute-start(f32[2,1024]{1,0:T(2,128)S(1)} %get-tuple-element.45), channel_id=1, source_target_pairs={{0,1},{1,0},{2,3},{3,2},{4,5},{5,4},{6,7},{7,6},{8,9},{9,8},{10,11... | collective-permute-start | bytes 24584 | tf_op jit(solution)/shard_map/ppermute | solution.py:393

commit v6 on v5

--- a/solution.py
+++ b/solution.py
@@ -39,7 +39,7 @@
 
     def gram_of(i):
         part = split[:, places[i]]
-        return lax.dot_general(part, part, NT, preferred_element_type=F32)
+        return lax.dot_general(part, part[0:rank], NT, preferred_element_type=F32)
 
     own = pltpu.make_async_copy(om, om_v, sems.at[2 * blocks])
     own.start()
@@ -77,8 +77,8 @@
     for part in (low, middle, high):
         projected = projected + jnp.dot(part, om_v[...], preferred_element_type=F32)
     crit[0:sketch, :] = projected
-    cross = gram[0:rank, rank:]
-    crit[sketch:, :] = gram[0:rank, 0:rank] + cross + cross.T
+    cross = gram[rank:, :]
+    crit[sketch:, :] = gram[0:rank, :] + cross + cross.T
     half = sketch // 2
     for h in range(2):
         turned = whole[h * half : (h + 1) * half, :].T
@@ -92,7 +92,7 @@
         leaving(i).wait()
 
 
-def sketches(snapshots, range_test, test_rows, shares=(1, 1, 2, 2, 2), ahead=3):
+def sketches(snapshots, range_test, test_rows, shares=(1, 1, 2, 2, 2), ahead=5):
     cells, times = snapshots.shape
     rank = range_test.shape[1]
     sketch = test_rows.shape[0]
@@ -115,7 +115,7 @@
             pltpu.VMEM((rank, cells), F32),
             pltpu.VMEM((rank, times), BF16),
             pltpu.VMEM((sketch, times), F32),
-            pltpu.VMEM((2 * rank, 2 * rank), F32),
+            pltpu.VMEM((2 * rank, rank), F32),
             pltpu.VMEM((2 * rank, cells), BF16),
             pltpu.SemaphoreType.DMA((3 * len(sizes) + 1,)),
         ],

time: 48.9 us -> 48.6 us (level)
  transfers between devices with their start and end apart: 13 -> 13, of which waited for: 9 -> 9; matrix products, arithmetic and copies ran while one was open for 1% -> 2% of each run, Pallas kernels for 5% -> 5%
where the time goes in v6:
time: 48.6 us; the launch traced here: 48.3 us
  starting transfers between devices  17 us (35%)
  Pallas kernels  16.4 us (34%)
  waiting for transfers between devices  12.2 us (25%)
  other arithmetic  0.94 us (2%)
  between operations  0.92 us (2%)
  local copies, waits for them, and re-layouts  0.88 us (2%)
    ppermute x7, starting transfers between devices, summed_pieces(): lax.ppermute(pick(pieces, me ^ p), AXES, partners(count, shift, p))  7.98 us
    pallas_call x1, Pallas kernels, sketches(): pl.pallas_call(functools.partial(sketch_kernel, sizes, ahead), in_specs=[...  7.87 us
    ppermute x7, waiting for transfers between devices, summed_pieces(): lax.ppermute(pick(pieces, me ^ p), AXES, partners(count, shift, p))  6.86 us
    ppermute x4, starting transfers between devices, gathered_pieces(): lax.ppermute(piece, AXES, partners(count, shift, p))  6.6 us
    pallas_call x1, Pallas kernels, solve(): pl.pallas_call(functools.partial(solve_kernel, cells_total, owned), in_sp...  6.28 us
    ppermute x4, waiting for transfers between devices, gathered_pieces(): lax.ppermute(piece, AXES, partners(count, shift, p))  3.5 us
    ppermute x1, starting transfers between devices, shards(): far = lax.ppermute(jnp.where(even, head, tail), AXES, across)  2.36 us
    pallas_call x1, Pallas kernels, fetch(): pl.pallas_call(fetch_kernel, in_specs=[pl.BlockSpec(memory_space=pltpu.HB...  2.22 us
  transfers between devices with their start and end apart: 13, of which 9 were waited for; matrix products, arithmetic and copies ran while one was open for 2% of the time, Pallas kernels for 5%

profile of v6, /device:TPU:1, one launch (start us, length us, event | category | flops | bytes accessed | tf_op | source)
XLA Modules:
  0.0 48.3 jit_solution(6079182382072167322)
XLA Ops:
  0.6 7.9 %sketches.1 = (f32[128,8192]{1,0:T(8,128)}, f32[2,512,128]{2,1,0:T(8,128)S(1)}, f32[384,128]{1,0:T(8,128)S(1)}) custom-call(bf16[8192,512]{1,0:T(8,128)(2,1)} %snap.1, bf16[256,8192]{1,0:T(8,128)(2,1)} %test.1, bf16[512,128]{1,0:T(8,128)(2,1)} %om.1), custom_call_target="tpu_custom_call" | custom-call | tf_op jit(solution)/shard_map/sketches/pallas_call | solution.py:102
  8.6 0.1 collective-permute-start
  8.7 1.6 %collective-permute-done = f32[704,128]{1,0:T(8,128)S(1)} collective-permute-done((f32[704,128]{1,0:T(8,128)S(1)}, f32[704,128]{1,0:T(8,128)S(1)}, u32[]{:S(2)}, u32[]{:S(2)}) %collective-permute-start) | collective-permute-done | bytes 360480 | tf_op jit(solution)/shard_map/ppermute | solution.py:327
  10.5 3.4 %collective-permute-start.1 = (f32[176,128]{1,0:T(8,128)S(1)}, f32[176,128]{1,0:T(8,128)S(1)}, u32[]{:S(2)}, u32[]{:S(2)}) collective-permute-start(f32[176,128]{1,0:T(8,128)S(1)} %get-tuple-element.26), channel_id=1, source_target_pairs={{0,6},{1,7},{2,4},{3,5},{4,2},{5,3},{6,0},{7,1},{8,14},{9,15},{10,... | collective-permute-start | bytes 270344 | tf_op jit(solution)/shard_map/ppermute | solution.py:327
  13.9 0.2 collective-permute-start.2
  14.1 0.1 collective-permute-start.3
  14.2 2.3 %collective-permute-done.1 = f32[176,128]{1,0:T(8,128)S(1)} collective-permute-done((f32[176,128]{1,0:T(8,128)S(1)}, f32[176,128]{1,0:T(8,128)S(1)}, u32[]{:S(2)}, u32[]{:S(2)}) %collective-permute-start.1) | collective-permute-done | bytes 90144 | tf_op jit(solution)/shard_map/ppermute | solution.py:327
  16.6 1.8 %collective-permute-done.2 = f32[176,128]{1,0:T(8,128)S(1)} collective-permute-done((f32[176,128]{1,0:T(8,128)S(1)}, f32[176,128]{1,0:T(8,128)S(1)}, u32[]{:S(2)}, u32[]{:S(2)}) %collective-permute-start.2) | collective-permute-done | bytes 90144 | tf_op jit(solution)/shard_map/ppermute | solution.py:327
  18.4 3.8 %collective-permute-start.4 = (f32[80,128]{1,0:T(8,128)S(1)}, f32[80,128]{1,0:T(8,128)S(1)}, u32[]{:S(2)}, u32[]{:S(2)}) collective-permute-start(f32[80,128]{1,0:T(8,128)S(1)} %get-tuple-element.29), channel_id=1, source_target_pairs={{0,24},{1,25},{2,26},{3,27},{4,28},{5,29},{6,30},{7,31},{8,16},{9,... | collective-permute-start | bytes 122888 | tf_op jit(solution)/shard_map/ppermute | solution.py:327
  22.2 0.4 collective-permute-start.6
  22.6 2.2 %fetch.1.range_t = f32[128,8192]{1,0:T(8,128)S(1)} custom-call(f32[128,8192]{1,0:T(8,128)} %get-tuple-element.16.source), custom_call_target="tpu_custom_call" | custom-call | bytes 8388608 | tf_op jit(solution)/shard_map/fetch/pallas_call | solution.py:275
  24.8 1.1 %collective-permute-done.5 = f32[80,128]{1,0:T(8,128)S(1)} collective-permute-done((f32[80,128]{1,0:T(8,128)S(1)}, f32[80,128]{1,0:T(8,128)S(1)}, u32[]{:S(2)}, u32[]{:S(2)}) %collective-permute-start.5) | collective-permute-done | bytes 40992 | tf_op jit(solution)/shard_map/ppermute | solution.py:327
  26.0 1.0 %collective-permute-start.7 = (f32[48,128]{1,0:T(8,128)S(1)}, f32[48,128]{1,0:T(8,128)S(1)}, u32[]{:S(2)}, u32[]{:S(2)}) collective-permute-start(f32[48,128]{1,0:T(8,128)S(1)} %slice.80), channel_id=1, source_target_pairs={{0,6},{1,7},{2,4},{3,5},{4,2},{5,3},{6,0},{7,1},{8,14},{9,15},{10,... | collective-permute-start | bytes 73736 | tf_op jit(solution)/shard_map/ppermute | solution.py:336
  26.9 2.3 %collective-permute-start.8 = (f32[48,128]{1,0:T(8,128)S(1)}, f32[48,128]{1,0:T(8,128)S(1)}, u32[]{:S(2)}, u32[]{:S(2)}) collective-permute-start(f32[48,128]{1,0:T(8,128)S(1)} %slice.80), channel_id=1, source_target_pairs={{0,4},{1,5},{2,6},{3,7},{4,0},{5,1},{6,2},{7,3},{8,12},{9,13},{10,... | collective-permute-start | bytes 73736 | tf_op jit(solution)/shard_map/ppermute | solution.py:336
  29.3 0.3 collective-permute-done.7
  29.6 0.8 %collective-permute-done.8 = f32[48,128]{1,0:T(8,128)S(1)} collective-permute-done((f32[48,128]{1,0:T(8,128)S(1)}, f32[48,128]{1,0:T(8,128)S(1)}, u32[]{:S(2)}, u32[]{:S(2)}) %collective-permute-start.8) | collective-permute-done | bytes 24608 | tf_op jit(solution)/shard_map/ppermute | solution.py:336
  30.5 1.5 %collective-permute-done.9 = f32[48,128]{1,0:T(8,128)S(1)} collective-permute-done((f32[48,128]{1,0:T(8,128)S(1)}, f32[48,128]{1,0:T(8,128)S(1)}, u32[]{:S(2)}, u32[]{:S(2)}) %collective-permute-start.9) | collective-permute-done | bytes 24608 | tf_op jit(solution)/shard_map/ppermute | solution.py:336
  31.9 3.3 %collective-permute-start.10 = (f32[192,128]{1,0:T(8,128)S(1)}, f32[192,128]{1,0:T(8,128)S(1)}, u32[]{:S(2)}, u32[]{:S(2)}) collective-permute-start(f32[192,128]{1,0:T(8,128)S(1)} %bitcast.79), channel_id=1, source_target_pairs={{0,1},{1,0},{2,3},{3,2},{4,5},{5,4},{6,7},{7,6},{8,9},{9,8},{10,11... | collective-permute-start | bytes 294920 | tf_op jit(solution)/shard_map/ppermute | solution.py:336
  35.3 0.9 %collective-permute-done.10 = f32[192,128]{1,0:T(8,128)S(1)} collective-permute-done((f32[192,128]{1,0:T(8,128)S(1)}, f32[192,128]{1,0:T(8,128)S(1)}, u32[]{:S(2)}, u32[]{:S(2)}) %collective-permute-start.10) | collective-permute-done | bytes 98336 | tf_op jit(solution)/shard_map/ppermute | solution.py:336
  36.2 6.3 %solve.1 = (f32[128,16]{1,0:T(8,128)S(1)}, f32[8,1024]{1,0:T(8,128)S(1)}, f32[8,1024]{1,0:T(8,128)S(1)}) custom-call(f32[384,128]{1,0:T(8,128)S(1)} %bitcast.65, f32[2,16,128]{2,1,0:T(8,128)S(1)} %bitcast.69, f32[128,8192]{1,0:T(8,128)S(1)} %fetch.1.range_t, f32[8,1024]{1,0:T(8,128)S(1)} %copy-done, s32[8,1024]{1,0:T(8,128)S(1)} %copy-done.1, f32[4]{0:T(128)S(1)} %copy-done.2), custom_call_target="tpu_custom_call" | custom-call | tf_op jit(solution)/shard_map/solve/pallas_call | solution.py:292
  42.6 2.4 %collective-permute-start.11 = (f32[2,1024]{1,0:T(2,128)S(1)}, f32[2,1024]{1,0:T(2,128)S(1)}, u32[]{:S(2)}, u32[]{:S(2)}) collective-permute-start(f32[2,1024]{1,0:T(2,128)S(1)} %get-tuple-element.44), channel_id=1, source_target_pairs={{1,2},{3,4},{5,6},{7,8},{9,10},{11,12},{13,14},{15,16},{17,18},{19... | collective-permute-start | bytes 24584 | tf_op jit(solution)/shard_map/ppermute | solution.py:392
  45.0 0.7 %copy.14 = f32[128,16]{0,1:T(8,128)} copy(f32[128,16]{1,0:T(8,128)S(1)} %get-tuple-element.25) | data formatting | bytes 16384
  45.7 1.8 %collective-permute-done.11 = f32[2,1024]{1,0:T(2,128)S(1)} collective-permute-done((f32[2,1024]{1,0:T(2,128)S(1)}, f32[2,1024]{1,0:T(2,128)S(1)}, u32[]{:S(2)}, u32[]{:S(2)}) %collective-permute-start.11) | collective-permute-done | bytes 8224 | tf_op jit(solution)/shard_map/ppermute | solution.py:392
  47.6 0.7 %fusion.32 = f32[8,1024]{1,0:T(8,128)} fusion(f32[8,1024]{1,0:T(8,128)S(1)} %pad_maximum_fusion, f32[1,1024]{1,0:T(1,128)S(1)} %get-tuple-element.40, f32[1,1024]{1,0:T(1,128)S(1)} %get-tuple-element.35, f32[6,1024]{1,0:T(8,128)S(1)} %slice.70, f32[1,1024]{1,0:T(1,128)S(1)} %get-tuple-element.34, f32[1,1024]{1,0:T(1,128)S(1)} %get-tuple-element.41, ...), kind=kLoop, calls=%fused_computation.56 | loop fusion | flops 106496 | bytes 139264 | tf_op jit(solution)/shard_map/add | solution.py:404
  (43 shorter events, 0.6 us)
Async XLA Ops:
  8.6 1.7 %collective-permute-start = (f32[704,128]{1,0:T(8,128)S(1)}, f32[704,128]{1,0:T(8,128)S(1)}, u32[]{:S(2)}, u32[]{:S(2)}) collective-permute-start(f32[704,128]{1,0:T(8,128)S(1)} %fusion.1), channel_id=1, source_target_pairs={{0,1},{1,0},{2,3},{3,2},{4,5},{5,4},{6,7},{7,6},{8,9},{9,8},{10,11... | collective-permute-start | bytes 1081352 | tf_op jit(solution)/shard_map/ppermute | solution.py:327
  10.5 6.1 %collective-permute-start.1 = (f32[176,128]{1,0:T(8,128)S(1)}, f32[176,128]{1,0:T(8,128)S(1)}, u32[]{:S(2)}, u32[]{:S(2)}) collective-permute-start(f32[176,128]{1,0:T(8,128)S(1)} %get-tuple-element.26), channel_id=1, source_target_pairs={{0,6},{1,7},{2,4},{3,5},{4,2},{5,3},{6,0},{7,1},{8,14},{9,15},{10,... | collective-permute-start | bytes 270344 | tf_op jit(solution)/shard_map/ppermute | solution.py:327
  13.9 4.5 %collective-permute-start.2 = (f32[176,128]{1,0:T(8,128)S(1)}, f32[176,128]{1,0:T(8,128)S(1)}, u32[]{:S(2)}, u32[]{:S(2)}) collective-permute-start(f32[176,128]{1,0:T(8,128)S(1)} %get-tuple-element.27), channel_id=1, source_target_pairs={{0,4},{1,5},{2,6},{3,7},{4,0},{5,1},{6,2},{7,3},{8,12},{9,13},{10,... | collective-permute-start | bytes 270344 | tf_op jit(solution)/shard_map/ppermute | solution.py:327
  14.1 4.2 %collective-permute-start.3 = (f32[176,128]{1,0:T(8,128)S(1)}, f32[176,128]{1,0:T(8,128)S(1)}, u32[]{:S(2)}, u32[]{:S(2)}) collective-permute-start(f32[176,128]{1,0:T(8,128)S(1)} %get-tuple-element.28), channel_id=1, source_target_pairs={{0,2},{1,3},{2,0},{3,1},{4,6},{5,7},{6,4},{7,5},{8,10},{9,11},{10,... | collective-permute-start | bytes 270344 | tf_op jit(solution)/shard_map/ppermute | solution.py:327
  18.4 6.4 %collective-permute-start.4 = (f32[80,128]{1,0:T(8,128)S(1)}, f32[80,128]{1,0:T(8,128)S(1)}, u32[]{:S(2)}, u32[]{:S(2)}) collective-permute-start(f32[80,128]{1,0:T(8,128)S(1)} %get-tuple-element.29), channel_id=1, source_target_pairs={{0,24},{1,25},{2,26},{3,27},{4,28},{5,29},{6,30},{7,31},{8,16},{9,... | collective-permute-start | bytes 122888 | tf_op jit(solution)/shard_map/ppermute | solution.py:327
  22.2 3.8 %collective-permute-start.5 = (f32[80,128]{1,0:T(8,128)S(1)}, f32[80,128]{1,0:T(8,128)S(1)}, u32[]{:S(2)}, u32[]{:S(2)}) collective-permute-start(f32[80,128]{1,0:T(8,128)S(1)} %get-tuple-element.30), channel_id=1, source_target_pairs={{0,16},{1,17},{2,18},{3,19},{4,20},{5,21},{6,22},{7,23},{8,24},{9,... | collective-permute-start | bytes 122888 | tf_op jit(solution)/shard_map/ppermute | solution.py:327
  22.2 3.8 %collective-permute-start.6 = (f32[80,128]{1,0:T(8,128)S(1)}, f32[80,128]{1,0:T(8,128)S(1)}, u32[]{:S(2)}, u32[]{:S(2)}) collective-permute-start(f32[80,128]{1,0:T(8,128)S(1)} %get-tuple-element.31), channel_id=1, source_target_pairs={{0,8},{1,9},{2,10},{3,11},{4,12},{5,13},{6,14},{7,15},{8,0},{9,1},... | collective-permute-start | bytes 122888 | tf_op jit(solution)/shard_map/ppermute | solution.py:327
  22.6 13.6 %copy-start = (f32[8,1024]{1,0:T(8,128)S(1)}, f32[8,1024]{1,0:T(8,128)}, u32[]{:S(2)}) copy-start(f32[8,1024]{1,0:T(8,128)} %adjoint.1) | copy-start | bytes 98308
  22.6 13.6 %copy-start.1 = (s32[8,1024]{1,0:T(8,128)S(1)}, s32[8,1024]{1,0:T(8,128)}, u32[]{:S(2)}) copy-start(s32[8,1024]{1,0:T(8,128)} %species.1) | copy-start | bytes 98308
  22.6 13.6 %copy-start.2 = (f32[4]{0:T(128)S(1)}, f32[4]{0:T(128)}, u32[]{:S(2)}) copy-start(f32[4]{0:T(128)} %rates.1) | copy-start | bytes 52
  26.0 3.6 %collective-permute-start.7 = (f32[48,128]{1,0:T(8,128)S(1)}, f32[48,128]{1,0:T(8,128)S(1)}, u32[]{:S(2)}, u32[]{:S(2)}) collective-permute-start(f32[48,128]{1,0:T(8,128)S(1)} %slice.80), channel_id=1, source_target_pairs={{0,6},{1,7},{2,4},{3,5},{4,2},{5,3},{6,0},{7,1},{8,14},{9,15},{10,... | collective-permute-start | bytes 73736 | tf_op jit(solution)/shard_map/ppermute | solution.py:336
  26.9 3.5 %collective-permute-start.8 = (f32[48,128]{1,0:T(8,128)S(1)}, f32[48,128]{1,0:T(8,128)S(1)}, u32[]{:S(2)}, u32[]{:S(2)}) collective-permute-start(f32[48,128]{1,0:T(8,128)S(1)} %slice.80), channel_id=1, source_target_pairs={{0,4},{1,5},{2,6},{3,7},{4,0},{5,1},{6,2},{7,3},{8,12},{9,13},{10,... | collective-permute-start | bytes 73736 | tf_op jit(solution)/shard_map/ppermute | solution.py:336
  29.2 2.7 %collective-permute-start.9 = (f32[48,128]{1,0:T(8,128)S(1)}, f32[48,128]{1,0:T(8,128)S(1)}, u32[]{:S(2)}, u32[]{:S(2)}) collective-permute-start(f32[48,128]{1,0:T(8,128)S(1)} %slice.80), channel_id=1, source_target_pairs={{0,2},{1,3},{2,0},{3,1},{4,6},{5,7},{6,4},{7,5},{8,10},{9,11},{10,... | collective-permute-start | bytes 73736 | tf_op jit(solution)/shard_map/ppermute | solution.py:336
  31.9 4.2 %collective-permute-start.10 = (f32[192,128]{1,0:T(8,128)S(1)}, f32[192,128]{1,0:T(8,128)S(1)}, u32[]{:S(2)}, u32[]{:S(2)}) collective-permute-start(f32[192,128]{1,0:T(8,128)S(1)} %bitcast.79), channel_id=1, source_target_pairs={{0,1},{1,0},{2,3},{3,2},{4,5},{5,4},{6,7},{7,6},{8,9},{9,8},{10,11... | collective-permute-start | bytes 294920 | tf_op jit(solution)/shard_map/ppermute | solution.py:336
  42.6 5.0 %collective-permute-start.11 = (f32[2,1024]{1,0:T(2,128)S(1)}, f32[2,1024]{1,0:T(2,128)S(1)}, u32[]{:S(2)}, u32[]{:S(2)}) collective-permute-start(f32[2,1024]{1,0:T(2,128)S(1)} %get-tuple-element.44), channel_id=1, source_target_pairs={{1,2},{3,4},{5,6},{7,8},{9,10},{11,12},{13,14},{15,16},{17,18},{19... | collective-permute-start | bytes 24584 | tf_op jit(solution)/shard_map/ppermute | solution.py:392
  44.9 2.6 %collective-permute-start.12 = (f32[2,1024]{1,0:T(2,128)S(1)}, f32[2,1024]{1,0:T(2,128)S(1)}, u32[]{:S(2)}, u32[]{:S(2)}) collective-permute-start(f32[2,1024]{1,0:T(2,128)S(1)} %get-tuple-element.45), channel_id=1, source_target_pairs={{0,1},{1,0},{2,3},{3,2},{4,5},{5,4},{6,7},{7,6},{8,9},{9,8},{10,11... | collective-permute-start | bytes 24584 | tf_op jit(solution)/shard_map/ppermute | solution.py:393

commit v7 on v6

--- a/solution.py
+++ b/solution.py
@@ -324,7 +324,7 @@
 def summed_pieces(pieces, count, shift):
     size = pieces.shape[0]
     me = member(shift, size)
-    got = [lax.ppermute(pick(pieces, me ^ p), AXES, partners(count, shift, p)) for p in range(size - 1, 0, -1)]
+    got = [lax.ppermute(pick(pieces, me ^ p), AXES, partners(count, shift, p)) for p in ([2, 3, 1] if size == 4 and shift > 1 else range(size - 1, 0, -1))]
     total = pick(pieces, me)
     for piece in got:
         total = total + piece
@@ -389,8 +389,8 @@
     tail = jnp.concatenate([partial[-1:], adjoint_end[-1:]], axis=0)
     pairs = [(i, i ^ 1) for i in range(count)]
     across = [(i, i + 1) for i in range(1, count - 1, 2)] + [(i + 1, i) for i in range(1, count - 1, 2)]
+    near = lax.ppermute(jnp.where(even, tail, head), AXES, pairs)
     far = lax.ppermute(jnp.where(even, head, tail), AXES, across)
-    near = lax.ppermute(jnp.where(even, tail, head), AXES, pairs)
     above = jnp.where(even, far, near)
     below = jnp.where(even, near, far)
     adjoint = jnp.concatenate(

time: 48.6 us -> 48.4 us (level)
  no operation moved by 1% of the time
where the time goes in v7:
time: 48.4 us; the launch traced here: 48.2 us
  starting transfers between devices  16.9 us (35%)
  Pallas kernels  16.4 us (34%)
  waiting for transfers between devices  12.2 us (25%)
  other arithmetic  0.94 us (2%)
  between operations  0.92 us (2%)
  local copies, waits for them, and re-layouts  0.88 us (2%)
    ppermute x7, starting transfers between devices, summed_pieces(): lax.ppermute(pick(pieces, me ^ p), AXES, partners(count, shift, p))  7.9 us
    pallas_call x1, Pallas kernels, sketches(): pl.pallas_call(functools.partial(sketch_kernel, sizes, ahead), in_specs=[...  7.87 us
    ppermute x7, waiting for transfers between devices, summed_pieces(): lax.ppermute(pick(pieces, me ^ p), AXES, partners(count, shift, p))  6.86 us
    ppermute x4, starting transfers between devices, gathered_pieces(): lax.ppermute(piece, AXES, partners(count, shift, p))  6.55 us
    pallas_call x1, Pallas kernels, solve(): pl.pallas_call(functools.partial(solve_kernel, cells_total, owned), in_sp...  6.28 us
    ppermute x4, waiting for transfers between devices, gathered_pieces(): lax.ppermute(piece, AXES, partners(count, shift, p))  3.51 us
    ppermute x1, starting transfers between devices, shards(): far = lax.ppermute(jnp.where(even, head, tail), AXES, across)  2.36 us
    pallas_call x1, Pallas kernels, fetch(): pl.pallas_call(fetch_kernel, in_specs=[pl.BlockSpec(memory_space=pltpu.HB...  2.22 us
  transfers between devices with their start and end apart: 13, of which 9 were waited for; matrix products, arithmetic and copies ran while one was open for 2% of the time, Pallas kernels for 5%

profile of v7, /device:TPU:1, one launch (start us, length us, event | category | flops | bytes accessed | tf_op | source)
XLA Modules:
  0.0 48.2 jit_solution(1737919787869460639)
XLA Ops:
  0.6 7.9 %sketches.1 = (f32[128,8192]{1,0:T(8,128)}, f32[2,512,128]{2,1,0:T(8,128)S(1)}, f32[384,128]{1,0:T(8,128)S(1)}) custom-call(bf16[8192,512]{1,0:T(8,128)(2,1)} %snap.1, bf16[256,8192]{1,0:T(8,128)(2,1)} %test.1, bf16[512,128]{1,0:T(8,128)(2,1)} %om.1), custom_call_target="tpu_custom_call" | custom-call | tf_op jit(solution)/shard_map/sketches/pallas_call | solution.py:102
  8.7 1.6 %collective-permute-done = f32[704,128]{1,0:T(8,128)S(1)} collective-permute-done((f32[704,128]{1,0:T(8,128)S(1)}, f32[704,128]{1,0:T(8,128)S(1)}, u32[]{:S(2)}, u32[]{:S(2)}) %collective-permute-start) | collective-permute-done | bytes 360480 | tf_op jit(solution)/shard_map/ppermute | solution.py:327
  10.5 3.4 %collective-permute-start.1 = (f32[176,128]{1,0:T(8,128)S(1)}, f32[176,128]{1,0:T(8,128)S(1)}, u32[]{:S(2)}, u32[]{:S(2)}) collective-permute-start(f32[176,128]{1,0:T(8,128)S(1)} %get-tuple-element.26), channel_id=1, source_target_pairs={{0,6},{1,7},{2,4},{3,5},{4,2},{5,3},{6,0},{7,1},{8,14},{9,15},{10,... | collective-permute-start | bytes 270344 | tf_op jit(solution)/shard_map/ppermute | solution.py:327
  13.9 0.2 collective-permute-start.2
  14.1 0.1 collective-permute-start.3
  14.2 2.3 %collective-permute-done.1 = f32[176,128]{1,0:T(8,128)S(1)} collective-permute-done((f32[176,128]{1,0:T(8,128)S(1)}, f32[176,128]{1,0:T(8,128)S(1)}, u32[]{:S(2)}, u32[]{:S(2)}) %collective-permute-start.1) | collective-permute-done | bytes 90144 | tf_op jit(solution)/shard_map/ppermute | solution.py:327
  16.6 1.8 %collective-permute-done.2 = f32[176,128]{1,0:T(8,128)S(1)} collective-permute-done((f32[176,128]{1,0:T(8,128)S(1)}, f32[176,128]{1,0:T(8,128)S(1)}, u32[]{:S(2)}, u32[]{:S(2)}) %collective-permute-start.2) | collective-permute-done | bytes 90144 | tf_op jit(solution)/shard_map/ppermute | solution.py:327
  18.4 2.8 %collective-permute-start.4 = (f32[80,128]{1,0:T(8,128)S(1)}, f32[80,128]{1,0:T(8,128)S(1)}, u32[]{:S(2)}, u32[]{:S(2)}) collective-permute-start(f32[80,128]{1,0:T(8,128)S(1)} %get-tuple-element.29), channel_id=1, source_target_pairs={{0,16},{1,17},{2,18},{3,19},{4,20},{5,21},{6,22},{7,23},{8,24},{9,... | collective-permute-start | bytes 122888 | tf_op jit(solution)/shard_map/ppermute | solution.py:327
  21.2 1.1 %collective-permute-start.5 = (f32[80,128]{1,0:T(8,128)S(1)}, f32[80,128]{1,0:T(8,128)S(1)}, u32[]{:S(2)}, u32[]{:S(2)}) collective-permute-start(f32[80,128]{1,0:T(8,128)S(1)} %get-tuple-element.30), channel_id=1, source_target_pairs={{0,24},{1,25},{2,26},{3,27},{4,28},{5,29},{6,30},{7,31},{8,16},{9,... | collective-permute-start | bytes 122888 | tf_op jit(solution)/shard_map/ppermute | solution.py:327
  22.3 0.2 collective-permute-start.6
  22.5 2.2 %fetch.1.range_t = f32[128,8192]{1,0:T(8,128)S(1)} custom-call(f32[128,8192]{1,0:T(8,128)} %get-tuple-element.16.source), custom_call_target="tpu_custom_call" | custom-call | bytes 8388608 | tf_op jit(solution)/shard_map/fetch/pallas_call | solution.py:275
  24.7 1.1 %collective-permute-done.5 = f32[80,128]{1,0:T(8,128)S(1)} collective-permute-done((f32[80,128]{1,0:T(8,128)S(1)}, f32[80,128]{1,0:T(8,128)S(1)}, u32[]{:S(2)}, u32[]{:S(2)}) %collective-permute-start.5) | collective-permute-done | bytes 40992 | tf_op jit(solution)/shard_map/ppermute | solution.py:327
  25.9 1.1 %collective-permute-start.7 = (f32[48,128]{1,0:T(8,128)S(1)}, f32[48,128]{1,0:T(8,128)S(1)}, u32[]{:S(2)}, u32[]{:S(2)}) collective-permute-start(f32[48,128]{1,0:T(8,128)S(1)} %slice.80), channel_id=1, source_target_pairs={{0,6},{1,7},{2,4},{3,5},{4,2},{5,3},{6,0},{7,1},{8,14},{9,15},{10,... | collective-permute-start | bytes 73736 | tf_op jit(solution)/shard_map/ppermute | solution.py:336
  27.0 1.7 %collective-permute-start.8 = (f32[48,128]{1,0:T(8,128)S(1)}, f32[48,128]{1,0:T(8,128)S(1)}, u32[]{:S(2)}, u32[]{:S(2)}) collective-permute-start(f32[48,128]{1,0:T(8,128)S(1)} %slice.80), channel_id=1, source_target_pairs={{0,4},{1,5},{2,6},{3,7},{4,0},{5,1},{6,2},{7,3},{8,12},{9,13},{10,... | collective-permute-start | bytes 73736 | tf_op jit(solution)/shard_map/ppermute | solution.py:336
  28.8 0.8 %collective-permute-done.7 = f32[48,128]{1,0:T(8,128)S(1)} collective-permute-done((f32[48,128]{1,0:T(8,128)S(1)}, f32[48,128]{1,0:T(8,128)S(1)}, u32[]{:S(2)}, u32[]{:S(2)}) %collective-permute-start.7) | collective-permute-done | bytes 24608 | tf_op jit(solution)/shard_map/ppermute | solution.py:336
  29.6 0.4 collective-permute-done.8
  29.9 1.5 %collective-permute-done.9 = f32[48,128]{1,0:T(8,128)S(1)} collective-permute-done((f32[48,128]{1,0:T(8,128)S(1)}, f32[48,128]{1,0:T(8,128)S(1)}, u32[]{:S(2)}, u32[]{:S(2)}) %collective-permute-start.9) | collective-permute-done | bytes 24608 | tf_op jit(solution)/shard_map/ppermute | solution.py:336
  31.4 3.7 %collective-permute-start.10 = (f32[192,128]{1,0:T(8,128)S(1)}, f32[192,128]{1,0:T(8,128)S(1)}, u32[]{:S(2)}, u32[]{:S(2)}) collective-permute-start(f32[192,128]{1,0:T(8,128)S(1)} %bitcast.79), channel_id=1, source_target_pairs={{0,1},{1,0},{2,3},{3,2},{4,5},{5,4},{6,7},{7,6},{8,9},{9,8},{10,11... | collective-permute-start | bytes 294920 | tf_op jit(solution)/shard_map/ppermute | solution.py:336
  35.2 0.9 %collective-permute-done.10 = f32[192,128]{1,0:T(8,128)S(1)} collective-permute-done((f32[192,128]{1,0:T(8,128)S(1)}, f32[192,128]{1,0:T(8,128)S(1)}, u32[]{:S(2)}, u32[]{:S(2)}) %collective-permute-start.10) | collective-permute-done | bytes 98336 | tf_op jit(solution)/shard_map/ppermute | solution.py:336
  36.1 6.3 %solve.1 = (f32[128,16]{1,0:T(8,128)S(1)}, f32[8,1024]{1,0:T(8,128)S(1)}, f32[8,1024]{1,0:T(8,128)S(1)}) custom-call(f32[384,128]{1,0:T(8,128)S(1)} %bitcast.65, f32[2,16,128]{2,1,0:T(8,128)S(1)} %bitcast.69, f32[128,8192]{1,0:T(8,128)S(1)} %fetch.1.range_t, f32[8,1024]{1,0:T(8,128)S(1)} %copy-done, s32[8,1024]{1,0:T(8,128)S(1)} %copy-done.1, f32[4]{0:T(128)S(1)} %copy-done.2), custom_call_target="tpu_custom_call" | custom-call | tf_op jit(solution)/shard_map/solve/pallas_call | solution.py:292
  42.4 2.4 %collective-permute-start.11 = (f32[2,1024]{1,0:T(2,128)S(1)}, f32[2,1024]{1,0:T(2,128)S(1)}, u32[]{:S(2)}, u32[]{:S(2)}) collective-permute-start(f32[2,1024]{1,0:T(2,128)S(1)} %get-tuple-element.44), channel_id=1, source_target_pairs={{1,2},{3,4},{5,6},{7,8},{9,10},{11,12},{13,14},{15,16},{17,18},{19... | collective-permute-start | bytes 24584 | tf_op jit(solution)/shard_map/ppermute | solution.py:393
  44.9 0.7 %copy.14 = f32[128,16]{0,1:T(8,128)} copy(f32[128,16]{1,0:T(8,128)S(1)} %get-tuple-element.25) | data formatting | bytes 16384
  45.6 1.8 %collective-permute-done.11 = f32[2,1024]{1,0:T(2,128)S(1)} collective-permute-done((f32[2,1024]{1,0:T(2,128)S(1)}, f32[2,1024]{1,0:T(2,128)S(1)}, u32[]{:S(2)}, u32[]{:S(2)}) %collective-permute-start.11) | collective-permute-done | bytes 8224 | tf_op jit(solution)/shard_map/ppermute | solution.py:393
  47.5 0.7 %fusion.32 = f32[8,1024]{1,0:T(8,128)} fusion(f32[8,1024]{1,0:T(8,128)S(1)} %pad_maximum_fusion, f32[1,1024]{1,0:T(1,128)S(1)} %get-tuple-element.40, f32[1,1024]{1,0:T(1,128)S(1)} %get-tuple-element.35, f32[6,1024]{1,0:T(8,128)S(1)} %slice.70, f32[1,1024]{1,0:T(1,128)S(1)} %get-tuple-element.34, f32[1,1024]{1,0:T(1,128)S(1)} %get-tuple-element.41, ...), kind=kLoop, calls=%fused_computation.56 | loop fusion | flops 106496 | bytes 139264 | tf_op jit(solution)/shard_map/add | solution.py:404
  (43 shorter events, 0.7 us)
Async XLA Ops:
  8.6 1.7 %collective-permute-start = (f32[704,128]{1,0:T(8,128)S(1)}, f32[704,128]{1,0:T(8,128)S(1)}, u32[]{:S(2)}, u32[]{:S(2)}) collective-permute-start(f32[704,128]{1,0:T(8,128)S(1)} %fusion.1), channel_id=1, source_target_pairs={{0,1},{1,0},{2,3},{3,2},{4,5},{5,4},{6,7},{7,6},{8,9},{9,8},{10,11... | collective-permute-start | bytes 1081352 | tf_op jit(solution)/shard_map/ppermute | solution.py:327
  10.5 6.1 %collective-permute-start.1 = (f32[176,128]{1,0:T(8,128)S(1)}, f32[176,128]{1,0:T(8,128)S(1)}, u32[]{:S(2)}, u32[]{:S(2)}) collective-permute-start(f32[176,128]{1,0:T(8,128)S(1)} %get-tuple-element.26), channel_id=1, source_target_pairs={{0,6},{1,7},{2,4},{3,5},{4,2},{5,3},{6,0},{7,1},{8,14},{9,15},{10,... | collective-permute-start | bytes 270344 | tf_op jit(solution)/shard_map/ppermute | solution.py:327
  13.9 4.5 %collective-permute-start.2 = (f32[176,128]{1,0:T(8,128)S(1)}, f32[176,128]{1,0:T(8,128)S(1)}, u32[]{:S(2)}, u32[]{:S(2)}) collective-permute-start(f32[176,128]{1,0:T(8,128)S(1)} %get-tuple-element.27), channel_id=1, source_target_pairs={{0,4},{1,5},{2,6},{3,7},{4,0},{5,1},{6,2},{7,3},{8,12},{9,13},{10,... | collective-permute-start | bytes 270344 | tf_op jit(solution)/shard_map/ppermute | solution.py:327
  14.1 4.2 %collective-permute-start.3 = (f32[176,128]{1,0:T(8,128)S(1)}, f32[176,128]{1,0:T(8,128)S(1)}, u32[]{:S(2)}, u32[]{:S(2)}) collective-permute-start(f32[176,128]{1,0:T(8,128)S(1)} %get-tuple-element.28), channel_id=1, source_target_pairs={{0,2},{1,3},{2,0},{3,1},{4,6},{5,7},{6,4},{7,5},{8,10},{9,11},{10,... | collective-permute-start | bytes 270344 | tf_op jit(solution)/shard_map/ppermute | solution.py:327
  18.4 6.3 %collective-permute-start.4 = (f32[80,128]{1,0:T(8,128)S(1)}, f32[80,128]{1,0:T(8,128)S(1)}, u32[]{:S(2)}, u32[]{:S(2)}) collective-permute-start(f32[80,128]{1,0:T(8,128)S(1)} %get-tuple-element.29), channel_id=1, source_target_pairs={{0,16},{1,17},{2,18},{3,19},{4,20},{5,21},{6,22},{7,23},{8,24},{9,... | collective-permute-start | bytes 122888 | tf_op jit(solution)/shard_map/ppermute | solution.py:327
  21.2 4.7 %collective-permute-start.5 = (f32[80,128]{1,0:T(8,128)S(1)}, f32[80,128]{1,0:T(8,128)S(1)}, u32[]{:S(2)}, u32[]{:S(2)}) collective-permute-start(f32[80,128]{1,0:T(8,128)S(1)} %get-tuple-element.30), channel_id=1, source_target_pairs={{0,24},{1,25},{2,26},{3,27},{4,28},{5,29},{6,30},{7,31},{8,16},{9,... | collective-permute-start | bytes 122888 | tf_op jit(solution)/shard_map/ppermute | solution.py:327
  22.3 3.6 %collective-permute-start.6 = (f32[80,128]{1,0:T(8,128)S(1)}, f32[80,128]{1,0:T(8,128)S(1)}, u32[]{:S(2)}, u32[]{:S(2)}) collective-permute-start(f32[80,128]{1,0:T(8,128)S(1)} %get-tuple-element.31), channel_id=1, source_target_pairs={{0,8},{1,9},{2,10},{3,11},{4,12},{5,13},{6,14},{7,15},{8,0},{9,1},... | collective-permute-start | bytes 122888 | tf_op jit(solution)/shard_map/ppermute | solution.py:327
  22.5 13.6 %copy-start = (f32[8,1024]{1,0:T(8,128)S(1)}, f32[8,1024]{1,0:T(8,128)}, u32[]{:S(2)}) copy-start(f32[8,1024]{1,0:T(8,128)} %adjoint.1) | copy-start | bytes 98308
  22.5 13.6 %copy-start.1 = (s32[8,1024]{1,0:T(8,128)S(1)}, s32[8,1024]{1,0:T(8,128)}, u32[]{:S(2)}) copy-start(s32[8,1024]{1,0:T(8,128)} %species.1) | copy-start | bytes 98308
  22.5 13.6 %copy-start.2 = (f32[4]{0:T(128)S(1)}, f32[4]{0:T(128)}, u32[]{:S(2)}) copy-start(f32[4]{0:T(128)} %rates.1) | copy-start | bytes 52
  25.9 3.6 %collective-permute-start.7 = (f32[48,128]{1,0:T(8,128)S(1)}, f32[48,128]{1,0:T(8,128)S(1)}, u32[]{:S(2)}, u32[]{:S(2)}) collective-permute-start(f32[48,128]{1,0:T(8,128)S(1)} %slice.80), channel_id=1, source_target_pairs={{0,6},{1,7},{2,4},{3,5},{4,2},{5,3},{6,0},{7,1},{8,14},{9,15},{10,... | collective-permute-start | bytes 73736 | tf_op jit(solution)/shard_map/ppermute | solution.py:336
  27.0 2.9 %collective-permute-start.8 = (f32[48,128]{1,0:T(8,128)S(1)}, f32[48,128]{1,0:T(8,128)S(1)}, u32[]{:S(2)}, u32[]{:S(2)}) collective-permute-start(f32[48,128]{1,0:T(8,128)S(1)} %slice.80), channel_id=1, source_target_pairs={{0,4},{1,5},{2,6},{3,7},{4,0},{5,1},{6,2},{7,3},{8,12},{9,13},{10,... | collective-permute-start | bytes 73736 | tf_op jit(solution)/shard_map/ppermute | solution.py:336
  28.7 2.7 %collective-permute-start.9 = (f32[48,128]{1,0:T(8,128)S(1)}, f32[48,128]{1,0:T(8,128)S(1)}, u32[]{:S(2)}, u32[]{:S(2)}) collective-permute-start(f32[48,128]{1,0:T(8,128)S(1)} %slice.80), channel_id=1, source_target_pairs={{0,2},{1,3},{2,0},{3,1},{4,6},{5,7},{6,4},{7,5},{8,10},{9,11},{10,... | collective-permute-start | bytes 73736 | tf_op jit(solution)/shard_map/ppermute | solution.py:336
  31.4 4.7 %collective-permute-start.10 = (f32[192,128]{1,0:T(8,128)S(1)}, f32[192,128]{1,0:T(8,128)S(1)}, u32[]{:S(2)}, u32[]{:S(2)}) collective-permute-start(f32[192,128]{1,0:T(8,128)S(1)} %bitcast.79), channel_id=1, source_target_pairs={{0,1},{1,0},{2,3},{3,2},{4,5},{5,4},{6,7},{7,6},{8,9},{9,8},{10,11... | collective-permute-start | bytes 294920 | tf_op jit(solution)/shard_map/ppermute | solution.py:336
  42.4 5.0 %collective-permute-start.11 = (f32[2,1024]{1,0:T(2,128)S(1)}, f32[2,1024]{1,0:T(2,128)S(1)}, u32[]{:S(2)}, u32[]{:S(2)}) collective-permute-start(f32[2,1024]{1,0:T(2,128)S(1)} %get-tuple-element.44), channel_id=1, source_target_pairs={{1,2},{3,4},{5,6},{7,8},{9,10},{11,12},{13,14},{15,16},{17,18},{19... | collective-permute-start | bytes 24584 | tf_op jit(solution)/shard_map/ppermute | solution.py:393
  44.8 2.6 %collective-permute-start.12 = (f32[2,1024]{1,0:T(2,128)S(1)}, f32[2,1024]{1,0:T(2,128)S(1)}, u32[]{:S(2)}, u32[]{:S(2)}) collective-permute-start(f32[2,1024]{1,0:T(2,128)S(1)} %get-tuple-element.45), channel_id=1, source_target_pairs={{0,1},{1,0},{2,3},{3,2},{4,5},{5,4},{6,7},{7,6},{8,9},{9,8},{10,11... | collective-permute-start | bytes 24584 | tf_op jit(solution)/shard_map/ppermute | solution.py:392
